TPU v7x, 128 devices: a whole 4x4x4 slice. The times are simulated.
128 devices in a mesh: chan: 16 (over y, x), tm: 8 (over z, core).
Axes of the slice: x: 4, y: 4, z: 4, core: 2. Of those that a mesh axis runs over, the one named last changes fastest.
Arguments:
- samples: bfloat16 [256, 192, 4096], P('chan', 'tm'), may hold values from -6 to 6
- taps: float32 [16, 4096], replicated, may hold values from -1.5 to 1.5
- block_tile: int32 [120], replicated, may hold values from 0 to 15, as said below
- tile_slots: int32 [16], replicated, may hold values from 0 to 15, as said below
- kern_u: bfloat16 [16, 30720], replicated, may hold values from -1.1953125 to 1.1953125
- kern_v: bfloat16 [16, 30720], replicated, may hold values from -1.1953125 to 1.1953125
Outputs:
- uv_grid: float32 [16, 2048, 2, 256], P('tm', 'chan')
Inputs may be any that keep to these rules, and one draw needn't show every extreme that they name: `block_tile`: A tile's owner is (its position in tile_slots) // 2. The blocks that fall in the tiles of one owner are at most 30; in every draw one owner has exactly 30. `tile_slots`: each tile number stands once.
All inputs are finite; a program needn't handle non-finite values.
Results may differ from a plain program's by a relative error of at most 0.0077.
Values may be sent and summed in bfloat16 or wider, within the bound.
No kernel may reach another device: no remote copies, remote signals or barrier semaphores. Data moves between devices by JAX's collectives and lax.ppermute only.
A program may use at most 192 MiB of HBM per device.

v0:
```python
import math

import jax
import jax.numpy as jnp
import numpy as np
from jax import lax
from jax.sharding import PartitionSpec as P

SBLK = 16
GRID = 16


def passed_along(value, axis, steps):
    count = lax.axis_size(axis)
    leading, last = (max(0, -steps), min(count, count - steps))
    return lax.ppermute(value, axis, [(source, source + steps) for source in range(leading, last)])


def block_pairs(block_total):
    left_list = []
    right_list = []
    for p in range(block_total):
        for q in range(p + 1, block_total):
            left_list.append(p)
            right_list.append(q)
    return (np.array(left_list, dtype=np.int32), np.array(right_list, dtype=np.int32))


def make_kernel(u_part, v_part, block_total):
    u_cols = u_part.astype(jnp.float32).reshape(GRID, block_total, SBLK * SBLK).transpose(1, 2, 0)
    v_cols = v_part.astype(jnp.float32).reshape(GRID, block_total, SBLK * SBLK).transpose(1, 2, 0)
    product = u_cols[:, :, :, None] * v_cols[:, :, None, :]
    return product.reshape(block_total, SBLK * SBLK, GRID * GRID).astype(jnp.bfloat16)


def body(samples, taps, block_tile, tile_slots, kern_u, kern_v):
    station_count, frame_count, length = samples.shape
    channel_count = length // 2
    chan_size = lax.axis_size("chan")
    tm_size = lax.axis_size("tm")
    group_count = chan_size * tm_size
    group_width = channel_count // group_count
    tap_count = taps.shape[0]
    history = passed_along(samples[:, frame_count - (tap_count - 1) :], "tm", 1)
    padded = jnp.concatenate([history, samples], axis=1)
    filtered = jnp.zeros((station_count, frame_count, length), jnp.float32)
    for tap_index in range(tap_count):
        offset = tap_count - 1 - tap_index
        filtered = filtered + taps[tap_index] * padded[:, offset : offset + frame_count].astype(
            jnp.float32
        )
    rows_in = filtered.astype(jnp.bfloat16).reshape(station_count * frame_count, length)
    dft_scale = 1.0 / math.sqrt(length)
    block_cols = min(channel_count, 256)
    groups_per_block = block_cols // group_width
    positions = jnp.arange(length, dtype=jnp.int32)[:, None, None]
    pieces = []
    for column_block in range(channel_count // block_cols):
        channels = column_block * block_cols + jnp.arange(block_cols, dtype=jnp.int32).reshape(
            1, groups_per_block, group_width
        )
        phase_int = positions * channels % length
        phase_angle = phase_int.astype(jnp.float32) * (2.0 * math.pi / length)
        cosine = jnp.cos(phase_angle).astype(jnp.bfloat16)
        sine_neg = (-jnp.sin(phase_angle)).astype(jnp.bfloat16)
        dft_table = jnp.stack([cosine, sine_neg], axis=2).reshape(length, 2 * block_cols)
        spectrum = (
            lax.dot_general(
                dft_table, rows_in, (((0,), (1,)), ((), ())), preferred_element_type=jnp.float32
            )
            * dft_scale
        )
        pieces.append(
            spectrum.astype(jnp.bfloat16).reshape(
                groups_per_block, 2, group_width, station_count, frame_count
            )
        )
    spectra = jnp.concatenate(pieces, axis=0)
    stations = station_count * chan_size
    frames = frame_count * tm_size
    arranged = spectra.reshape(chan_size, tm_size, 2, group_width, station_count, frame_count)
    turned = lax.all_to_all(
        lax.all_to_all(arranged, "chan", split_axis=0, concat_axis=4, tiled=True),
        "tm",
        split_axis=1,
        concat_axis=5,
        tiled=True,
    )
    turned = turned.reshape(2, group_width, stations, frames)
    block_rows = stations // SBLK
    block_total = block_rows * (block_rows - 1) // 2
    vis_scale = 1.0 / math.sqrt(frames)
    swapped = jnp.stack([turned[1], -turned[0]], axis=0)
    real_part = (
        jnp.einsum("cgib,cgjb->gij", turned, turned, preferred_element_type=jnp.float32) * vis_scale
    )
    imag_part = (
        jnp.einsum("cgib,cgjb->gij", swapped, turned, preferred_element_type=jnp.float32)
        * vis_scale
    )
    left_idx, right_idx = block_pairs(block_rows)
    visibility = jnp.stack([real_part, imag_part], axis=1).reshape(
        group_width, 2, block_rows, SBLK, block_rows, SBLK
    )
    visibility = visibility[:, :, left_idx, :, right_idx, :]
    blocks = visibility.reshape(block_total, group_width, 2, SBLK * SBLK).astype(jnp.bfloat16)
    tile_count = tile_slots.shape[0]
    slot_ids = jnp.arange(tile_count, dtype=jnp.int32)
    tile_match = block_tile[:, None] == tile_slots[None, :]
    slot_of_block = jnp.sum(jnp.where(tile_match, slot_ids[None, :], 0), axis=1)
    kernel = make_kernel(kern_u, kern_v, block_total)
    per_block = jnp.einsum("mgce,mel->mgcl", blocks, kernel, preferred_element_type=jnp.float32)
    slot_hits = (slot_of_block[:, None] == slot_ids[None, :]).astype(jnp.float32)
    partial_value = jnp.einsum(
        "mgcl,ms->sgcl", per_block, slot_hits, precision=lax.Precision.HIGHEST
    )
    uv_grid = lax.all_to_all(partial_value, "tm", split_axis=0, concat_axis=1, tiled=True)
    return uv_grid


def solution(mesh):
    placed = (P("chan", "tm", None), P(), P(), P(), P(), P())
    return jax.shard_map(
        body, mesh=mesh, in_specs=placed, out_specs=P("tm", "chan", None, None), check_vma=False
    )
```

profile of v0, /device:TPU:1, one launch (start us, length us, event | category | flops | bytes accessed | tf_op | source)
XLA Modules:
  0.0 647.3 jit_solution(4451937538021533933)
XLA Ops:
  2.2 2.5 copy.103
  4.6 4.9 collective-permute-start
  9.7 18.1 %cosine_convert_fusion.7 = (bf16[4096,16,1,16]{0,3,2,1:T(8,128)(2,1)S(1)}, bf16[4096,16,1,16]{0,3,2,1:T(8,128)(2,1)S(1)}) fusion(s32[16,16]{1,0:T(8,128)S(1)} %multiply_add_fusion), kind=kLoop, calls=%fused_computation.119 | loop fusion | flops 17825792 | bytes 4195328 | tf_op jit(solution)/shard_map/convert_element_type | solution.py:64
  27.7 18.1 %cosine_convert_fusion.6 = (bf16[4096,16,1,16]{0,3,2,1:T(8,128)(2,1)S(1)}, bf16[4096,16,1,16]{0,3,2,1:T(8,128)(2,1)S(1)}) fusion(s32[16,16]{1,0:T(8,128)S(1)} %fusion.84), kind=kLoop, calls=%fused_computation.115 | loop fusion | flops 17825792 | bytes 4195328 | tf_op jit(solution)/shard_map/convert_element_type | solution.py:64
  45.8 18.1 %cosine_convert_fusion.5 = (bf16[4096,16,1,16]{0,3,2,1:T(8,128)(2,1)S(1)}, bf16[4096,16,1,16]{0,3,2,1:T(8,128)(2,1)S(1)}) fusion(s32[16,16]{1,0:T(8,128)S(1)} %fusion.83), kind=kLoop, calls=%fused_computation.111 | loop fusion | flops 17825792 | bytes 4195328 | tf_op jit(solution)/shard_map/convert_element_type | solution.py:64
  63.9 18.1 %cosine_convert_fusion.4 = (bf16[4096,16,1,16]{0,3,2,1:T(8,128)(2,1)S(1)}, bf16[4096,16,1,16]{0,3,2,1:T(8,128)(2,1)S(1)}) fusion(s32[16,16]{1,0:T(8,128)S(1)} %fusion.82), kind=kLoop, calls=%fused_computation.107 | loop fusion | flops 17825792 | bytes 4195328 | tf_op jit(solution)/shard_map/convert_element_type | solution.py:64
  82.0 18.1 %cosine_convert_fusion.3 = (bf16[4096,16,1,16]{0,3,2,1:T(8,128)(2,1)S(1)}, bf16[4096,16,1,16]{0,3,2,1:T(8,128)(2,1)S(1)}) fusion(s32[16,16]{1,0:T(8,128)S(1)} %fusion.81), kind=kLoop, calls=%fused_computation.103 | loop fusion | flops 17825792 | bytes 4195328 | tf_op jit(solution)/shard_map/convert_element_type | solution.py:64
  100.0 18.1 %cosine_convert_fusion.2 = (bf16[4096,16,1,16]{0,3,2,1:T(8,128)(2,1)S(1)}, bf16[4096,16,1,16]{0,3,2,1:T(8,128)(2,1)S(1)}) fusion(s32[16,16]{1,0:T(8,128)S(1)} %fusion.80), kind=kLoop, calls=%fused_computation.99 | loop fusion | flops 17825792 | bytes 4195328 | tf_op jit(solution)/shard_map/convert_element_type | solution.py:64
  118.1 18.1 %cosine_convert_fusion.1 = (bf16[4096,16,1,16]{0,3,2,1:T(8,128)(2,1)S(1)}, bf16[4096,16,1,16]{0,3,2,1:T(8,128)(2,1)S(1)}) fusion(s32[16,16]{1,0:T(8,128)S(1)} %fusion.79), kind=kLoop, calls=%fused_computation.95 | loop fusion | flops 17825792 | bytes 4195328 | tf_op jit(solution)/shard_map/convert_element_type | solution.py:64
  136.2 19.0 %cosine_convert_fusion = (bf16[4096,16,1,16]{0,3,2,1:T(8,128)(2,1)S(1)}, bf16[4096,16,1,16]{0,3,2,1:T(8,128)(2,1)}) fusion(s32[16,16]{1,0:T(8,128)S(1)} %fusion.78), kind=kLoop, calls=%fused_computation.91 | loop fusion | flops 17825792 | bytes 4195328 | tf_op jit(solution)/shard_map/convert_element_type | solution.py:64
  174.2 4.1 copy.81
  178.3 23.2 %add_convert_fusion = bf16[16,24,4096]{2,1,0:T(8,128)(2,1)} fusion(bf16[16,24,4096]{2,1,0:T(8,128)(2,1)S(1)} %copy-done, bf16[16,15,4096]{2,1,0:T(8,128)(2,1)} %copy.81, f32[4096]{0:T(1024)S(1)} %bitcast.136, f32[4096]{0:T(1024)S(1)} %bitcast.137, f32[4096]{0:T(1024)S(1)} %bitcast.123, f32[4096]{0:T(1024)S(1)} %bitcast.124, f32[4096]{0:T(1024)S(1)} %bitcast.125, ...), kind=kLoop, calls=%fused_computation.52 | loop fusion | flops 146276352 | bytes 8519680 | tf_op jit(solution)/shard_map/convert_element_type | solution.py:52
  201.5 5.5 fusion.70
  207.0 2.7 reshape.710
  212.7 4.3 fusion.71
  217.0 3.1 reshape.712
  220.1 5.5 fusion.72
  225.7 3.7 reshape.714
  229.3 5.5 fusion.73
  234.9 3.7 reshape.716
  238.5 5.5 fusion.74
  244.1 3.7 reshape.718
  247.8 5.5 fusion.75
  253.3 3.9 reshape.720
  257.2 5.5 fusion.76
  262.7 3.7 reshape.722
  266.4 5.5 fusion.77
  271.9 3.7 reshape.724
  288.1 22.6 %reshape.779 = bf16[16,2,49152]{2,1,0:T(2,128)(2,1)S(1)} reshape(bf16[16,8,2,16,16,24]{5,4,3,2,1,0:T(8,128)(2,1)} %bitcast.96) | data formatting | bytes 6291456
  310.7 47.5 %all_to_all.51 = bf16[16,2,49152]{2,1,0:T(2,128)(2,1)} all-to-all(bf16[16,2,49152]{2,1,0:T(2,128)(2,1)S(1)} %reshape.779), channel_id=1, replica_groups=mesh['chan'=16,'tm'=8] {'chan'}, dimensions={0} | all-to-all | bytes 6291456 | tf_op jit(solution)/shard_map/all_to_all | solution.py:83
  358.2 25.0 %reshape.780 = bf16[16,8,2,16,16,24]{5,4,3,2,1,0:T(8,128)(2,1)} reshape(bf16[16,2,49152]{2,1,0:T(2,128)(2,1)} %all_to_all.51) | data formatting | bytes 6291456
  383.2 32.4 %copy.82 = bf16[1,8,2,16,16,16,24]{5,4,6,3,2,1,0:T(8,128)(2,1)} copy(bf16[1,8,2,16,16,16,24]{6,5,3,2,1,4,0:T(8,128)(2,1)} %bitcast.92) | data formatting | bytes 6291456 | tf_op jit(solution)/shard_map/all_to_all | solution.py:83
  415.6 30.1 %all_to_all.40 = bf16[1,8,2,16,256,24]{4,5,3,2,1,0:T(8,128)(2,1)} reshape(bf16[1,8,2,16,16,16,24]{5,4,6,3,2,1,0:T(8,128)(2,1)} %copy.82) | data formatting | bytes 6291456 | tf_op jit(solution)/shard_map/all_to_all | solution.py:83
  445.7 4.4 all-to-all-start.1
  453.6 8.7 %multiply_convert_fusion = bf16[120,256,16,16]{1,3,2,0:T(8,128)(2,1)} fusion(f32[120,256,16]{1,2,0:T(8,128)S(1)} %get-tuple-element.39, f32[120,256,16]{1,2,0:T(8,128)S(1)} %get-tuple-element.40), kind=kLoop, calls=%fused_computation.2 | loop fusion | flops 15728640 | bytes 19660800 | tf_op jit(solution)/shard_map/convert_element_type | solution.py:33
  462.2 25.4 %all-to-all-done.1 = bf16[1,8,2,16,256,24]{4,5,3,2,0,1:T(8,128)(2,1)S(1)} async-done(((bf16[1,8,2,16,256,24]{4,5,3,2,0,1:T(8,128)(2,1)}), bf16[1,8,2,16,256,24]{4,5,3,2,0,1:T(8,128)(2,1)S(1)}, u32[]{:S(2)}, u32[]{:S(2)}) %all-to-all-start.1) | async-done | bytes 3145760 | tf_op jit(solution)/shard_map/all_to_all | solution.py:82
  490.0 2.8 bitcast_multiply_fusion
  492.8 17.4 %stack.63 = bf16[16,1,16,16,16,16]{5,4,3,2,0,1:T(8,128)(2,1)} reshape(bf16[16,256,256]{2,1,0:T(8,128)(2,1)} %bitcast_multiply_fusion) | data formatting | bytes 4194304 | tf_op jit(solution)/shard_map/stack | solution.py:102
  510.2 16.6 %copy.88 = bf16[16,1,16,16,16,16]{5,3,4,2,1,0:T(8,128)(2,1)} copy(bf16[16,1,16,16,16,16]{5,4,3,2,0,1:T(8,128)(2,1)} %stack.63) | data formatting | bytes 4194304 | tf_op jit(solution)/shard_map/stack | solution.py:102
  526.9 14.3 %stack.61 = bf16[16,1,16,16,16,16]{5,4,3,2,0,1:T(8,128)(2,1)} reshape(bf16[16,256,256]{2,1,0:T(8,128)(2,1)S(1)} %bitcast_multiply_fusion.1) | data formatting | bytes 4194304 | tf_op jit(solution)/shard_map/stack | solution.py:102
  541.2 16.6 %copy.87 = bf16[16,1,16,16,16,16]{5,3,4,2,1,0:T(8,128)(2,1)} copy(bf16[16,1,16,16,16,16]{5,4,3,2,0,1:T(8,128)(2,1)} %stack.61) | data formatting | bytes 4194304 | tf_op jit(solution)/shard_map/stack | solution.py:102
  557.8 22.7 %pad_maximum_fusion = bf16[16,2,16,16,16,16]{5,3,4,2,1,0:T(8,128)(2,1)} fusion(bf16[16,1,16,16,16,16]{5,3,4,2,1,0:T(8,128)(2,1)} %copy.88, bf16[16,1,16,16,16,16]{5,3,4,2,1,0:T(8,128)(2,1)} %copy.87), kind=kLoop, calls=%fused_computation.1 | loop fusion | flops 2097152 | bytes 8388608 | tf_op jit(solution)/shard_map/stack | solution.py:102
  580.5 12.2 %gather_fusion = bf16[120,16,2,16,16]{4,3,2,1,0:T(8,128)(2,1)} fusion(bf16[16,2,16,16,16,16]{5,3,4,2,1,0:T(8,128)(2,1)} %pad_maximum_fusion, s32[120]{0:T(128)S(1)} %copy-done.8), kind=kCustom, calls=%fused_computation | custom fusion | bytes 3933120 | tf_op jit(solution)/shard_map/gather | solution.py:105
  592.7 18.3 %copy.89 = bf16[120,16,2,16,16]{0,4,3,2,1:T(8,128)(2,1)S(1)} copy(bf16[120,16,2,16,16]{4,3,2,1,0:T(8,128)(2,1)} %gather_fusion) | data formatting | bytes 3932160 | tf_op jit(solution)/shard_map/gather | solution.py:105
  611.1 3.2 copy.92
  614.3 12.6 %fusion.91 = f32[120,16,2,256]{3,1,2,0:T(8,128)} fusion(bf16[120,16,2,256]{3,1,2,0:T(8,128)(2,1)} %copy.92, bf16[120,256,256,1]{1,2,3,0:T(8,128)(2,1)} %bitcast.93), kind=kOutput, calls=%fused_computation.193 | convolution fusion | flops 503316480 | bytes 21626880 | tf_op jit(solution)/shard_map/mgce,mel->mgcl/dot_general | solution.py:112
  626.9 5.8 fusion.48
  633.2 12.6 %all_to_all.52 = f32[16,16,2,256]{3,2,1,0:T(2,128)S(1)} all-to-all(f32[16,16,2,256]{3,2,1,0:T(2,128)S(1)} %copy.95), channel_id=1, replica_groups=mesh['chan'=16,'tm'=8] {'tm'}, dimensions={0} | all-to-all | bytes 1048576 | tf_op jit(solution)/shard_map/all_to_all | solution.py:117
  (64 shorter events, 43.7 us)
Async XLA Ops:
  4.6 169.6 %collective-permute-start = (bf16[16,15,4096]{2,0,1:T(8,128)(2,1)}, bf16[16,15,4096]{2,0,1:T(8,128)(2,1)}, u32[]{:S(2)}, u32[]{:S(2)}) collective-permute-start(bf16[16,15,4096]{2,0,1:T(8,128)(2,1)} %copy.103), channel_id=1, source_target_pairs={{0,1},{1,2},{2,3},{3,4},{4,5},{5,6},{6,7},{8,9},{9,10},{10,11},{11... | collective-permute-start | bytes 5898248 | tf_op jit(solution)/shard_map/ppermute | solution.py:16
  169.3 2.3 copy-start.7
  171.6 2.4 copy-start.10
  174.0 4.4 copy-start
  209.8 2.9 copy-start.9
  275.6 2.2 copy-start.1
  275.6 3.9 copy-start.2
  277.8 3.4 copy-start.3
  279.5 3.5 copy-start.4
  281.2 3.5 copy-start.5
  283.0 3.4 copy-start.6
  445.7 42.0 %all-to-all-start.1 = ((bf16[1,8,2,16,256,24]{4,5,3,2,0,1:T(8,128)(2,1)}), bf16[1,8,2,16,256,24]{4,5,3,2,0,1:T(8,128)(2,1)S(1)}, u32[]{:S(2)}, u32[]{:S(2)}) async-start(bf16[1,8,2,16,256,24]{4,5,3,2,0,1:T(8,128)(2,1)} %bitcast.97), calls=%async_computation.1 | async-start | bytes 6291456 | tf_op jit(solution)/shard_map/all_to_all | solution.py:82
  450.1 2.7 copy-start.11
  450.1 2.7 copy-start.12
  557.8 22.7 %copy-start.8 = (s32[120]{0:T(128)S(1)}, s32[120]{0:T(128)}, u32[]{:S(2)}) copy-start(s32[120]{0:T(128)} %constant.106) | copy-start | bytes 1444
where the time goes:
time: 658 us; the launch traced here: 647 us
  local copies, waits for them, and re-layouts  264 us (40%)
  other arithmetic  222 us (34%)
  matrix products  65.5 us (10%)
  blocking collectives  60.1 us (9%)
  waiting for transfers between devices  25.4 us (4%)
  starting transfers between devices  9.37 us (1%)
    convert_element_type x8, other arithmetic, body(): cosine = jnp.cos(phase_angle).astype(jnp.bfloat16)  145 us
    another operation x4, local copies, waits for them, and re-layouts, body(): jnp.stack([real_part, imag_part], axis=1)  65 us
    unnamed x36, local copies, waits for them, and re-layouts  63.9 us
    all_to_all x2, local copies, waits for them, and re-layouts, body(): lax.all_to_all(arranged, 'chan', split_axis=0, concat_axis=4, tiled=True)  62.5 us
    all_to_all x1, blocking collectives, body(): lax.all_to_all(arranged, 'chan', split_axis=0, concat_axis=4, tiled=True)  47.5 us
    dot_general x8, matrix products, body(): lax.dot_general(dft_table, rows_in, (((0,), (1,)), ((), ())), preferred_e...  42.9 us
    gather x2, local copies, waits for them, and re-layouts, body(): visibility = visibility[:, :, left_idx, :, right_idx, :]  30.6 us
    reshape x8, local copies, waits for them, and re-layouts, body(): spectrum.astype(jnp.bfloat16)  28.2 us
  transfers between devices with their start and end apart: 2, of which 1 were waited for; matrix products, arithmetic and copies ran while one was open for 27% of the time, Pallas kernels for 0%

commit v1 on v0

v1 whole, which is shorter than its diff:
```python
import functools
import math

import jax
import jax.numpy as jnp
import ml_dtypes
import numpy as np
from jax import lax
from jax.experimental import pallas as pl
from jax.experimental.pallas import tpu as pltpu
from jax.sharding import PartitionSpec as P

SBLK = 16
GRID = 16
RADIX = 16
HALO = 16
LANES = 128
BF = jnp.bfloat16
F32 = jnp.float32
NT = (((1,), (1,)), ((), ()))
TN = (((0,), (0,)), ((), ()))


def dft_tables(length):
    span = length // RADIX
    place = np.arange(span)[None, :]
    dest = np.arange(length // (2 * RADIX))[:, None]

    def table(low):
        angle = (place * (low + RADIX * dest) % length) * (2.0 * np.pi / length)
        c, s = np.cos(angle), np.sin(angle)
        sign = -1.0 if low > RADIX // 2 else 1.0
        return np.block([[c, sign * s], [-s, sign * c]]) / math.sqrt(length)

    pairs = np.stack(
        [np.concatenate([table(k), table(RADIX - k)], axis=0) for k in range(1, RADIX // 2)]
    )
    ends = np.stack([table(0)[:, :span], table(RADIX // 2)[:, :span]])
    return pairs.astype(ml_dtypes.bfloat16), ends.astype(ml_dtypes.bfloat16)


def real_dft(x):
    n = len(x)
    if n == 2:
        return [(x[0] + x[1], None), (x[0] - x[1], None)]
    even, odd = real_dft(x[0::2]), real_dft(x[1::2])
    out = [None] * (n // 2 + 1)
    for k in range(n // 4 + 1):
        er, ei = even[k]
        dr, di = odd[k]
        if k == 0:
            out[0], out[n // 2] = (er + dr, None), (er - dr, None)
        elif k == n // 4:
            out[k] = (er, -dr)
        else:
            c, s = math.cos(2 * math.pi * k / n), math.sin(2 * math.pi * k / n)
            if 8 * k == n:
                tr, ti = (dr + di) * c, (di - dr) * c
            else:
                tr, ti = dr * c + di * s, di * c - dr * s
            out[k] = (er + tr, ei + ti)
            out[n // 2 - k] = (er - tr, ti - ei)
    return out


def channelize_kernel(
    x_ref, halo_ref, taps_ref, pairs_ref, ends_ref, out_ref, xs, filt, low, turned
):
    stations, frames, length = x_ref.shape
    taps = taps_ref.shape[0]
    span = length // RADIX
    rows = stations * frames
    dests = length // (2 * RADIX)

    for half in range(span // LANES):

        def fir(tile, _):
            at = pl.ds(pl.multiple_of(tile * span + half * LANES, LANES), LANES)
            for s in range(stations):
                xs[pl.ds(s, HALO, stride=stations), :] = halo_ref[s, :, at].astype(F32)
                xs[pl.ds(HALO * stations + s, frames, stride=stations), :] = x_ref[
                    s, :, at
                ].astype(F32)
            weights = [taps_ref[pl.ds(k, 1), at] for k in range(taps)]
            sums = {}
            for step in range(HALO - taps + 1, HALO + frames):
                x = xs[step * stations : (step + 1) * stations, :]
                for k in range(taps - 1, -1, -1):
                    b = step - HALO + k
                    if 0 <= b < frames:
                        term = weights[k] * x
                        sums[b] = sums[b] + term if b in sums else term
                if step >= HALO:
                    b = step - HALO
                    filt[tile, b * stations : (b + 1) * stations, :] = sums.pop(b).astype(BF)
            return 0

        lax.fori_loop(0, RADIX, fir, 0)

        def butterfly(b, _):
            at = pl.ds(pl.multiple_of(b * stations, stations), stations)
            parts = real_dft([filt[tile, at, :].astype(F32) for tile in range(RADIX)])
            to = slice(half * LANES, (half + 1) * LANES)
            for k, (re, im) in enumerate(parts):
                low[k, at, to] = re.astype(BF)
                if im is not None:
                    low[RADIX // 2 + k, at, to] = im.astype(BF)
            return 0

        lax.fori_loop(0, frames, butterfly, 0)

    def keep(channel, part, value):
        for tile in range(rows // LANES):
            turned[
                tile, pl.ds(channel * 2 + part, dests, stride=2 * RADIX), :
            ] = value[:, tile * LANES : (tile + 1) * LANES]

    for end in range(2):
        z = lax.dot_general(
            ends_ref[end], low[end * (RADIX // 2)], NT, preferred_element_type=F32
        )
        for part in range(2):
            keep(end * (RADIX // 2), part, z[part * dests : (part + 1) * dests])

    def pair(k, _):
        spectrum = jnp.concatenate([low[k], low[RADIX // 2 + k]], axis=1)
        for mirrored in range(2):
            z = lax.dot_general(
                pairs_ref[k - 1, mirrored * 2 * dests : (mirrored + 1) * 2 * dests, :],
                spectrum,
                NT,
                preferred_element_type=F32,
            )
            channel = RADIX - k if mirrored else k
            for part in range(2):
                keep(channel, part, z[part * dests : (part + 1) * dests])
        return 0

    lax.fori_loop(1, RADIX // 2, pair, 0)

    def give(d, _):
        at = pl.ds(pl.multiple_of(d * 2 * RADIX, 2 * RADIX), 2 * RADIX)
        for tile in range(rows // LANES):
            out_ref[d, :, tile * LANES : (tile + 1) * LANES] = turned[tile, at, :].astype(BF)
        return 0

    lax.fori_loop(0, dests, give, 0, unroll=4)


def channelize(samples, halo, taps):
    stations, frames, length = samples.shape
    rows = stations * frames
    span = length // RADIX
    dests = length // (2 * RADIX)
    pairs, ends = dft_tables(length)
    whole = pl.BlockSpec(memory_space=pltpu.VMEM)
    return pl.pallas_call(
        channelize_kernel,
        out_shape=jax.ShapeDtypeStruct((dests, 2 * RADIX, rows), BF),
        in_specs=[whole] * 5,
        out_specs=whole,
        scratch_shapes=[
            pltpu.VMEM(((HALO + frames) * stations, LANES), F32),
            pltpu.VMEM((RADIX, rows, LANES), BF),
            pltpu.VMEM((RADIX, rows, span), BF),
            pltpu.VMEM((rows // LANES, dests * 2 * RADIX, LANES), F32),
        ],
        compiler_params=pltpu.CompilerParams(vmem_limit_bytes=50 << 20),
        name="channelize",
    )(samples, halo, taps, jnp.asarray(pairs), jnp.asarray(ends))


def swap_groups(v):
    lane = lax.broadcasted_iota(jnp.int32, v[0].shape, 1)
    v = list(v)
    for bit in (1, 2, 4):
        low = (lane // (bit * SBLK)) % 2 == 0
        for i in range(8):
            if not i & bit:
                a, b = v[i], v[i + bit]
                v[i] = jnp.where(low, a, pltpu.roll(b, bit * SBLK, 1))
                v[i + bit] = jnp.where(low, pltpu.roll(a, LANES - bit * SBLK, 1), b)
    return v


def correlate_kernel(sizes, slots_ref, left_ref, right_ref, r_ref, u_ref, v_ref, out_ref, arr, vis, blocks):
    owners, times, frames = sizes
    group2 = r_ref.shape[1]
    total = times * frames
    stations = owners * SBLK
    sides = stations // LANES
    scale = 1.0 / math.sqrt(total)

    def turn(t, _):
        for tile in range(frames // 8):
            for side in range(sides):
                got = [
                    r_ref[(side * 8 + i) * times + t, :, tile * LANES : (tile + 1) * LANES].astype(F32)
                    for i in range(8)
                ]
                for i, w in enumerate(swap_groups(got)):
                    arr[side, pl.ds(t * frames + tile * 8 + i, group2, stride=total), :] = w
        return 0

    lax.fori_loop(0, times, turn, 0)

    def correlate(g, _):
        def part(c):
            at = pl.ds(pl.multiple_of((2 * g + c) * total, total), total)
            return jnp.concatenate([arr[side, at, :] for side in range(sides)], axis=1)

        re, im = part(0), part(1)
        left = jnp.concatenate([re, im], axis=0).astype(BF)
        for c in range(2):
            right = left if c == 0 else jnp.concatenate([-im, re], axis=0).astype(BF)
            z = lax.dot_general(left, right, TN, preferred_element_type=F32) * scale
            for side in range(sides):
                vis[side, pl.ds(2 * g + c, stations, stride=group2), :] = z[
                    :, side * LANES : (side + 1) * LANES
                ]
        return 0

    lax.fori_loop(0, group2 // 2, correlate, 0)

    def regroup(p, _):
        for side in range(sides):

            @pl.when(p < side * 8 + 7)
            def _():
                for half in range(2):
                    got = [
                        vis[side, pl.ds(pl.multiple_of((p * SBLK + half * 8 + i) * group2, group2), group2), :]
                        for i in range(8)
                    ]
                    for i, w in enumerate(swap_groups(got)):
                        blocks[p * owners + side * 8 + i, :, half * LANES : (half + 1) * LANES] = w.astype(BF)

        return 0

    lax.fori_loop(0, owners - 1, regroup, 0)

    out_ref[...] = jnp.zeros_like(out_ref)
    cells = SBLK * SBLK

    def grid(m, _):
        at = pl.ds(pl.multiple_of(m * cells, cells), cells)
        u, v = u_ref[:, at].astype(F32), v_ref[:, at].astype(F32)
        kernel = jnp.concatenate([u[i : i + 1, :] * v for i in range(GRID)], axis=0).astype(BF)
        z = lax.dot_general(
            blocks[left_ref[m] * owners + right_ref[m]], kernel, NT, preferred_element_type=F32
        )
        slot = slots_ref[m]
        out_ref[slot] = out_ref[slot] + z
        return 0

    lax.fori_loop(0, owners * (owners - 1) // 2, grid, 0, unroll=2)


def correlate(turned, slots, left, right, kern_u, kern_v, owners, times, frames, tiles):
    group2 = turned.shape[1]
    stations = owners * SBLK
    whole = pl.BlockSpec(memory_space=pltpu.VMEM)
    smem = pl.BlockSpec(memory_space=pltpu.SMEM)
    return pl.pallas_call(
        functools.partial(correlate_kernel, (owners, times, frames)),
        out_shape=jax.ShapeDtypeStruct((tiles, group2, GRID * GRID), F32),
        in_specs=[smem] * 3 + [whole] * 3,
        out_specs=whole,
        scratch_shapes=[
            pltpu.VMEM((stations // LANES, group2 * times * frames, LANES), F32),
            pltpu.VMEM((stations // LANES, stations * group2, LANES), F32),
            pltpu.VMEM((owners * owners, group2, SBLK * SBLK), BF),
        ],
        compiler_params=pltpu.CompilerParams(vmem_limit_bytes=50 << 20),
        name="correlate",
    )(slots, left, right, turned, kern_u, kern_v)


def body(samples, taps, block_tile, tile_slots, kern_u, kern_v):
    frame_count = samples.shape[1]
    chan_size = lax.axis_size("chan")
    tm_size = lax.axis_size("tm")
    history = lax.ppermute(
        samples[:, frame_count - HALO :], "tm", [(i, i + 1) for i in range(tm_size - 1)]
    )
    spectra = channelize(samples, history, taps)
    turned = lax.all_to_all(spectra, ("chan", "tm"), split_axis=0, concat_axis=0, tiled=True)
    left, right = np.triu_indices(chan_size, 1)
    tile_count = tile_slots.shape[0]
    slot_ids = jnp.arange(tile_count, dtype=jnp.int32)
    slots = jnp.sum(
        jnp.where(block_tile[:, None] == tile_slots[None, :], slot_ids[None, :], 0), axis=1
    )
    grids = correlate(
        turned,
        slots,
        jnp.asarray(left, jnp.int32),
        jnp.asarray(right, jnp.int32),
        kern_u,
        kern_v,
        chan_size,
        tm_size,
        frame_count,
        tile_count,
    )
    width = grids.shape[1] // 2
    partial_value = grids.reshape(tile_count, width, 2, GRID * GRID)
    return lax.all_to_all(partial_value, "tm", split_axis=0, concat_axis=1, tiled=True)


def solution(mesh):
    placed = (P("chan", "tm", None), P(), P(), P(), P(), P())
    return jax.shard_map(
        body, mesh=mesh, in_specs=placed, out_specs=P("tm", "chan", None, None), check_vma=False
    )
```

time: 658 us -> 164 us (0.25); the launches traced: 647 us -> 164 us
  local copies, waits for them, and re-layouts: 264 us -> 3.15 us
  other arithmetic: 222 us -> 0.09 us
  Pallas kernels: 0 us -> 67.4 us
  matrix products: 65.5 us -> 0 us
  blocking collectives: 60.1 us -> 13.1 us
  waiting for transfers between devices: 25.4 us -> 64 us
  starting transfers between devices: 9.37 us -> 16.3 us
    convert_element_type x10 -> x0, other arithmetic: 177 us -> none  [the longest x8 145 us: body(): cosine = jnp.cos(phase_angle).astype(jnp.bfloat16)]
    pallas_call x0 -> x2, Pallas kernels: none -> 67.4 us  [the longest x1 41.1 us: correlate(): pl.pallas_call(functools.partial(correlate_kernel, (owners, times, frames...]
    dot_general x12 -> x0, matrix products: 65.5 us -> none  [the longest x8 42.9 us: body(): lax.dot_general(dft_table, rows_in, (((0,), (1,)), ((), ())), preferred_e...]
    another operation x4 -> x0, local copies, waits for them, and re-layouts: 65 us -> none  [body(): jnp.stack([real_part, imag_part], axis=1)]
    unnamed x36 -> x16, local copies, waits for them, and re-layouts: 63.9 us -> 0.04 us
    all_to_all x3 -> x0, local copies, waits for them, and re-layouts: 62.9 us -> none  [the longest x2 62.5 us: body(): lax.all_to_all(arranged, 'chan', split_axis=0, concat_axis=4, tiled=True)]
    all_to_all x1 -> x0, blocking collectives: 47.5 us -> none  [body(): lax.all_to_all(arranged, 'chan', split_axis=0, concat_axis=4, tiled=True)]
    another operation x9 -> x0, other arithmetic: 41.4 us -> none  [the longest x1 22.7 us: body(): jnp.stack([real_part, imag_part], axis=1)]
  transfers between devices with their start and end apart: 2 -> 2, of which waited for: 1 -> 2; matrix products, arithmetic and copies ran while one was open for 27% -> 0% of each run, Pallas kernels for 0% -> 0%
where the time goes in v1:
time: 164 us
  Pallas kernels  67.4 us (41%)
  waiting for transfers between devices  64 us (39%)
  starting transfers between devices  16.3 us (10%)
  blocking collectives  13.1 us (8%)
  local copies, waits for them, and re-layouts  3.15 us (2%)
    pallas_call x1, Pallas kernels, correlate(): pl.pallas_call(functools.partial(correlate_kernel, (owners, times, frames...  41.1 us
    all_to_all x1, waiting for transfers between devices, body(): lax.all_to_all(spectra, ('chan', 'tm'), split_axis=0, concat_axis=0, tile...  41 us
    pallas_call x1, Pallas kernels, channelize(): pl.pallas_call(channelize_kernel, out_shape=jax.ShapeDtypeStruct((dests,...  26.3 us
    ppermute x1, waiting for transfers between devices, body(): lax.ppermute(samples[:, frame_count - HALO:], 'tm', [(i, i + 1) for i in...  23 us
    all_to_all x1, blocking collectives, body(): lax.all_to_all(partial_value, 'tm', split_axis=0, concat_axis=1, tiled=True)  13.1 us
    all_to_all x1, starting transfers between devices, body(): lax.all_to_all(spectra, ('chan', 'tm'), split_axis=0, concat_axis=0, tile...  11.4 us
    ppermute x1, starting transfers between devices, body(): lax.ppermute(samples[:, frame_count - HALO:], 'tm', [(i, i + 1) for i in...  4.94 us
  transfers between devices with their start and end apart: 2, of which 2 were waited for; matrix products, arithmetic and copies ran while one was open for 0% of the time, Pallas kernels for 0%

profile of v1, /device:TPU:1, one launch (start us, length us, event | category | flops | bytes accessed | tf_op | source)
XLA Modules:
  0.0 164.1 jit_solution(11920612980612685181)
XLA Ops:
  0.0 0.0 copy-start.3
  0.0 0.0 copy-start.2
  0.0 1.8 %slice.3 = bf16[16,16,4096]{2,1,0:T(8,128)(2,1)S(1)} slice(bf16[16,24,4096]{2,1,0:T(8,128)(2,1)} %x_ref.1), slice={[0:16], [8:24], [0:4096]} | slice | bytes 4194304 | tf_op jit(solution)/shard_map/slice | solution.py:284
  1.8 4.9 %collective-permute-start = (bf16[16,16,4096]{2,1,0:T(8,128)(2,1)S(1)}, bf16[16,16,4096]{2,1,0:T(8,128)(2,1)S(1)}, u32[]{:S(2)}, u32[]{:S(2)}) collective-permute-start(bf16[16,16,4096]{2,1,0:T(8,128)(2,1)S(1)} %slice.3), channel_id=1, source_target_pairs={{0,1},{1,2},{2,3},{3,4},{4,5},{5,6},{6,7},{8,9},{9,10},{10,11},{11... | collective-permute-start | bytes 6291464 | tf_op jit(solution)/shard_map/ppermute | solution.py:283
  6.7 23.0 %collective-permute-done.halo_ref = bf16[16,16,4096]{2,1,0:T(8,128)(2,1)S(1)} collective-permute-done((bf16[16,16,4096]{2,1,0:T(8,128)(2,1)S(1)}, bf16[16,16,4096]{2,1,0:T(8,128)(2,1)S(1)}, u32[]{:S(2)}, u32[]{:S(2)}) %collective-permute-start) | collective-permute-done | bytes 2097184 | tf_op jit(solution)/shard_map/ppermute | solution.py:283
  29.7 0.0 copy-done.3
  29.7 0.0 copy-done.2
  29.7 26.3 %channelize.1 = bf16[128,32,384]{2,1,0:T(8,128)(2,1)} custom-call(bf16[16,24,4096]{2,1,0:T(8,128)(2,1)} %x_ref.1, bf16[16,16,4096]{2,1,0:T(8,128)(2,1)S(1)} %collective-permute-done.halo_ref, f32[16,4096]{1,0:T(8,128)S(1)} %copy-done.2, bf16[7,512,512]{2,1,0:T(8,128)(2,1)} %constant.10.clone.pairs_ref, bf16[2,256,256]{2,1,0:T(8,128)(2,1)S(1)} %copy-done.3), custom_call_target="tpu_custom_call" | custom-call | tf_op jit(solution)/shard_map/channelize/pallas_call | solution.py:157
  56.0 0.0 copy-start.6
  56.0 0.0 copy-start.7
  56.0 0.0 copy-start
  56.0 0.0 copy-start.1
  56.0 0.0 copy-start.4
  56.1 0.0 copy-start.5
  56.1 11.4 %all-to-all-start = ((bf16[128,32,384]{2,1,0:T(8,128)(2,1)}), bf16[128,32,384]{2,1,0:T(8,128)(2,1)}, u32[]{:S(2)}, u32[]{:S(2)}) async-start(bf16[128,32,384]{2,1,0:T(8,128)(2,1)} %channelize.1), calls=%async_computation | async-start | bytes 6291456 | tf_op jit(solution)/shard_map/all_to_all | solution.py:287
  67.4 0.0 copy-done.6
  67.4 0.0 copy-done.7
  67.5 0.1 select_reduce_fusion.slots_ref
  67.5 41.0 %all-to-all-done.r_ref = bf16[128,32,384]{2,1,0:T(8,128)(2,1)} async-done(((bf16[128,32,384]{2,1,0:T(8,128)(2,1)}), bf16[128,32,384]{2,1,0:T(8,128)(2,1)}, u32[]{:S(2)}, u32[]{:S(2)}) %all-to-all-start) | async-done | bytes 3145760 | tf_op jit(solution)/shard_map/all_to_all | solution.py:287
  108.6 0.0 copy-done
  108.6 0.0 copy-done.1
  108.6 0.0 copy-done.4
  108.6 0.0 copy-done.5
  108.6 41.1 %correlate.1 = f32[16,32,256]{2,1,0:T(8,128)S(1)} custom-call(s32[120]{0:T(128)S(1)} %select_reduce_fusion.slots_ref, s32[120]{0:T(128)S(1)} %copy-done.4, s32[120]{0:T(128)S(1)} %copy-done.5, bf16[128,32,384]{2,1,0:T(8,128)(2,1)} %all-to-all-done.r_ref, bf16[16,30720]{1,0:T(8,128)(2,1)S(1)} %copy-done, bf16[16,30720]{1,0:T(8,128)(2,1)S(1)} %copy-done.1), custom_call_target="tpu_custom_call" | custom-call | tf_op jit(solution)/shard_map/correlate/pallas_call | solution.py:264
  149.6 0.3 reshape.5
  150.0 13.1 %all_to_all.23 = f32[16,16,2,256]{3,2,1,0:T(2,128)S(1)} all-to-all(f32[16,16,2,256]{3,2,1,0:T(2,128)S(1)} %reshape.5), channel_id=1, replica_groups=mesh['chan'=16,'tm'=8] {'tm'}, dimensions={0} | all-to-all | bytes 1048576 | tf_op jit(solution)/shard_map/all_to_all | solution.py:308
  163.0 1.0 copy.12
Async XLA Ops:
  0.0 29.7 %copy-start.3 = (bf16[2,256,256]{2,1,0:T(8,128)(2,1)S(1)}, bf16[2,256,256]{2,1,0:T(8,128)(2,1)}, u32[]{:S(2)}) copy-start(bf16[2,256,256]{2,1,0:T(8,128)(2,1)} %constant.11.clone.ends_ref) | copy-start | bytes 786436
  0.0 29.7 %copy-start.2 = (f32[16,4096]{1,0:T(8,128)S(1)}, f32[16,4096]{1,0:T(8,128)}, u32[]{:S(2)}) copy-start(f32[16,4096]{1,0:T(8,128)} %taps_ref.1) | copy-start | bytes 786436
  1.8 27.9 %collective-permute-start = (bf16[16,16,4096]{2,1,0:T(8,128)(2,1)S(1)}, bf16[16,16,4096]{2,1,0:T(8,128)(2,1)S(1)}, u32[]{:S(2)}, u32[]{:S(2)}) collective-permute-start(bf16[16,16,4096]{2,1,0:T(8,128)(2,1)S(1)} %slice.3), channel_id=1, source_target_pairs={{0,1},{1,2},{2,3},{3,4},{4,5},{5,6},{6,7},{8,9},{9,10},{10,11},{11... | collective-permute-start | bytes 6291464 | tf_op jit(solution)/shard_map/ppermute | solution.py:283
  56.0 11.4 %copy-start.6 = (s32[120]{0:T(128)S(1)}, s32[120]{0:T(128)}, u32[]{:S(2)}) copy-start(s32[120]{0:T(128)} %param.12) | copy-start | bytes 1444
  56.0 11.4 %copy-start.7 = (s32[16]{0:T(128)S(1)}, s32[16]{0:T(128)}, u32[]{:S(2)}) copy-start(s32[16]{0:T(128)} %param.13) | copy-start | bytes 196
  56.0 52.5 %copy-start = (bf16[16,30720]{1,0:T(8,128)(2,1)S(1)}, bf16[16,30720]{1,0:T(8,128)(2,1)}, u32[]{:S(2)}) copy-start(bf16[16,30720]{1,0:T(8,128)(2,1)} %u_ref.1) | copy-start | bytes 2949124
  56.0 52.5 %copy-start.1 = (bf16[16,30720]{1,0:T(8,128)(2,1)S(1)}, bf16[16,30720]{1,0:T(8,128)(2,1)}, u32[]{:S(2)}) copy-start(bf16[16,30720]{1,0:T(8,128)(2,1)} %v_ref.1) | copy-start | bytes 2949124
  56.0 52.5 %copy-start.4 = (s32[120]{0:T(128)S(1)}, s32[120]{0:T(128)}, u32[]{:S(2)}) copy-start(s32[120]{0:T(128)} %constant.12.clone.left_ref) | copy-start | bytes 1444
  56.1 52.5 %copy-start.5 = (s32[120]{0:T(128)S(1)}, s32[120]{0:T(128)}, u32[]{:S(2)}) copy-start(s32[120]{0:T(128)} %constant.13.clone.right_ref) | copy-start | bytes 1444
  56.1 52.5 %all-to-all-start = ((bf16[128,32,384]{2,1,0:T(8,128)(2,1)}), bf16[128,32,384]{2,1,0:T(8,128)(2,1)}, u32[]{:S(2)}, u32[]{:S(2)}) async-start(bf16[128,32,384]{2,1,0:T(8,128)(2,1)} %channelize.1), calls=%async_computation | async-start | bytes 6291456 | tf_op jit(solution)/shard_map/all_to_all | solution.py:287

commit v2 on v1

v2 whole, which is shorter than its diff:
```python
import functools
import math

import jax
import jax.numpy as jnp
import ml_dtypes
import numpy as np
from jax import lax
from jax.experimental import pallas as pl
from jax.experimental.pallas import tpu as pltpu
from jax.sharding import PartitionSpec as P

SBLK = 16
GRID = 16
RADIX = 16
HALO = 8
PITCH = 24
PAD = 8
LANES = 128
BF = jnp.bfloat16
F32 = jnp.float32
NT = (((1,), (1,)), ((), ()))
TN = (((0,), (0,)), ((), ()))


def dft_tables(length):
    span = length // RADIX
    place = np.arange(span)[None, :]
    dest = np.arange(length // (2 * RADIX))[:, None]

    def table(low):
        angle = (place * (low + RADIX * dest) % length) * (2.0 * np.pi / length)
        c, s = np.cos(angle), np.sin(angle)
        sign = -1.0 if low > RADIX // 2 else 1.0
        return np.block([[c, sign * s], [-s, sign * c]]) / math.sqrt(length)

    pairs = np.stack(
        [np.concatenate([table(k), table(RADIX - k)], axis=0) for k in range(1, RADIX // 2)]
    )
    ends = np.stack([table(0)[:, :span], table(RADIX // 2)[:, :span]])
    return pairs.astype(ml_dtypes.bfloat16), ends.astype(ml_dtypes.bfloat16)


def real_dft(x):
    n = len(x)
    if n == 2:
        return [(x[0] + x[1], None), (x[0] - x[1], None)]
    even, odd = real_dft(x[0::2]), real_dft(x[1::2])
    out = [None] * (n // 2 + 1)
    for k in range(n // 4 + 1):
        er, ei = even[k]
        dr, di = odd[k]
        if k == 0:
            out[0], out[n // 2] = (er + dr, None), (er - dr, None)
        elif k == n // 4:
            out[k] = (er, -dr)
        else:
            c, s = math.cos(2 * math.pi * k / n), math.sin(2 * math.pi * k / n)
            if 8 * k == n:
                tr, ti = (dr + di) * c, (di - dr) * c
            else:
                tr, ti = dr * c + di * s, di * c - dr * s
            out[k] = (er + tr, ei + ti)
            out[n // 2 - k] = (er - tr, ti - ei)
    return out


def channelize_kernel(
    keep_ref, x_ref, left_ref, right_ref, taps_ref, pairs_ref, ends_ref, out_ref, xs, filt, low, turned
):
    stations, frames, length = x_ref.shape
    taps = taps_ref.shape[0]
    span = length // RADIX
    rows = stations * frames
    dests = length // (2 * RADIX)
    pitch = 2 * RADIX + PAD
    own = keep_ref[0]

    for half in range(span // LANES):

        def fir(tile, _):
            at = pl.ds(pl.multiple_of(tile * span + half * LANES, LANES), LANES)
            for s in range(stations):
                for ref, first in ((left_ref, 0), (x_ref, HALO), (right_ref, HALO + frames)):
                    xs[pl.ds(first * PITCH + s, ref.shape[1], stride=PITCH), :] = ref[
                        s, :, at
                    ].astype(F32)
            weights = [taps_ref[pl.ds(k, 1), at] for k in range(taps)]
            sums = {}
            for step in range(frames + taps - 1):
                if step == HALO + frames:
                    sums = {b: own * value for b, value in sums.items()}
                x = xs[step * PITCH : step * PITCH + stations, :]
                for k in range(taps - 1, -1, -1):
                    b = step - (taps - 1) + k
                    if 0 <= b < frames:
                        term = weights[k] * x
                        sums[b] = sums[b] + term if b in sums else term
                if step >= taps - 1:
                    b = step - (taps - 1)
                    filt[tile, b * stations : (b + 1) * stations, :] = sums.pop(b).astype(BF)
            return 0

        lax.fori_loop(0, RADIX, fir, 0)

        def butterfly(b, _):
            at = pl.ds(pl.multiple_of(b * stations, stations), stations)
            parts = real_dft([filt[tile, at, :].astype(F32) for tile in range(RADIX)])
            to = slice(half * LANES, (half + 1) * LANES)
            for k, (re, im) in enumerate(parts):
                low[k, at, to] = re.astype(BF)
                if im is not None:
                    low[RADIX // 2 + k, at, to] = im.astype(BF)
            return 0

        lax.fori_loop(0, frames, butterfly, 0)

    def keep(channel, part, value):
        for tile in range(rows // LANES):
            turned[
                tile, pl.ds(channel * 2 + part, dests, stride=pitch), :
            ] = value[:, tile * LANES : (tile + 1) * LANES]

    for end in range(2):
        z = lax.dot_general(
            ends_ref[end], low[end * (RADIX // 2)], NT, preferred_element_type=F32
        )
        for part in range(2):
            keep(end * (RADIX // 2), part, z[part * dests : (part + 1) * dests])

    def pair(k, _):
        spectrum = jnp.concatenate([low[k], low[RADIX // 2 + k]], axis=1)
        for mirrored in range(2):
            z = lax.dot_general(
                pairs_ref[k - 1, mirrored * 2 * dests : (mirrored + 1) * 2 * dests, :],
                spectrum,
                NT,
                preferred_element_type=F32,
            )
            channel = RADIX - k if mirrored else k
            for part in range(2):
                keep(channel, part, z[part * dests : (part + 1) * dests])
        return 0

    lax.fori_loop(1, RADIX // 2, pair, 0)

    def give(d, _):
        at = pl.ds(pl.multiple_of(d * pitch, 8), 2 * RADIX)
        for tile in range(rows // LANES):
            out_ref[d, :, tile * LANES : (tile + 1) * LANES] = turned[tile, at, :].astype(BF)
        return 0

    lax.fori_loop(0, dests, give, 0, unroll=4)


def channelize(keep, samples, before, after, taps):
    stations, frames, length = samples.shape
    rows = stations * frames
    span = length // RADIX
    dests = length // (2 * RADIX)
    pairs, ends = dft_tables(length)
    whole = pl.BlockSpec(memory_space=pltpu.VMEM)
    return pl.pallas_call(
        channelize_kernel,
        out_shape=jax.ShapeDtypeStruct((dests, 2 * RADIX, rows), BF),
        in_specs=[pl.BlockSpec(memory_space=pltpu.SMEM)] + [whole] * 6,
        out_specs=whole,
        scratch_shapes=[
            pltpu.VMEM(((2 * HALO + frames) * PITCH, LANES), F32),
            pltpu.VMEM((RADIX, rows, LANES), BF),
            pltpu.VMEM((RADIX, rows, span), BF),
            pltpu.VMEM((rows // LANES, dests * (2 * RADIX + PAD), LANES), F32),
        ],
        compiler_params=pltpu.CompilerParams(vmem_limit_bytes=50 << 20),
        name="channelize",
    )(keep, samples, before, after, taps, jnp.asarray(pairs), jnp.asarray(ends))


def swap_groups(v):
    lane = lax.broadcasted_iota(jnp.int32, v[0].shape, 1)
    v = list(v)
    for bit in (1, 2, 4):
        low = (lane // (bit * SBLK)) % 2 == 0
        for i in range(8):
            if not i & bit:
                a, b = v[i], v[i + bit]
                v[i] = jnp.where(low, a, pltpu.roll(b, bit * SBLK, 1))
                v[i + bit] = jnp.where(low, pltpu.roll(a, LANES - bit * SBLK, 1), b)
    return v


def weights_kernel(u_ref, v_ref, out_ref):
    cells = SBLK * SBLK
    for m in range(out_ref.shape[0]):
        u = u_ref[:, m * cells : (m + 1) * cells].astype(F32)
        v = v_ref[:, m * cells : (m + 1) * cells].astype(F32)
        for i in range(GRID):
            out_ref[m, i * GRID : (i + 1) * GRID, :] = (u[i : i + 1, :] * v).astype(BF)


def grid_weights(kern_u, kern_v):
    cells = SBLK * SBLK
    count = kern_u.shape[1] // cells
    step = math.gcd(count, 8)
    part = pl.BlockSpec((GRID, step * cells), lambda m: (0, m))
    return pl.pallas_call(
        weights_kernel,
        grid=(count // step,),
        out_shape=jax.ShapeDtypeStruct((count, GRID * GRID, cells), BF),
        in_specs=[part, part],
        out_specs=pl.BlockSpec((step, GRID * GRID, cells), lambda m: (m, 0, 0)),
        compiler_params=pltpu.CompilerParams(vmem_limit_bytes=16 << 20),
        cost_estimate=pl.CostEstimate(
            flops=count * GRID * GRID * cells, bytes_accessed=2 * count * GRID * GRID * cells, transcendentals=0
        ),
        name="grid_weights",
    )(kern_u, kern_v)


def correlate_kernel(sizes, slots_ref, pair_ref, r_ref, k_ref, out_ref, arr, vis, blocks, weights, acc, sem):
    owners, times, frames = sizes
    group2 = r_ref.shape[1]
    total = times * frames
    stations = owners * SBLK
    sides = stations // LANES
    arr_pitch = total + PAD
    vis_pitch = group2 + PAD
    fetch = pltpu.make_async_copy(k_ref, weights, sem)
    fetch.start()

    def turn(t, _):
        for tile in range(frames // 8):
            for side in range(sides):
                got = [
                    r_ref[(side * 8 + i) * times + t, :, tile * LANES : (tile + 1) * LANES]
                    for i in range(8)
                ]
                for i, w in enumerate(swap_groups(got)):
                    arr[side, pl.ds(t * frames + tile * 8 + i, group2, stride=arr_pitch), :] = w.astype(F32)
        return 0

    lax.fori_loop(0, times, turn, 0)

    def correlate(g, _):
        def part(side, c):
            at = pl.ds(pl.multiple_of((2 * g + c) * arr_pitch, 8), total)
            return arr[side, at, :].astype(BF)

        re = [part(side, 0) for side in range(sides)]
        im = [part(side, 1) for side in range(sides)]
        for side in range(sides):
            left = jnp.concatenate(
                [jnp.concatenate(re[: side + 1], axis=1), jnp.concatenate(im[: side + 1], axis=1)], axis=0
            )
            right = jnp.concatenate(
                [
                    jnp.concatenate([re[side], -im[side]], axis=1),
                    jnp.concatenate([im[side], re[side]], axis=1),
                ],
                axis=0,
            )
            z = lax.dot_general(left, right, TN, preferred_element_type=F32)
            for c in range(2):
                vis[side, pl.ds(2 * g + c, (side + 1) * LANES, stride=vis_pitch), :] = z[
                    :, c * LANES : (c + 1) * LANES
                ]
        return 0

    lax.fori_loop(0, group2 // 2, correlate, 0)

    def regroup(p, _):
        for side in range(sides):

            @pl.when(p < side * 8 + 7)
            def _():
                for half in range(2):
                    got = [
                        vis[
                            side,
                            pl.ds(pl.multiple_of((p * SBLK + half * 8 + i) * vis_pitch, 8), group2),
                            :,
                        ].astype(BF)
                        for i in range(8)
                    ]
                    for i, w in enumerate(swap_groups(got)):
                        blocks[p * owners + side * 8 + i, :, half * LANES : (half + 1) * LANES] = w

        return 0

    lax.fori_loop(0, owners - 1, regroup, 0)

    acc[...] = jnp.zeros_like(acc)
    fetch.wait()

    def grid(m, _):
        z = lax.dot_general(blocks[pair_ref[m]], weights[m], NT, preferred_element_type=F32)
        slot = slots_ref[m]
        acc[slot] = acc[slot] + z
        return 0

    lax.fori_loop(0, owners * (owners - 1) // 2, grid, 0, unroll=4)
    out_ref[...] = (acc[...] * (1.0 / math.sqrt(total))).astype(BF)


def correlate(turned, slots, pair, weights, owners, times, frames, tiles):
    group2 = turned.shape[1]
    stations = owners * SBLK
    whole = pl.BlockSpec(memory_space=pltpu.VMEM)
    smem = pl.BlockSpec(memory_space=pltpu.SMEM)
    return pl.pallas_call(
        functools.partial(correlate_kernel, (owners, times, frames)),
        out_shape=jax.ShapeDtypeStruct((tiles, group2, GRID * GRID), BF),
        in_specs=[smem, smem, whole, pl.BlockSpec(memory_space=pl.ANY)],
        out_specs=whole,
        scratch_shapes=[
            pltpu.VMEM((stations // LANES, group2 * (times * frames + PAD), LANES), F32),
            pltpu.VMEM((stations // LANES, stations * (group2 + PAD), LANES), F32),
            pltpu.VMEM((owners * owners, group2, SBLK * SBLK), BF),
            pltpu.VMEM(weights.shape, BF),
            pltpu.VMEM((tiles, group2, GRID * GRID), F32),
            pltpu.SemaphoreType.DMA,
        ],
        compiler_params=pltpu.CompilerParams(vmem_limit_bytes=52 << 20),
        name="correlate",
    )(slots, pair, turned, weights)


def body(samples, taps, block_tile, tile_slots, kern_u, kern_v):
    frame_count = samples.shape[1]
    chan_size = lax.axis_size("chan")
    tm_size = lax.axis_size("tm")
    before = lax.ppermute(
        samples[:, frame_count - HALO :], "tm", [(i, i + 1) for i in range(tm_size - 1)]
    )
    after = lax.ppermute(
        samples[:, :HALO], "tm", [((i + 1) % tm_size, i) for i in range(tm_size)]
    )
    keep = (lax.axis_index("tm") < tm_size - 1).astype(F32).reshape(1)
    weights = grid_weights(kern_u, kern_v)
    spectra = channelize(keep, samples, before, after, taps)
    turned = lax.all_to_all(spectra, ("chan", "tm"), split_axis=0, concat_axis=0, tiled=True)
    left, right = np.triu_indices(chan_size, 1)
    tile_count = tile_slots.shape[0]
    slot_ids = jnp.arange(tile_count, dtype=jnp.int32)
    slots = jnp.sum(
        jnp.where(block_tile[:, None] == tile_slots[None, :], slot_ids[None, :], 0), axis=1
    )
    pair = jnp.asarray(left * chan_size + right, jnp.int32)
    grids = correlate(turned, slots, pair, weights, chan_size, tm_size, frame_count, tile_count)
    width = grids.shape[1] // 2
    partial_value = grids.reshape(tile_count, width, 2, GRID * GRID)
    return lax.all_to_all(partial_value, "tm", split_axis=0, concat_axis=1, tiled=True).astype(F32)


def solution(mesh):
    placed = (P("chan", "tm", None), P(), P(), P(), P(), P())
    return jax.shard_map(
        body, mesh=mesh, in_specs=placed, out_specs=P("tm", "chan", None, None), check_vma=False
    )
```

time: 164 us -> 130 us (0.79)
  waiting for transfers between devices: 64 us -> 44.9 us
  Pallas kernels: 67.4 us -> 48.7 us
  local copies, waits for them, and re-layouts: 3.15 us -> 9.8 us
  blocking collectives: 13.1 us -> 10.2 us
    ppermute x1, waiting for transfers between devices: 23 us -> 1.25 us  [body(): lax.ppermute(samples[:, frame_count - HALO:], 'tm', [(i, i + 1) for i in...]
    pallas_call x1, Pallas kernels: 41.1 us -> 26.5 us  [correlate(): pl.pallas_call(functools.partial(correlate_kernel, (owners, times, frames...]
    ppermute x0 -> x1, waiting for transfers between devices: none -> 10.8 us  [body(): lax.ppermute(samples[:, :HALO], 'tm', [((i + 1) % tm_size, i) for i in ra...]
    all_to_all x1, waiting for transfers between devices: 41 us -> 32.9 us  [body(): lax.all_to_all(spectra, ('chan', 'tm'), split_axis=0, concat_axis=0, tile...]
    pallas_call x1, Pallas kernels: 26.3 us -> 19.6 us  [channelize(): pl.pallas_call(channelize_kernel, out_shape=jax.ShapeDtypeStruct((dests,...]
    unnamed x16, local copies, waits for them, and re-layouts: 0.04 us -> 5.53 us
    all_to_all x1, blocking collectives: 13.1 us -> 10.2 us  [body(): lax.all_to_all(partial_value, 'tm', split_axis=0, concat_axis=1, tiled=True)]
    pallas_call x0 -> x1, Pallas kernels: none -> 2.6 us  [grid_weights(): pl.pallas_call(weights_kernel, grid=(count // step,), out_shape=jax.Shape...]
  transfers between devices with their start and end apart: 2 -> 3, of which waited for: 2 -> 3; matrix products, arithmetic and copies ran while one was open for 0% -> 0% of each run, Pallas kernels for 0% -> 2%
where the time goes in v2:
time: 130 us
  Pallas kernels  48.7 us (37%)
  waiting for transfers between devices  44.9 us (35%)
  starting transfers between devices  16.2 us (12%)
  blocking collectives  10.2 us (8%)
  local copies, waits for them, and re-layouts  9.8 us (8%)
    all_to_all x1, waiting for transfers between devices, body(): lax.all_to_all(spectra, ('chan', 'tm'), split_axis=0, concat_axis=0, tile...  32.9 us
    pallas_call x1, Pallas kernels, correlate(): pl.pallas_call(functools.partial(correlate_kernel, (owners, times, frames...  26.5 us
    pallas_call x1, Pallas kernels, channelize(): pl.pallas_call(channelize_kernel, out_shape=jax.ShapeDtypeStruct((dests,...  19.6 us
    all_to_all x1, starting transfers between devices, body(): lax.all_to_all(spectra, ('chan', 'tm'), split_axis=0, concat_axis=0, tile...  11.3 us
    ppermute x1, waiting for transfers between devices, body(): lax.ppermute(samples[:, :HALO], 'tm', [((i + 1) % tm_size, i) for i in ra...  10.8 us
    all_to_all x1, blocking collectives, body(): lax.all_to_all(partial_value, 'tm', split_axis=0, concat_axis=1, tiled=True)  10.2 us
    unnamed x16, local copies, waits for them, and re-layouts  5.53 us
    ppermute x1, starting transfers between devices, body(): lax.ppermute(samples[:, frame_count - HALO:], 'tm', [(i, i + 1) for i in...  3.5 us
  transfers between devices with their start and end apart: 3, of which 3 were waited for; matrix products, arithmetic and copies ran while one was open for 0% of the time, Pallas kernels for 2%

profile of v2, /device:TPU:1, one launch (start us, length us, event | category | flops | bytes accessed | tf_op | source)
XLA Modules:
  0.0 129.9 jit_solution(8733341332595534105)
XLA Ops:
  0.0 0.0 copy-start.4
  0.0 0.0 copy-start.3
  0.0 3.2 %fusion = (bf16[16,8,4096]{2,1,0:T(8,128)(2,1)}, bf16[16,8,4096]{2,1,0:T(8,128)(2,1)}) fusion(bf16[16,24,4096]{2,1,0:T(8,128)(2,1)} %x_ref.1), kind=kLoop, calls=%fused_computation.1 | loop fusion | bytes 4194304 | tf_op jit(solution)/shard_map/slice | solution.py:336
  3.2 1.4 %collective-permute-start.1 = (bf16[16,8,4096]{2,1,0:T(8,128)(2,1)}, bf16[16,8,4096]{2,1,0:T(8,128)(2,1)S(1)}, u32[]{:S(2)}, u32[]{:S(2)}) collective-permute-start(bf16[16,8,4096]{2,1,0:T(8,128)(2,1)} %get-tuple-element.5), channel_id=1, source_target_pairs={{1,0},{2,1},{3,2},{4,3},{5,4},{6,5},{7,6},{0,7},{9,8},{10,9},{11,1... | collective-permute-start | bytes 3145736 | tf_op jit(solution)/shard_map/ppermute | solution.py:335
  4.6 3.5 %collective-permute-start = (bf16[16,8,4096]{2,1,0:T(8,128)(2,1)}, bf16[16,8,4096]{2,1,0:T(8,128)(2,1)S(1)}, u32[]{:S(2)}, u32[]{:S(2)}) collective-permute-start(bf16[16,8,4096]{2,1,0:T(8,128)(2,1)} %get-tuple-element.6), channel_id=1, source_target_pairs={{0,1},{1,2},{2,3},{3,4},{4,5},{5,6},{6,7},{8,9},{9,10},{10,11},{11... | collective-permute-start | bytes 3145736 | tf_op jit(solution)/shard_map/ppermute | solution.py:332
  8.1 10.8 %collective-permute-done.1.right_ref = bf16[16,8,4096]{2,1,0:T(8,128)(2,1)S(1)} collective-permute-done((bf16[16,8,4096]{2,1,0:T(8,128)(2,1)}, bf16[16,8,4096]{2,1,0:T(8,128)(2,1)S(1)}, u32[]{:S(2)}, u32[]{:S(2)}) %collective-permute-start.1) | collective-permute-done | bytes 1048608 | tf_op jit(solution)/shard_map/ppermute | solution.py:335
  18.9 1.3 collective-permute-done.left_ref
  20.1 0.0 copy-done.4
  20.1 0.0 copy-done.3
  20.1 19.6 %channelize.1 = bf16[128,32,384]{2,1,0:T(8,128)(2,1)} custom-call(f32[1]{0:T(128)} %bitcast.keep_ref, bf16[16,24,4096]{2,1,0:T(8,128)(2,1)} %x_ref.1, bf16[16,8,4096]{2,1,0:T(8,128)(2,1)S(1)} %collective-permute-done.left_ref, bf16[16,8,4096]{2,1,0:T(8,128)(2,1)S(1)} %collective-permute-done.1.right_ref, f32[16,4096]{1,0:T(8,128)S(1)} %copy-done.3, ...), custom_call_target="tpu_custom_call" | custom-call | tf_op jit(solution)/shard_map/channelize/pallas_call | solution.py:163
  39.7 0.0 copy-start.1
  39.7 0.0 copy-start.2
  39.7 11.3 %all-to-all-start = ((bf16[128,32,384]{2,1,0:T(8,128)(2,1)}), bf16[128,32,384]{2,1,0:T(8,128)(2,1)}, u32[]{:S(2)}, u32[]{:S(2)}) async-start(bf16[128,32,384]{2,1,0:T(8,128)(2,1)} %channelize.1), calls=%async_computation | async-start | bytes 6291456 | tf_op jit(solution)/shard_map/all_to_all | solution.py:341
  51.0 0.0 copy-done.1
  51.0 0.0 copy-done.2
  51.0 0.0 copy-start.6
  51.0 0.0 copy-start.7
  51.0 0.0 copy-start.5
  51.0 2.6 %grid_weights.1.k_ref = bf16[120,256,256]{2,1,0:T(8,128)(2,1)S(1)} custom-call(bf16[16,30720]{1,0:T(8,128)(2,1)S(1)} %copy-done.1, bf16[16,30720]{1,0:T(8,128)(2,1)S(1)} %copy-done.2), custom_call_target="tpu_custom_call" | custom-call | flops 7864320 | bytes 15728640 | tf_op jit(solution)/shard_map/grid_weights/pallas_call | solution.py:206
  53.6 0.0 copy-start
  53.6 5.5 %copy-done = bf16[120,256,256]{2,1,0:T(8,128)(2,1)} copy-done((bf16[120,256,256]{2,1,0:T(8,128)(2,1)}, bf16[120,256,256]{2,1,0:T(8,128)(2,1)S(1)}, u32[]{:S(2)}) %copy-start) | copy-done | bytes 15728664
  59.1 0.0 copy-done.6
  59.1 0.0 copy-done.7
  59.1 0.1 select_reduce_fusion.slots_ref
  59.2 32.9 %all-to-all-done.r_ref = bf16[128,32,384]{2,1,0:T(8,128)(2,1)} async-done(((bf16[128,32,384]{2,1,0:T(8,128)(2,1)}), bf16[128,32,384]{2,1,0:T(8,128)(2,1)}, u32[]{:S(2)}, u32[]{:S(2)}) %all-to-all-start) | async-done | bytes 3145760 | tf_op jit(solution)/shard_map/all_to_all | solution.py:341
  92.1 0.0 copy-done.5
  92.1 26.5 %correlate.1 = bf16[16,32,256]{2,1,0:T(8,128)(2,1)S(1)} custom-call(s32[120]{0:T(128)S(1)} %select_reduce_fusion.slots_ref, s32[120]{0:T(128)S(1)} %copy-done.5, bf16[128,32,384]{2,1,0:T(8,128)(2,1)} %all-to-all-done.r_ref, bf16[120,256,256]{2,1,0:T(8,128)(2,1)} %copy-done), custom_call_target="tpu_custom_call" | custom-call | tf_op jit(solution)/shard_map/correlate/pallas_call | solution.py:310
  118.6 0.1 reshape.16
  118.7 10.2 %all_to_all.14 = bf16[16,16,2,256]{3,2,1,0:T(2,128)(2,1)S(1)} all-to-all(bf16[16,16,2,256]{3,2,1,0:T(2,128)(2,1)S(1)} %reshape.16), channel_id=1, replica_groups=mesh['chan'=16,'tm'=8] {'tm'}, dimensions={0} | all-to-all | bytes 524288 | tf_op jit(solution)/shard_map/all_to_all | solution.py:352
  128.9 1.0 copy.11
Async XLA Ops:
  0.0 20.1 %copy-start.4 = (bf16[2,256,256]{2,1,0:T(8,128)(2,1)S(1)}, bf16[2,256,256]{2,1,0:T(8,128)(2,1)}, u32[]{:S(2)}) copy-start(bf16[2,256,256]{2,1,0:T(8,128)(2,1)} %constant.15.clone.ends_ref) | copy-start | bytes 786436
  0.0 20.1 %copy-start.3 = (f32[16,4096]{1,0:T(8,128)S(1)}, f32[16,4096]{1,0:T(8,128)}, u32[]{:S(2)}) copy-start(f32[16,4096]{1,0:T(8,128)} %taps_ref.1) | copy-start | bytes 786436
  3.2 15.7 %collective-permute-start.1 = (bf16[16,8,4096]{2,1,0:T(8,128)(2,1)}, bf16[16,8,4096]{2,1,0:T(8,128)(2,1)S(1)}, u32[]{:S(2)}, u32[]{:S(2)}) collective-permute-start(bf16[16,8,4096]{2,1,0:T(8,128)(2,1)} %get-tuple-element.5), channel_id=1, source_target_pairs={{1,0},{2,1},{3,2},{4,3},{5,4},{6,5},{7,6},{0,7},{9,8},{10,9},{11,1... | collective-permute-start | bytes 3145736 | tf_op jit(solution)/shard_map/ppermute | solution.py:335
  4.6 15.6 %collective-permute-start = (bf16[16,8,4096]{2,1,0:T(8,128)(2,1)}, bf16[16,8,4096]{2,1,0:T(8,128)(2,1)S(1)}, u32[]{:S(2)}, u32[]{:S(2)}) collective-permute-start(bf16[16,8,4096]{2,1,0:T(8,128)(2,1)} %get-tuple-element.6), channel_id=1, source_target_pairs={{0,1},{1,2},{2,3},{3,4},{4,5},{5,6},{6,7},{8,9},{9,10},{10,11},{11... | collective-permute-start | bytes 3145736 | tf_op jit(solution)/shard_map/ppermute | solution.py:332
  39.7 11.3 %copy-start.1 = (bf16[16,30720]{1,0:T(8,128)(2,1)S(1)}, bf16[16,30720]{1,0:T(8,128)(2,1)}, u32[]{:S(2)}) copy-start(bf16[16,30720]{1,0:T(8,128)(2,1)} %u_ref.1) | copy-start | bytes 2949124
  39.7 11.3 %copy-start.2 = (bf16[16,30720]{1,0:T(8,128)(2,1)S(1)}, bf16[16,30720]{1,0:T(8,128)(2,1)}, u32[]{:S(2)}) copy-start(bf16[16,30720]{1,0:T(8,128)(2,1)} %v_ref.1) | copy-start | bytes 2949124
  39.7 52.4 %all-to-all-start = ((bf16[128,32,384]{2,1,0:T(8,128)(2,1)}), bf16[128,32,384]{2,1,0:T(8,128)(2,1)}, u32[]{:S(2)}, u32[]{:S(2)}) async-start(bf16[128,32,384]{2,1,0:T(8,128)(2,1)} %channelize.1), calls=%async_computation | async-start | bytes 6291456 | tf_op jit(solution)/shard_map/all_to_all | solution.py:341
  51.0 8.2 %copy-start.6 = (s32[120]{0:T(128)S(1)}, s32[120]{0:T(128)}, u32[]{:S(2)}) copy-start(s32[120]{0:T(128)} %param.11) | copy-start | bytes 1444
  51.0 8.1 %copy-start.7 = (s32[16]{0:T(128)S(1)}, s32[16]{0:T(128)}, u32[]{:S(2)}) copy-start(s32[16]{0:T(128)} %param.12) | copy-start | bytes 196
  51.0 41.1 %copy-start.5 = (s32[120]{0:T(128)S(1)}, s32[120]{0:T(128)}, u32[]{:S(2)}) copy-start(s32[120]{0:T(128)} %constant.16.clone.pair_ref) | copy-start | bytes 1444
  53.6 5.5 %copy-start = (bf16[120,256,256]{2,1,0:T(8,128)(2,1)}, bf16[120,256,256]{2,1,0:T(8,128)(2,1)S(1)}, u32[]{:S(2)}) copy-start(bf16[120,256,256]{2,1,0:T(8,128)(2,1)S(1)} %grid_weights.1.k_ref) | copy-start | bytes 47185924

commit v3 on v2

v3 whole, which is shorter than its diff:
```python
import functools
import math

import jax
import jax.numpy as jnp
import ml_dtypes
import numpy as np
from jax import lax
from jax.experimental import pallas as pl
from jax.experimental.pallas import tpu as pltpu
from jax.sharding import PartitionSpec as P

SBLK = 16
GRID = 16
RADIX = 16
HALO = 8
PITCH = 24
PAD = 8
LANES = 128
BF = jnp.bfloat16
F32 = jnp.float32
NT = (((1,), (1,)), ((), ()))
TN = (((0,), (0,)), ((), ()))


def dft_tables(length):
    span = length // RADIX
    place = np.arange(span)[None, :]
    dest = np.arange(length // (2 * RADIX))[:, None]

    def table(low):
        angle = (place * (low + RADIX * dest) % length) * (2.0 * np.pi / length)
        c, s = np.cos(angle), np.sin(angle)
        sign = -1.0 if low > RADIX // 2 else 1.0
        return np.block([[c, sign * s], [-s, sign * c]]) / math.sqrt(length)

    pairs = np.stack(
        [np.concatenate([table(k), table(RADIX - k)], axis=0) for k in range(1, RADIX // 2)]
    )
    ends = np.stack([table(0)[:, :span], table(RADIX // 2)[:, :span]])
    return pairs.astype(ml_dtypes.bfloat16), ends.astype(ml_dtypes.bfloat16)


def real_dft(x):
    n = len(x)
    if n == 2:
        return [(x[0] + x[1], None), (x[0] - x[1], None)]
    even, odd = real_dft(x[0::2]), real_dft(x[1::2])
    out = [None] * (n // 2 + 1)
    for k in range(n // 4 + 1):
        er, ei = even[k]
        dr, di = odd[k]
        if k == 0:
            out[0], out[n // 2] = (er + dr, None), (er - dr, None)
        elif k == n // 4:
            out[k] = (er, -dr)
        else:
            c, s = math.cos(2 * math.pi * k / n), math.sin(2 * math.pi * k / n)
            if 8 * k == n:
                tr, ti = (dr + di) * c, (di - dr) * c
            else:
                tr, ti = dr * c + di * s, di * c - dr * s
            out[k] = (er + tr, ei + ti)
            out[n // 2 - k] = (er - tr, ti - ei)
    return out


def spread(source, target, first, at):
    for s in range(source.shape[0]):
        target[pl.ds(first * PITCH + s, source.shape[1], stride=PITCH), :] = source[s, :, at].astype(F32)


def butterflies(filt, low, half):
    to = slice(half * LANES, (half + 1) * LANES)

    def butterfly(b, _):
        at = pl.ds(pl.multiple_of(b * SBLK, SBLK), SBLK)
        parts = real_dft([filt[tile, at, :].astype(F32) for tile in range(RADIX)])
        for k, (re, im) in enumerate(parts):
            low[k, at, to] = re.astype(BF)
            if im is not None:
                low[RADIX // 2 + k, at, to] = im.astype(BF)
        return 0

    lax.fori_loop(0, filt.shape[1] // SBLK, butterfly, 0, unroll=2)


def products(low, turned, pairs_ref, ends_ref):
    dests = ends_ref.shape[1] // 2
    pitch = 2 * RADIX + PAD

    def keep(channel, part, value):
        for tile in range(low.shape[1] // LANES):
            turned[tile, pl.ds(channel * 2 + part, dests, stride=pitch), :] = value[
                :, tile * LANES : (tile + 1) * LANES
            ]

    for end in range(2):
        z = lax.dot_general(
            ends_ref[end], low[end * (RADIX // 2)], NT, preferred_element_type=F32
        )
        for part in range(2):
            keep(end * (RADIX // 2), part, z[part * dests : (part + 1) * dests])

    def pair(k, _):
        spectrum = jnp.concatenate([low[k], low[RADIX // 2 + k]], axis=1)
        for mirrored in range(2):
            z = lax.dot_general(
                pairs_ref[k - 1, mirrored * 2 * dests : (mirrored + 1) * 2 * dests, :],
                spectrum,
                NT,
                preferred_element_type=F32,
            )
            channel = RADIX - k if mirrored else k
            for part in range(2):
                keep(channel, part, z[part * dests : (part + 1) * dests])
        return 0

    lax.fori_loop(1, RADIX // 2, pair, 0)


def own_kernel(keep_ref, x_ref, taps_ref, pairs_ref, ends_ref, out_ref, part_ref, xs, filt, low, turned):
    stations, frames, length = x_ref.shape
    taps = taps_ref.shape[0]
    span = length // RADIX
    own = keep_ref[0]
    done = range(HALO, 2 * HALO)

    for half in range(span // LANES):

        def fir(tile, _):
            at = pl.ds(pl.multiple_of(tile * span + half * LANES, LANES), LANES)
            spread(x_ref, xs, 0, at)
            weights = [taps_ref[pl.ds(k, 1), at] for k in range(taps)]
            sums = {}
            for step in range(frames):
                x = xs[step * PITCH : step * PITCH + stations, :]
                for k in range(taps - 1, -1, -1):
                    b = step + HALO - (taps - 1) + k
                    if 0 <= b < frames:
                        term = weights[k] * x
                        sums[b] = sums[b] + term if b in sums else term
                ready = [b for b in sums if b == step + HALO - (taps - 1) or step == frames - 1]
                for b in ready:
                    value = sums.pop(b)
                    if b in done:
                        place = b - done.start
                        filt[tile, place * stations : (place + 1) * stations, :] = value.astype(BF)
                    else:
                        place = b if b < done.start else b - len(done)
                        if b + taps - 1 >= HALO + frames:
                            value = own * value
                        part_ref[2 * tile + half, place * stations : (place + 1) * stations, :] = value
            return 0

        lax.fori_loop(0, RADIX, fir, 0)
        butterflies(filt, low, half)

    products(low, turned, pairs_ref, ends_ref)

    def give(d, _):
        at = pl.ds(pl.multiple_of(d * (2 * RADIX + PAD), 8), 2 * RADIX)
        out_ref[d] = turned[0, at, :].astype(BF)
        return 0

    lax.fori_loop(0, out_ref.shape[0], give, 0, unroll=8)


def rest_kernel(left_ref, right_ref, taps_ref, pairs_ref, ends_ref, done_ref, part_ref, out_ref, xs, filt, low, turned):
    stations, _, length = left_ref.shape
    taps = taps_ref.shape[0]
    span = length // RADIX
    count = part_ref.shape[1] // stations

    for half in range(span // LANES):

        def fir(tile, _):
            at = pl.ds(pl.multiple_of(tile * span + half * LANES, LANES), LANES)
            spread(left_ref, xs, 0, at)
            spread(right_ref, xs, HALO, at)
            weights = [taps_ref[pl.ds(k, 1), at] for k in range(taps)]
            x = [xs[step * PITCH : step * PITCH + stations, :] for step in range(2 * HALO)]
            for place in range(count):
                to = slice(place * stations, (place + 1) * stations)
                value = part_ref[2 * tile + half, to, :]
                if place < HALO:
                    terms = [(j, taps - 1 - (j - place)) for j in range(place, HALO)]
                else:
                    first = place - (count - (HALO - 1))
                    terms = [(HALO + j, first - j) for j in range(first + 1)]
                for j, k in terms:
                    value = value + weights[k] * x[j]
                filt[tile, to, :] = value.astype(BF)
            return 0

        lax.fori_loop(0, RADIX, fir, 0)
        butterflies(filt, low, half)

    products(low, turned, pairs_ref, ends_ref)
    tiles = low.shape[1] // LANES

    def give(d, _):
        at = pl.ds(pl.multiple_of(d * (2 * RADIX + PAD), 8), 2 * RADIX)
        for tile in range(tiles):
            out_ref[d, :, tile * LANES : (tile + 1) * LANES] = turned[tile, at, :].astype(BF)
        out_ref[d, :, tiles * LANES :] = done_ref[d]
        return 0

    lax.fori_loop(0, out_ref.shape[0], give, 0, unroll=8)


def channel_scratch(frames, steps, length):
    rows = frames * SBLK
    return [
        pltpu.VMEM((steps * PITCH, LANES), F32),
        pltpu.VMEM((RADIX, rows, LANES), BF),
        pltpu.VMEM((RADIX, rows, length // RADIX), BF),
        pltpu.VMEM((rows // LANES, length // (2 * RADIX) * (2 * RADIX + PAD), LANES), F32),
    ]


def channelize_own(keep, samples, taps, pairs, ends):
    stations, frames, length = samples.shape
    dests = length // (2 * RADIX)
    whole = pl.BlockSpec(memory_space=pltpu.VMEM)
    return pl.pallas_call(
        own_kernel,
        out_shape=[
            jax.ShapeDtypeStruct((dests, 2 * RADIX, HALO * stations), BF),
            jax.ShapeDtypeStruct((length // LANES, (frames - HALO) * stations, LANES), F32),
        ],
        in_specs=[pl.BlockSpec(memory_space=pltpu.SMEM)] + [whole] * 4,
        out_specs=[whole] * 2,
        scratch_shapes=channel_scratch(HALO, frames, length),
        compiler_params=pltpu.CompilerParams(vmem_limit_bytes=32 << 20),
        cost_estimate=pl.CostEstimate(
            flops=10 * samples.size * 1000, bytes_accessed=20 << 20, transcendentals=0
        ),
        name="own",
    )(keep, samples, taps, pairs, ends)


def channelize_rest(before, after, taps, pairs, ends, done, part):
    stations, _, length = before.shape
    dests = length // (2 * RADIX)
    frames = part.shape[1] // stations
    whole = pl.BlockSpec(memory_space=pltpu.VMEM)
    return pl.pallas_call(
        rest_kernel,
        out_shape=jax.ShapeDtypeStruct((dests, 2 * RADIX, part.shape[1] + done.shape[2]), BF),
        in_specs=[whole] * 7,
        out_specs=whole,
        scratch_shapes=channel_scratch(frames, 2 * HALO, length),
        compiler_params=pltpu.CompilerParams(vmem_limit_bytes=32 << 20),
        name="rest",
    )(before, after, taps, pairs, ends, done, part)


def swap_groups(v):
    lane = lax.broadcasted_iota(jnp.int32, v[0].shape, 1)
    v = list(v)
    for bit in (1, 2, 4):
        low = (lane // (bit * SBLK)) % 2 == 0
        for i in range(8):
            if not i & bit:
                a, b = v[i], v[i + bit]
                v[i] = jnp.where(low, a, pltpu.roll(b, bit * SBLK, 1))
                v[i + bit] = jnp.where(low, pltpu.roll(a, LANES - bit * SBLK, 1), b)
    return v


def weights_kernel(u_ref, v_ref, out_ref):
    cells = SBLK * SBLK
    for m in range(out_ref.shape[0]):
        u = u_ref[:, m * cells : (m + 1) * cells].astype(F32)
        v = v_ref[:, m * cells : (m + 1) * cells].astype(F32)
        cell_rows = jnp.concatenate([u[i : i + 1, :] * v for i in range(GRID)], axis=0)
        out_ref[m] = cell_rows.T.astype(BF)


def grid_weights(kern_u, kern_v):
    cells = SBLK * SBLK
    count = kern_u.shape[1] // cells
    step = math.gcd(count, 8)
    part = pl.BlockSpec((GRID, step * cells), lambda m: (0, m))
    return pl.pallas_call(
        weights_kernel,
        grid=(count // step,),
        out_shape=jax.ShapeDtypeStruct((count, cells, GRID * GRID), BF),
        in_specs=[part, part],
        out_specs=pl.BlockSpec((step, cells, GRID * GRID), lambda m: (m, 0, 0)),
        compiler_params=pltpu.CompilerParams(vmem_limit_bytes=16 << 20),
        cost_estimate=pl.CostEstimate(
            flops=count * GRID * GRID * cells, bytes_accessed=2 * count * GRID * GRID * cells, transcendentals=0
        ),
        name="grid_weights",
    )(kern_u, kern_v)


def correlate_kernel(sizes, slots_ref, r_ref, k_ref, out_ref, arr, vis, weights, acc, sem):
    owners, times, frames = sizes
    group2 = r_ref.shape[1]
    total = times * frames
    stations = owners * SBLK
    sides = stations // LANES
    arr_pitch = total + PAD
    vis_pitch = group2 + PAD
    fetch = pltpu.make_async_copy(k_ref, weights, sem)
    fetch.start()

    def turn(t, _):
        for tile in range(frames // 8):
            for side in range(sides):
                got = [
                    r_ref[(side * 8 + i) * times + t, :, tile * LANES : (tile + 1) * LANES]
                    for i in range(8)
                ]
                for i, w in enumerate(swap_groups(got)):
                    arr[side, pl.ds(t * frames + tile * 8 + i, group2, stride=arr_pitch), :] = w.astype(F32)
        return 0

    lax.fori_loop(0, times, turn, 0)

    def correlate(g, _):
        def part(side, c):
            at = pl.ds(pl.multiple_of((2 * g + c) * arr_pitch, 8), total)
            return arr[side, at, :].astype(BF)

        re = [part(side, 0) for side in range(sides)]
        im = [part(side, 1) for side in range(sides)]
        for side in range(sides):
            left = jnp.concatenate(
                [jnp.concatenate(re[: side + 1], axis=1), jnp.concatenate(im[: side + 1], axis=1)], axis=0
            )
            right = jnp.concatenate(
                [
                    jnp.concatenate([re[side], -im[side]], axis=1),
                    jnp.concatenate([im[side], re[side]], axis=1),
                ],
                axis=0,
            )
            z = lax.dot_general(left, right, TN, preferred_element_type=F32)
            for c in range(2):
                vis[side, pl.ds(2 * g + c, (side + 1) * LANES, stride=vis_pitch), :] = z[
                    :, c * LANES : (c + 1) * LANES
                ]
        return 0

    lax.fori_loop(0, group2 // 2, correlate, 0, unroll=2)

    acc[...] = jnp.zeros_like(acc)
    fetch.wait()

    m = 0
    for p in range(owners - 1):
        halves = {}
        for side in range(sides):
            if p >= side * 8 + 7:
                continue
            for half in range(2):
                got = [
                    vis[side, pl.ds((p * SBLK + half * 8 + i) * vis_pitch, group2), :].astype(BF)
                    for i in range(8)
                ]
                for i, w in enumerate(swap_groups(got)):
                    halves[side * 8 + i, half] = w
        for q in range(p + 1, owners):
            block = jnp.concatenate([halves[q, 0], halves[q, 1]], axis=1)
            z = jnp.dot(block, weights[m], preferred_element_type=F32)
            slot = slots_ref[m]
            acc[slot] = acc[slot] + z
            m += 1
    out_ref[...] = (acc[...] * (1.0 / math.sqrt(total))).astype(BF)


def correlate(turned, slots, weights, owners, times, frames, tiles):
    group2 = turned.shape[1]
    stations = owners * SBLK
    whole = pl.BlockSpec(memory_space=pltpu.VMEM)
    smem = pl.BlockSpec(memory_space=pltpu.SMEM)
    return pl.pallas_call(
        functools.partial(correlate_kernel, (owners, times, frames)),
        out_shape=jax.ShapeDtypeStruct((tiles, group2, GRID * GRID), BF),
        in_specs=[smem, whole, pl.BlockSpec(memory_space=pl.ANY)],
        out_specs=whole,
        scratch_shapes=[
            pltpu.VMEM((stations // LANES, group2 * (times * frames + PAD), LANES), F32),
            pltpu.VMEM((stations // LANES, stations * (group2 + PAD), LANES), F32),
            pltpu.VMEM(weights.shape, BF),
            pltpu.VMEM((tiles, group2, GRID * GRID), F32),
            pltpu.SemaphoreType.DMA,
        ],
        compiler_params=pltpu.CompilerParams(vmem_limit_bytes=42 << 20),
        name="correlate",
    )(slots, turned, weights)


def body(samples, taps, block_tile, tile_slots, kern_u, kern_v):
    frame_count = samples.shape[1]
    chan_size = lax.axis_size("chan")
    tm_size = lax.axis_size("tm")
    before = lax.ppermute(
        samples[:, frame_count - HALO :], "tm", [(i, i + 1) for i in range(tm_size - 1)]
    )
    after = lax.ppermute(
        samples[:, :HALO], "tm", [((i + 1) % tm_size, i) for i in range(tm_size)]
    )
    keep = (lax.axis_index("tm") < tm_size - 1).astype(F32).reshape(1)
    weights = grid_weights(kern_u, kern_v)
    pairs, ends = (jnp.asarray(table) for table in dft_tables(samples.shape[2]))
    done, part = channelize_own(keep, samples, taps, pairs, ends)
    spectra = channelize_rest(before, after, taps, pairs, ends, done, part)
    turned = lax.all_to_all(spectra, ("chan", "tm"), split_axis=0, concat_axis=0, tiled=True)
    tile_count = tile_slots.shape[0]
    slot_ids = jnp.arange(tile_count, dtype=jnp.int32)
    slots = jnp.sum(
        jnp.where(block_tile[:, None] == tile_slots[None, :], slot_ids[None, :], 0), axis=1
    )
    grids = correlate(turned, slots, weights, chan_size, tm_size, frame_count, tile_count)
    width = grids.shape[1] // 2
    partial_value = grids.reshape(tile_count, width, 2, GRID * GRID)
    return lax.all_to_all(partial_value, "tm", split_axis=0, concat_axis=1, tiled=True).astype(F32)


def solution(mesh):
    placed = (P("chan", "tm", None), P(), P(), P(), P(), P())
    return jax.shard_map(
        body, mesh=mesh, in_specs=placed, out_specs=P("tm", "chan", None, None), check_vma=False
    )
```

time: 130 us -> 108 us (0.83)
  waiting for transfers between devices: 44.9 us -> 28 us
  Pallas kernels: 48.7 us -> 39.5 us
  local copies, waits for them, and re-layouts: 9.8 us -> 15.2 us
  starting transfers between devices: 16.2 us -> 14.8 us
    pallas_call x1, Pallas kernels: 26.5 us -> 13.6 us  [correlate(): pl.pallas_call(functools.partial(correlate_kernel, (owners, times, frames...]
    ppermute x1, waiting for transfers between devices: 10.8 us -> 0.01 us  [body(): lax.ppermute(samples[:, :HALO], 'tm', [((i + 1) % tm_size, i) for i in ra...]
    unnamed x16 -> x20, local copies, waits for them, and re-layouts: 5.53 us -> 10.9 us
    all_to_all x1, waiting for transfers between devices: 32.9 us -> 28 us  [body(): lax.all_to_all(spectra, ('chan', 'tm'), split_axis=0, concat_axis=0, tile...]
    pallas_call x1, Pallas kernels: 2.6 us -> 5.46 us  [grid_weights(): pl.pallas_call(weights_kernel, grid=(count // step,), out_shape=jax.Shape...]
    all_to_all x1, starting transfers between devices: 11.3 us -> 9.85 us  [body(): lax.all_to_all(spectra, ('chan', 'tm'), split_axis=0, concat_axis=0, tile...]
    pallas_call x1 -> x2, Pallas kernels: 19.6 us -> 20.4 us  [the longest x1 10.4 us: channelize_rest(): pl.pallas_call(rest_kernel, out_shape=jax.ShapeDtypeStruct((dests, 2 * RA...]
  transfers between devices with their start and end apart: 3 -> 3, of which waited for: 3 -> 1; matrix products, arithmetic and copies ran while one was open for 0% -> 0% of each run, Pallas kernels for 2% -> 14%
where the time goes in v3:
time: 108 us
  Pallas kernels  39.5 us (37%)
  waiting for transfers between devices  28 us (26%)
  local copies, waits for them, and re-layouts  15.2 us (14%)
  starting transfers between devices  14.8 us (14%)
  blocking collectives  10.2 us (9%)
    all_to_all x1, waiting for transfers between devices, body(): lax.all_to_all(spectra, ('chan', 'tm'), split_axis=0, concat_axis=0, tile...  28 us
    pallas_call x1, Pallas kernels, correlate(): pl.pallas_call(functools.partial(correlate_kernel, (owners, times, frames...  13.6 us
    unnamed x20, local copies, waits for them, and re-layouts  10.9 us
    pallas_call x1, Pallas kernels, channelize_rest(): pl.pallas_call(rest_kernel, out_shape=jax.ShapeDtypeStruct((dests, 2 * RA...  10.4 us
    all_to_all x1, blocking collectives, body(): lax.all_to_all(partial_value, 'tm', split_axis=0, concat_axis=1, tiled=True)  10.2 us
    pallas_call x1, Pallas kernels, channelize_own(): pl.pallas_call(own_kernel, out_shape=[jax.ShapeDtypeStruct((dests, 2 * RA...  10.1 us
    all_to_all x1, starting transfers between devices, body(): lax.all_to_all(spectra, ('chan', 'tm'), split_axis=0, concat_axis=0, tile...  9.85 us
    pallas_call x1, Pallas kernels, grid_weights(): pl.pallas_call(weights_kernel, grid=(count // step,), out_shape=jax.Shape...  5.46 us
  transfers between devices with their start and end apart: 3, of which 1 were waited for; matrix products, arithmetic and copies ran while one was open for 0% of the time, Pallas kernels for 14%

profile of v3, /device:TPU:1, one launch (start us, length us, event | category | flops | bytes accessed | tf_op | source)
XLA Modules:
  0.0 107.9 jit_solution(6762866393590170263)
XLA Ops:
  0.0 0.0 copy-start.3
  0.0 0.0 copy-start.6
  0.0 3.2 %fusion = (bf16[16,8,4096]{2,1,0:T(8,128)(2,1)}, bf16[16,8,4096]{2,1,0:T(8,128)(2,1)}) fusion(bf16[16,24,4096]{2,1,0:T(8,128)(2,1)} %x_ref.1), kind=kLoop, calls=%fused_computation.1 | loop fusion | bytes 4194304 | tf_op jit(solution)/shard_map/slice | solution.py:406
  3.2 1.4 %collective-permute-start.1 = (bf16[16,8,4096]{2,1,0:T(8,128)(2,1)}, bf16[16,8,4096]{2,1,0:T(8,128)(2,1)}, u32[]{:S(2)}, u32[]{:S(2)}) collective-permute-start(bf16[16,8,4096]{2,1,0:T(8,128)(2,1)} %get-tuple-element.9), channel_id=1, source_target_pairs={{1,0},{2,1},{3,2},{4,3},{5,4},{6,5},{7,6},{0,7},{9,8},{10,9},{11,1... | collective-permute-start | bytes 3145736 | tf_op jit(solution)/shard_map/ppermute | solution.py:405
  4.6 3.5 %collective-permute-start = (bf16[16,8,4096]{2,1,0:T(8,128)(2,1)}, bf16[16,8,4096]{2,1,0:T(8,128)(2,1)}, u32[]{:S(2)}, u32[]{:S(2)}) collective-permute-start(bf16[16,8,4096]{2,1,0:T(8,128)(2,1)} %get-tuple-element.10), channel_id=1, source_target_pairs={{0,1},{1,2},{2,3},{3,4},{4,5},{5,6},{6,7},{8,9},{9,10},{10,11},{11... | collective-permute-start | bytes 3145736 | tf_op jit(solution)/shard_map/ppermute | solution.py:402
  8.2 0.0 copy-done.3
  8.2 0.0 copy-done.6
  8.2 0.0 copy-start.1
  8.2 2.0 %copy-done.1 = bf16[7,512,512]{2,1,0:T(8,128)(2,1)S(1)} copy-done((bf16[7,512,512]{2,1,0:T(8,128)(2,1)S(1)}, bf16[7,512,512]{2,1,0:T(8,128)(2,1)}, u32[]{:S(2)}) %copy-start.1) | copy-done | bytes 3670040
  10.2 0.0 copy-start.7
  10.2 0.9 copy-done.7
  11.2 0.0 copy-start.2
  11.2 10.1 %own.1 = (bf16[128,32,128]{2,1,0:T(8,128)(2,1)S(1)}, f32[32,256,128]{2,1,0:T(8,128)S(1)}) custom-call(f32[1]{0:T(128)} %bitcast.keep_ref, bf16[16,24,4096]{2,1,0:T(8,128)(2,1)S(1)} %copy-done.3, f32[16,4096]{1,0:T(8,128)S(1)} %copy-done.6, bf16[7,512,512]{2,1,0:T(8,128)(2,1)S(1)} %copy-done.1, bf16[2,256,256]{2,1,0:T(8,128)(2,1)S(1)} %copy-done.7), custom_call_target="tpu_custom_call" | custom-call | flops 15728640000 | bytes 20971520 | tf_op jit(solution)/shard_map/own/pallas_call | solution.py:226
  21.3 0.0 collective-permute-done.1.right_ref
  21.3 0.0 collective-permute-done.left_ref
  21.3 0.0 copy-done.2
  21.3 10.4 %rest.1 = bf16[128,32,384]{2,1,0:T(8,128)(2,1)} custom-call(bf16[16,8,4096]{2,1,0:T(8,128)(2,1)} %collective-permute-done.left_ref, bf16[16,8,4096]{2,1,0:T(8,128)(2,1)} %collective-permute-done.1.right_ref, f32[16,4096]{1,0:T(8,128)S(1)} %copy-done.6, bf16[7,512,512]{2,1,0:T(8,128)(2,1)S(1)} %copy-done.2, bf16[2,256,256]{2,1,0:T(8,128)(2,1)S(1)} %copy-done.7, ...), custom_call_target="tpu_custom_call" | custom-call | tf_op jit(solution)/shard_map/rest/pallas_call | solution.py:248
  31.7 9.9 %all-to-all-start = ((bf16[128,32,384]{2,1,0:T(8,128)(2,1)}), bf16[128,32,384]{2,1,0:T(8,128)(2,1)S(1)}, u32[]{:S(2)}, u32[]{:S(2)}) async-start(bf16[128,32,384]{2,1,0:T(8,128)(2,1)} %rest.1), calls=%async_computation | async-start | bytes 6291456 | tf_op jit(solution)/shard_map/all_to_all | solution.py:413
  41.5 0.0 copy-start.4
  41.5 1.2 %copy-done.4 = bf16[16,30720]{1,0:T(8,128)(2,1)S(1)} copy-done((bf16[16,30720]{1,0:T(8,128)(2,1)S(1)}, bf16[16,30720]{1,0:T(8,128)(2,1)}, u32[]{:S(2)}) %copy-start.4) | copy-done | bytes 983064
  42.7 0.0 copy-start.5
  42.7 1.2 %copy-done.5 = bf16[16,30720]{1,0:T(8,128)(2,1)S(1)} copy-done((bf16[16,30720]{1,0:T(8,128)(2,1)S(1)}, bf16[16,30720]{1,0:T(8,128)(2,1)}, u32[]{:S(2)}) %copy-start.5) | copy-done | bytes 983064
  43.9 0.0 copy-start.8
  43.9 0.0 copy-start.9
  43.9 5.5 %grid_weights.1.k_ref = bf16[120,256,256]{2,1,0:T(8,128)(2,1)S(1)} custom-call(bf16[16,30720]{1,0:T(8,128)(2,1)S(1)} %copy-done.4, bf16[16,30720]{1,0:T(8,128)(2,1)S(1)} %copy-done.5), custom_call_target="tpu_custom_call" | custom-call | flops 7864320 | bytes 15728640 | tf_op jit(solution)/shard_map/grid_weights/pallas_call | solution.py:286
  49.4 0.0 copy-start
  49.4 5.5 %copy-done = bf16[120,256,256]{2,1,0:T(8,128)(2,1)} copy-done((bf16[120,256,256]{2,1,0:T(8,128)(2,1)}, bf16[120,256,256]{2,1,0:T(8,128)(2,1)S(1)}, u32[]{:S(2)}) %copy-start) | copy-done | bytes 15728664
  54.9 0.0 copy-done.8
  54.9 0.0 copy-done.9
  54.9 0.1 select_reduce_fusion.slots_ref
  55.0 28.0 %all-to-all-done.r_ref = bf16[128,32,384]{2,1,0:T(8,128)(2,1)S(1)} async-done(((bf16[128,32,384]{2,1,0:T(8,128)(2,1)}), bf16[128,32,384]{2,1,0:T(8,128)(2,1)S(1)}, u32[]{:S(2)}, u32[]{:S(2)}) %all-to-all-start) | async-done | bytes 3145760 | tf_op jit(solution)/shard_map/all_to_all | solution.py:413
  82.9 13.6 %correlate.1 = bf16[16,32,256]{2,1,0:T(8,128)(2,1)S(1)} custom-call(s32[120]{0:T(128)S(1)} %select_reduce_fusion.slots_ref, bf16[128,32,384]{2,1,0:T(8,128)(2,1)S(1)} %all-to-all-done.r_ref, bf16[120,256,256]{2,1,0:T(8,128)(2,1)} %copy-done), custom_call_target="tpu_custom_call" | custom-call | tf_op jit(solution)/shard_map/correlate/pallas_call | solution.py:381
  96.5 0.1 reshape.16
  96.7 10.2 %all_to_all.14 = bf16[16,16,2,256]{3,2,1,0:T(2,128)(2,1)S(1)} all-to-all(bf16[16,16,2,256]{3,2,1,0:T(2,128)(2,1)S(1)} %reshape.16), channel_id=1, replica_groups=mesh['chan'=16,'tm'=8] {'tm'}, dimensions={0} | all-to-all | bytes 524288 | tf_op jit(solution)/shard_map/all_to_all | solution.py:422
  106.9 1.0 copy.10
Async XLA Ops:
  0.0 8.2 %copy-start.3 = (bf16[16,24,4096]{2,1,0:T(8,128)(2,1)S(1)}, bf16[16,24,4096]{2,1,0:T(8,128)(2,1)}, u32[]{:S(2)}) copy-start(bf16[16,24,4096]{2,1,0:T(8,128)(2,1)} %x_ref.1) | copy-start | bytes 9437188
  0.0 8.2 %copy-start.6 = (f32[16,4096]{1,0:T(8,128)S(1)}, f32[16,4096]{1,0:T(8,128)}, u32[]{:S(2)}) copy-start(f32[16,4096]{1,0:T(8,128)} %taps_ref.3) | copy-start | bytes 786436
  3.2 18.0 %collective-permute-start.1 = (bf16[16,8,4096]{2,1,0:T(8,128)(2,1)}, bf16[16,8,4096]{2,1,0:T(8,128)(2,1)}, u32[]{:S(2)}, u32[]{:S(2)}) collective-permute-start(bf16[16,8,4096]{2,1,0:T(8,128)(2,1)} %get-tuple-element.9), channel_id=1, source_target_pairs={{1,0},{2,1},{3,2},{4,3},{5,4},{6,5},{7,6},{0,7},{9,8},{10,9},{11,1... | collective-permute-start | bytes 3145736 | tf_op jit(solution)/shard_map/ppermute | solution.py:405
  4.6 16.6 %collective-permute-start = (bf16[16,8,4096]{2,1,0:T(8,128)(2,1)}, bf16[16,8,4096]{2,1,0:T(8,128)(2,1)}, u32[]{:S(2)}, u32[]{:S(2)}) collective-permute-start(bf16[16,8,4096]{2,1,0:T(8,128)(2,1)} %get-tuple-element.10), channel_id=1, source_target_pairs={{0,1},{1,2},{2,3},{3,4},{4,5},{5,6},{6,7},{8,9},{9,10},{10,11},{11... | collective-permute-start | bytes 3145736 | tf_op jit(solution)/shard_map/ppermute | solution.py:402
  8.2 2.0 %copy-start.1 = (bf16[7,512,512]{2,1,0:T(8,128)(2,1)S(1)}, bf16[7,512,512]{2,1,0:T(8,128)(2,1)}, u32[]{:S(2)}) copy-start(bf16[7,512,512]{2,1,0:T(8,128)(2,1)} %constant.12.clone.pairs_ref) | copy-start | bytes 11010052
  10.2 0.9 copy-start.7
  11.2 10.1 %copy-start.2 = (bf16[7,512,512]{2,1,0:T(8,128)(2,1)S(1)}, bf16[7,512,512]{2,1,0:T(8,128)(2,1)}, u32[]{:S(2)}) copy-start(bf16[7,512,512]{2,1,0:T(8,128)(2,1)} %constant.12.clone.pairs_ref) | copy-start | bytes 11010052
  31.7 51.3 %all-to-all-start = ((bf16[128,32,384]{2,1,0:T(8,128)(2,1)}), bf16[128,32,384]{2,1,0:T(8,128)(2,1)S(1)}, u32[]{:S(2)}, u32[]{:S(2)}) async-start(bf16[128,32,384]{2,1,0:T(8,128)(2,1)} %rest.1), calls=%async_computation | async-start | bytes 6291456 | tf_op jit(solution)/shard_map/all_to_all | solution.py:413
  41.5 1.2 %copy-start.4 = (bf16[16,30720]{1,0:T(8,128)(2,1)S(1)}, bf16[16,30720]{1,0:T(8,128)(2,1)}, u32[]{:S(2)}) copy-start(bf16[16,30720]{1,0:T(8,128)(2,1)} %u_ref.1) | copy-start | bytes 2949124
  42.7 1.2 %copy-start.5 = (bf16[16,30720]{1,0:T(8,128)(2,1)S(1)}, bf16[16,30720]{1,0:T(8,128)(2,1)}, u32[]{:S(2)}) copy-start(bf16[16,30720]{1,0:T(8,128)(2,1)} %v_ref.1) | copy-start | bytes 2949124
  43.9 11.0 %copy-start.8 = (s32[120]{0:T(128)S(1)}, s32[120]{0:T(128)}, u32[]{:S(2)}) copy-start(s32[120]{0:T(128)} %param.10) | copy-start | bytes 1444
  43.9 11.0 %copy-start.9 = (s32[16]{0:T(128)S(1)}, s32[16]{0:T(128)}, u32[]{:S(2)}) copy-start(s32[16]{0:T(128)} %param.11) | copy-start | bytes 196
  49.4 5.5 %copy-start = (bf16[120,256,256]{2,1,0:T(8,128)(2,1)}, bf16[120,256,256]{2,1,0:T(8,128)(2,1)S(1)}, u32[]{:S(2)}) copy-start(bf16[120,256,256]{2,1,0:T(8,128)(2,1)S(1)} %grid_weights.1.k_ref) | copy-start | bytes 47185924

commit v4 on v3

--- a/solution.py
+++ b/solution.py
@@ -116,10 +116,18 @@
                 keep(channel, part, z[part * dests : (part + 1) * dests])
         return 0
 
-    lax.fori_loop(1, RADIX // 2, pair, 0)
-
-
-def own_kernel(keep_ref, x_ref, taps_ref, pairs_ref, ends_ref, out_ref, part_ref, xs, filt, low, turned):
+    lax.fori_loop(1, RADIX // 2, pair, 0, unroll=RADIX // 2 - 1)
+
+
+def own_kernel(
+    keep_ref, x_ref, taps_ref, pairs_hbm, ends_hbm, out_ref, part_ref, xs, filt, low, turned, pairs_ref, ends_ref, sems
+):
+    fetches = [
+        pltpu.make_async_copy(pairs_hbm, pairs_ref, sems.at[0]),
+        pltpu.make_async_copy(ends_hbm, ends_ref, sems.at[1]),
+    ]
+    for fetch in fetches:
+        fetch.start()
     stations, frames, length = x_ref.shape
     taps = taps_ref.shape[0]
     span = length // RADIX
@@ -156,6 +164,8 @@
         lax.fori_loop(0, RADIX, fir, 0)
         butterflies(filt, low, half)
 
+    for fetch in fetches:
+        fetch.wait()
     products(low, turned, pairs_ref, ends_ref)
 
     def give(d, _):
@@ -229,15 +239,28 @@
             jax.ShapeDtypeStruct((dests, 2 * RADIX, HALO * stations), BF),
             jax.ShapeDtypeStruct((length // LANES, (frames - HALO) * stations, LANES), F32),
         ],
-        in_specs=[pl.BlockSpec(memory_space=pltpu.SMEM)] + [whole] * 4,
+        in_specs=[pl.BlockSpec(memory_space=pltpu.SMEM)]
+        + [whole] * 2
+        + [pl.BlockSpec(memory_space=pltpu.HBM)] * 2,
         out_specs=[whole] * 2,
-        scratch_shapes=channel_scratch(HALO, frames, length),
-        compiler_params=pltpu.CompilerParams(vmem_limit_bytes=32 << 20),
+        scratch_shapes=channel_scratch(HALO, frames, length)
+        + [
+            pltpu.VMEM(pairs.shape, BF),
+            pltpu.VMEM(ends.shape, BF),
+            pltpu.SemaphoreType.DMA((2,)),
+        ],
+        compiler_params=pltpu.CompilerParams(vmem_limit_bytes=22 << 20),
         cost_estimate=pl.CostEstimate(
             flops=10 * samples.size * 1000, bytes_accessed=20 << 20, transcendentals=0
         ),
         name="own",
-    )(keep, samples, taps, pairs, ends)
+    )(
+        keep,
+        samples,
+        taps,
+        pltpu.with_memory_space_constraint(pairs, pltpu.HBM),
+        pltpu.with_memory_space_constraint(ends, pltpu.HBM),
+    )
 
 
 def channelize_rest(before, after, taps, pairs, ends, done, part):
@@ -251,22 +274,19 @@
         in_specs=[whole] * 7,
         out_specs=whole,
         scratch_shapes=channel_scratch(frames, 2 * HALO, length),
-        compiler_params=pltpu.CompilerParams(vmem_limit_bytes=32 << 20),
+        compiler_params=pltpu.CompilerParams(vmem_limit_bytes=28 << 20),
         name="rest",
     )(before, after, taps, pairs, ends, done, part)
 
 
 def swap_groups(v):
-    lane = lax.broadcasted_iota(jnp.int32, v[0].shape, 1)
-    v = list(v)
+    group = lax.broadcasted_iota(jnp.int32, v[0].shape, 1) // SBLK
+    v = [pltpu.roll(a, i * SBLK, 1) if i else a for i, a in enumerate(v)]
+    v = [v[-i % 8] for i in range(8)]
     for bit in (1, 2, 4):
-        low = (lane // (bit * SBLK)) % 2 == 0
-        for i in range(8):
-            if not i & bit:
-                a, b = v[i], v[i + bit]
-                v[i] = jnp.where(low, a, pltpu.roll(b, bit * SBLK, 1))
-                v[i + bit] = jnp.where(low, pltpu.roll(a, LANES - bit * SBLK, 1), b)
-    return v
+        odd = (group & bit) != 0
+        v = [jnp.where(odd, v[(i - bit) % 8], v[i]) for i in range(8)]
+    return [pltpu.roll(a, LANES - j * SBLK, 1) if j else a for j, a in enumerate(v)]
 
 
 def weights_kernel(u_ref, v_ref, out_ref):
@@ -346,7 +366,7 @@
                 ]
         return 0
 
-    lax.fori_loop(0, group2 // 2, correlate, 0, unroll=2)
+    lax.fori_loop(0, group2 // 2, correlate, 0, unroll=8)
 
     acc[...] = jnp.zeros_like(acc)
     fetch.wait()
@@ -399,12 +419,9 @@
     frame_count = samples.shape[1]
     chan_size = lax.axis_size("chan")
     tm_size = lax.axis_size("tm")
-    before = lax.ppermute(
-        samples[:, frame_count - HALO :], "tm", [(i, i + 1) for i in range(tm_size - 1)]
-    )
-    after = lax.ppermute(
-        samples[:, :HALO], "tm", [((i + 1) % tm_size, i) for i in range(tm_size)]
-    )
+    last, first = samples[:, frame_count - HALO :], samples[:, :HALO]
+    before = lax.ppermute(last, "tm", [(i, i + 1) for i in range(tm_size - 1)])
+    after = lax.ppermute(first, "tm", [((i + 1) % tm_size, i) for i in range(tm_size)])
     keep = (lax.axis_index("tm") < tm_size - 1).astype(F32).reshape(1)
     weights = grid_weights(kern_u, kern_v)
     pairs, ends = (jnp.asarray(table) for table in dft_tables(samples.shape[2]))

time: 108 us -> 102 us (0.944)
  Pallas kernels: 39.5 us -> 31.8 us
  waiting for transfers between devices: 28 us -> 31.1 us
  local copies, waits for them, and re-layouts: 15.2 us -> 12.3 us
  starting transfers between devices: 14.8 us -> 15.9 us
    pallas_call x1, Pallas kernels: 13.6 us -> 8.8 us  [correlate(): pl.pallas_call(functools.partial(correlate_kernel, (owners, times, frames...]
    ppermute x2, waiting for transfers between devices: 0.01 us -> 3.15 us  [the longest x1 2 us: body(): lax.ppermute(first, 'tm', [((i + 1) % tm_size, i) for i in range(tm_size)])]
    unnamed x20 -> x18, local copies, waits for them, and re-layouts: 10.9 us -> 7.92 us
    pallas_call x1, Pallas kernels: 10.4 us -> 8.69 us  [channelize_rest(): pl.pallas_call(rest_kernel, out_shape=jax.ShapeDtypeStruct((dests, 2 * RA...]
    pallas_call x1, Pallas kernels: 10.1 us -> 8.83 us  [channelize_own(): pl.pallas_call(own_kernel, out_shape=[jax.ShapeDtypeStruct((dests, 2 * RA...]
    all_to_all x1, starting transfers between devices: 9.85 us -> 10.9 us  [body(): lax.all_to_all(spectra, ('chan', 'tm'), split_axis=0, concat_axis=0, tile...]
  transfers between devices with their start and end apart: 3 -> 3, of which waited for: 1 -> 3; matrix products, arithmetic and copies ran while one was open for 0% -> 0% of each run, Pallas kernels for 14% -> 14%
where the time goes in v4:
time: 102 us; the launch traced here: 101 us
  Pallas kernels  31.8 us (31%)
  waiting for transfers between devices  31.1 us (30%)
  starting transfers between devices  15.9 us (16%)
  local copies, waits for them, and re-layouts  12.3 us (12%)
  blocking collectives  10.2 us (10%)
    all_to_all x1, waiting for transfers between devices, body(): lax.all_to_all(spectra, ('chan', 'tm'), split_axis=0, concat_axis=0, tile...  28 us
    all_to_all x1, starting transfers between devices, body(): lax.all_to_all(spectra, ('chan', 'tm'), split_axis=0, concat_axis=0, tile...  10.9 us
    all_to_all x1, blocking collectives, body(): lax.all_to_all(partial_value, 'tm', split_axis=0, concat_axis=1, tiled=True)  10.2 us
    pallas_call x1, Pallas kernels, channelize_own(): pl.pallas_call(own_kernel, out_shape=[jax.ShapeDtypeStruct((dests, 2 * RA...  8.83 us
    pallas_call x1, Pallas kernels, correlate(): pl.pallas_call(functools.partial(correlate_kernel, (owners, times, frames...  8.8 us
    pallas_call x1, Pallas kernels, channelize_rest(): pl.pallas_call(rest_kernel, out_shape=jax.ShapeDtypeStruct((dests, 2 * RA...  8.69 us
    unnamed x18, local copies, waits for them, and re-layouts  7.92 us
    pallas_call x1, Pallas kernels, grid_weights(): pl.pallas_call(weights_kernel, grid=(count // step,), out_shape=jax.Shape...  5.46 us
  transfers between devices with their start and end apart: 3, of which 3 were waited for; matrix products, arithmetic and copies ran while one was open for 0% of the time, Pallas kernels for 14%

profile of v4, /device:TPU:1, one launch (start us, length us, event | category | flops | bytes accessed | tf_op | source)
XLA Modules:
  0.0 101.4 jit_solution(3796911335608903795)
XLA Ops:
  0.0 0.0 copy-start.2
  0.0 0.0 copy-start.5
  0.0 3.2 %fusion = (bf16[16,8,4096]{2,1,0:T(8,128)(2,1)}, bf16[16,8,4096]{2,1,0:T(8,128)(2,1)}) fusion(bf16[16,24,4096]{2,1,0:T(8,128)(2,1)} %x_ref.1), kind=kLoop, calls=%fused_computation.1 | loop fusion | bytes 4194304 | tf_op jit(solution)/shard_map/slice | solution.py:422
  3.2 1.4 %collective-permute-start.1 = (bf16[16,8,4096]{2,1,0:T(8,128)(2,1)}, bf16[16,8,4096]{2,1,0:T(8,128)(2,1)}, u32[]{:S(2)}, u32[]{:S(2)}) collective-permute-start(bf16[16,8,4096]{2,1,0:T(8,128)(2,1)} %get-tuple-element.9), channel_id=1, source_target_pairs={{1,0},{2,1},{3,2},{4,3},{5,4},{6,5},{7,6},{0,7},{9,8},{10,9},{11,1... | collective-permute-start | bytes 3145736 | tf_op jit(solution)/shard_map/ppermute | solution.py:424
  4.7 3.5 %collective-permute-start = (bf16[16,8,4096]{2,1,0:T(8,128)(2,1)}, bf16[16,8,4096]{2,1,0:T(8,128)(2,1)}, u32[]{:S(2)}, u32[]{:S(2)}) collective-permute-start(bf16[16,8,4096]{2,1,0:T(8,128)(2,1)} %get-tuple-element.10), channel_id=1, source_target_pairs={{0,1},{1,2},{2,3},{3,4},{4,5},{5,6},{6,7},{8,9},{9,10},{10,11},{11... | collective-permute-start | bytes 3145736 | tf_op jit(solution)/shard_map/ppermute | solution.py:423
  8.2 0.0 copy-done.2
  8.2 0.0 copy-done.5
  8.2 0.0 copy-start.1
  8.2 0.0 copy-start.6
  8.2 8.8 %own.1 = (bf16[128,32,128]{2,1,0:T(8,128)(2,1)S(1)}, f32[32,256,128]{2,1,0:T(8,128)S(1)}) custom-call(f32[1]{0:T(128)} %bitcast.keep_ref, bf16[16,24,4096]{2,1,0:T(8,128)(2,1)S(1)} %copy-done.2, f32[16,4096]{1,0:T(8,128)S(1)} %copy-done.5, bf16[7,512,512]{2,1,0:T(8,128)(2,1)} %constant.12.clone.pairs_hbm.pairs_ref, ...), custom_call_target="tpu_custom_call" | custom-call | flops 15728640000 | bytes 20971520 | tf_op jit(solution)/shard_map/own/pallas_call | solution.py:236
  17.0 2.0 %collective-permute-done.1.right_ref = bf16[16,8,4096]{2,1,0:T(8,128)(2,1)} collective-permute-done((bf16[16,8,4096]{2,1,0:T(8,128)(2,1)}, bf16[16,8,4096]{2,1,0:T(8,128)(2,1)}, u32[]{:S(2)}, u32[]{:S(2)}) %collective-permute-start.1) | collective-permute-done | bytes 1048608 | tf_op jit(solution)/shard_map/ppermute | solution.py:424
  19.1 1.1 %collective-permute-done.left_ref = bf16[16,8,4096]{2,1,0:T(8,128)(2,1)} collective-permute-done((bf16[16,8,4096]{2,1,0:T(8,128)(2,1)}, bf16[16,8,4096]{2,1,0:T(8,128)(2,1)}, u32[]{:S(2)}, u32[]{:S(2)}) %collective-permute-start) | collective-permute-done | bytes 1048608 | tf_op jit(solution)/shard_map/ppermute | solution.py:423
  20.2 0.0 copy-done.1
  20.2 0.0 copy-done.6
  20.2 8.7 %rest.1 = bf16[128,32,384]{2,1,0:T(8,128)(2,1)} custom-call(bf16[16,8,4096]{2,1,0:T(8,128)(2,1)} %collective-permute-done.left_ref, bf16[16,8,4096]{2,1,0:T(8,128)(2,1)} %collective-permute-done.1.right_ref, f32[16,4096]{1,0:T(8,128)S(1)} %copy-done.5, bf16[7,512,512]{2,1,0:T(8,128)(2,1)S(1)} %copy-done.1, bf16[2,256,256]{2,1,0:T(8,128)(2,1)S(1)} %copy-done.6, ...), custom_call_target="tpu_custom_call" | custom-call | tf_op jit(solution)/shard_map/rest/pallas_call | solution.py:271
  28.9 10.9 %all-to-all-start = ((bf16[128,32,384]{2,1,0:T(8,128)(2,1)}), bf16[128,32,384]{2,1,0:T(8,128)(2,1)S(1)}, u32[]{:S(2)}, u32[]{:S(2)}) async-start(bf16[128,32,384]{2,1,0:T(8,128)(2,1)} %rest.1), calls=%async_computation | async-start | bytes 6291456 | tf_op jit(solution)/shard_map/all_to_all | solution.py:430
  39.9 0.0 copy-start.3
  39.9 1.2 %copy-done.3 = bf16[16,30720]{1,0:T(8,128)(2,1)S(1)} copy-done((bf16[16,30720]{1,0:T(8,128)(2,1)S(1)}, bf16[16,30720]{1,0:T(8,128)(2,1)}, u32[]{:S(2)}) %copy-start.3) | copy-done | bytes 983064
  41.1 0.0 copy-start.4
  41.1 1.2 %copy-done.4 = bf16[16,30720]{1,0:T(8,128)(2,1)S(1)} copy-done((bf16[16,30720]{1,0:T(8,128)(2,1)S(1)}, bf16[16,30720]{1,0:T(8,128)(2,1)}, u32[]{:S(2)}) %copy-start.4) | copy-done | bytes 983064
  42.3 0.0 copy-start.7
  42.3 0.0 copy-start.8
  42.3 5.5 %grid_weights.1.k_ref = bf16[120,256,256]{2,1,0:T(8,128)(2,1)S(1)} custom-call(bf16[16,30720]{1,0:T(8,128)(2,1)S(1)} %copy-done.3, bf16[16,30720]{1,0:T(8,128)(2,1)S(1)} %copy-done.4), custom_call_target="tpu_custom_call" | custom-call | flops 7864320 | bytes 15728640 | tf_op jit(solution)/shard_map/grid_weights/pallas_call | solution.py:306
  47.7 0.0 copy-start
  47.7 5.5 %copy-done = bf16[120,256,256]{2,1,0:T(8,128)(2,1)} copy-done((bf16[120,256,256]{2,1,0:T(8,128)(2,1)}, bf16[120,256,256]{2,1,0:T(8,128)(2,1)S(1)}, u32[]{:S(2)}) %copy-start) | copy-done | bytes 15728664
  53.2 0.0 copy-done.7
  53.2 0.0 copy-done.8
  53.2 0.1 select_reduce_fusion.slots_ref
  53.3 28.0 %all-to-all-done.r_ref = bf16[128,32,384]{2,1,0:T(8,128)(2,1)S(1)} async-done(((bf16[128,32,384]{2,1,0:T(8,128)(2,1)}), bf16[128,32,384]{2,1,0:T(8,128)(2,1)S(1)}, u32[]{:S(2)}, u32[]{:S(2)}) %all-to-all-start) | async-done | bytes 3145760 | tf_op jit(solution)/shard_map/all_to_all | solution.py:430
  81.3 8.8 %correlate.1 = bf16[16,32,256]{2,1,0:T(8,128)(2,1)S(1)} custom-call(s32[120]{0:T(128)S(1)} %select_reduce_fusion.slots_ref, bf16[128,32,384]{2,1,0:T(8,128)(2,1)S(1)} %all-to-all-done.r_ref, bf16[120,256,256]{2,1,0:T(8,128)(2,1)} %copy-done), custom_call_target="tpu_custom_call" | custom-call | tf_op jit(solution)/shard_map/correlate/pallas_call | solution.py:401
  90.1 0.1 reshape.16
  90.2 10.2 %all_to_all.14 = bf16[16,16,2,256]{3,2,1,0:T(2,128)(2,1)S(1)} all-to-all(bf16[16,16,2,256]{3,2,1,0:T(2,128)(2,1)S(1)} %reshape.16), channel_id=1, replica_groups=mesh['chan'=16,'tm'=8] {'tm'}, dimensions={0} | all-to-all | bytes 524288 | tf_op jit(solution)/shard_map/all_to_all | solution.py:439
  100.4 1.0 copy.10
Async XLA Ops:
  0.0 8.2 %copy-start.2 = (bf16[16,24,4096]{2,1,0:T(8,128)(2,1)S(1)}, bf16[16,24,4096]{2,1,0:T(8,128)(2,1)}, u32[]{:S(2)}) copy-start(bf16[16,24,4096]{2,1,0:T(8,128)(2,1)} %x_ref.1) | copy-start | bytes 9437188
  0.0 8.2 %copy-start.5 = (f32[16,4096]{1,0:T(8,128)S(1)}, f32[16,4096]{1,0:T(8,128)}, u32[]{:S(2)}) copy-start(f32[16,4096]{1,0:T(8,128)} %taps_ref.3) | copy-start | bytes 786436
  3.2 15.8 %collective-permute-start.1 = (bf16[16,8,4096]{2,1,0:T(8,128)(2,1)}, bf16[16,8,4096]{2,1,0:T(8,128)(2,1)}, u32[]{:S(2)}, u32[]{:S(2)}) collective-permute-start(bf16[16,8,4096]{2,1,0:T(8,128)(2,1)} %get-tuple-element.9), channel_id=1, source_target_pairs={{1,0},{2,1},{3,2},{4,3},{5,4},{6,5},{7,6},{0,7},{9,8},{10,9},{11,1... | collective-permute-start | bytes 3145736 | tf_op jit(solution)/shard_map/ppermute | solution.py:424
  4.7 15.6 %collective-permute-start = (bf16[16,8,4096]{2,1,0:T(8,128)(2,1)}, bf16[16,8,4096]{2,1,0:T(8,128)(2,1)}, u32[]{:S(2)}, u32[]{:S(2)}) collective-permute-start(bf16[16,8,4096]{2,1,0:T(8,128)(2,1)} %get-tuple-element.10), channel_id=1, source_target_pairs={{0,1},{1,2},{2,3},{3,4},{4,5},{5,6},{6,7},{8,9},{9,10},{10,11},{11... | collective-permute-start | bytes 3145736 | tf_op jit(solution)/shard_map/ppermute | solution.py:423
  8.2 12.0 %copy-start.1 = (bf16[7,512,512]{2,1,0:T(8,128)(2,1)S(1)}, bf16[7,512,512]{2,1,0:T(8,128)(2,1)}, u32[]{:S(2)}) copy-start(bf16[7,512,512]{2,1,0:T(8,128)(2,1)} %constant.12.clone.pairs_hbm.pairs_ref) | copy-start | bytes 11010052
  8.2 12.0 %copy-start.6 = (bf16[2,256,256]{2,1,0:T(8,128)(2,1)S(1)}, bf16[2,256,256]{2,1,0:T(8,128)(2,1)}, u32[]{:S(2)}) copy-start(bf16[2,256,256]{2,1,0:T(8,128)(2,1)} %constant.13.clone.ends_hbm.ends_ref) | copy-start | bytes 786436
  28.9 52.4 %all-to-all-start = ((bf16[128,32,384]{2,1,0:T(8,128)(2,1)}), bf16[128,32,384]{2,1,0:T(8,128)(2,1)S(1)}, u32[]{:S(2)}, u32[]{:S(2)}) async-start(bf16[128,32,384]{2,1,0:T(8,128)(2,1)} %rest.1), calls=%async_computation | async-start | bytes 6291456 | tf_op jit(solution)/shard_map/all_to_all | solution.py:430
  39.9 1.2 %copy-start.3 = (bf16[16,30720]{1,0:T(8,128)(2,1)S(1)}, bf16[16,30720]{1,0:T(8,128)(2,1)}, u32[]{:S(2)}) copy-start(bf16[16,30720]{1,0:T(8,128)(2,1)} %u_ref.1) | copy-start | bytes 2949124
  41.1 1.2 %copy-start.4 = (bf16[16,30720]{1,0:T(8,128)(2,1)S(1)}, bf16[16,30720]{1,0:T(8,128)(2,1)}, u32[]{:S(2)}) copy-start(bf16[16,30720]{1,0:T(8,128)(2,1)} %v_ref.1) | copy-start | bytes 2949124
  42.3 11.0 %copy-start.7 = (s32[120]{0:T(128)S(1)}, s32[120]{0:T(128)}, u32[]{:S(2)}) copy-start(s32[120]{0:T(128)} %param.10) | copy-start | bytes 1444
  42.3 11.0 %copy-start.8 = (s32[16]{0:T(128)S(1)}, s32[16]{0:T(128)}, u32[]{:S(2)}) copy-start(s32[16]{0:T(128)} %param.11) | copy-start | bytes 196
  47.7 5.5 %copy-start = (bf16[120,256,256]{2,1,0:T(8,128)(2,1)}, bf16[120,256,256]{2,1,0:T(8,128)(2,1)S(1)}, u32[]{:S(2)}) copy-start(bf16[120,256,256]{2,1,0:T(8,128)(2,1)S(1)} %grid_weights.1.k_ref) | copy-start | bytes 47185924

commit v5 on v4

--- a/solution.py
+++ b/solution.py
@@ -16,6 +16,7 @@
 HALO = 8
 PITCH = 24
 PAD = 8
+PIECES = 4
 LANES = 128
 BF = jnp.bfloat16
 F32 = jnp.float32
@@ -120,8 +121,24 @@
 
 
 def own_kernel(
-    keep_ref, x_ref, taps_ref, pairs_hbm, ends_hbm, out_ref, part_ref, xs, filt, low, turned, pairs_ref, ends_ref, sems
+    keep_ref,
+    x_hbm,
+    taps_ref,
+    pairs_hbm,
+    ends_hbm,
+    out_ref,
+    part_ref,
+    xs,
+    filt,
+    low,
+    turned,
+    x_ref,
+    pairs_ref,
+    ends_ref,
+    sems,
 ):
+    samples = pltpu.make_async_copy(x_hbm, x_ref, sems.at[2])
+    samples.start()
     fetches = [
         pltpu.make_async_copy(pairs_hbm, pairs_ref, sems.at[0]),
         pltpu.make_async_copy(ends_hbm, ends_ref, sems.at[1]),
@@ -133,6 +150,7 @@
     span = length // RADIX
     own = keep_ref[0]
     done = range(HALO, 2 * HALO)
+    samples.wait()
 
     for half in range(span // LANES):
 
@@ -176,7 +194,12 @@
     lax.fori_loop(0, out_ref.shape[0], give, 0, unroll=8)
 
 
-def rest_kernel(left_ref, right_ref, taps_ref, pairs_ref, ends_ref, done_ref, part_ref, out_ref, xs, filt, low, turned):
+def rest_kernel(
+    left_ref, right_ref, taps_ref, pairs_ref, ends_ref, done_ref, part_ref, out_hbm, xs, filt, low, turned, stage, sems
+):
+    width = stage.shape[2]
+    finished = pltpu.make_async_copy(done_ref, out_hbm.at[:, :, width:], sems.at[PIECES])
+    finished.start()
     stations, _, length = left_ref.shape
     taps = taps_ref.shape[0]
     span = length // RADIX
@@ -207,16 +230,23 @@
         butterflies(filt, low, half)
 
     products(low, turned, pairs_ref, ends_ref)
-    tiles = low.shape[1] // LANES
-
-    def give(d, _):
-        at = pl.ds(pl.multiple_of(d * (2 * RADIX + PAD), 8), 2 * RADIX)
-        for tile in range(tiles):
-            out_ref[d, :, tile * LANES : (tile + 1) * LANES] = turned[tile, at, :].astype(BF)
-        out_ref[d, :, tiles * LANES :] = done_ref[d]
-        return 0
-
-    lax.fori_loop(0, out_ref.shape[0], give, 0, unroll=8)
+    count = stage.shape[0] // PIECES
+    copies = []
+    for piece in range(PIECES):
+
+        def give(d, _):
+            at = pl.ds(pl.multiple_of(d * (2 * RADIX + PAD), 8), 2 * RADIX)
+            for tile in range(width // LANES):
+                stage[d, :, tile * LANES : (tile + 1) * LANES] = turned[tile, at, :].astype(BF)
+            return 0
+
+        lax.fori_loop(piece * count, (piece + 1) * count, give, 0, unroll=8)
+        to = pl.ds(piece * count, count)
+        copy = pltpu.make_async_copy(stage.at[to], out_hbm.at[to, :, :width], sems.at[piece])
+        copy.start()
+        copies.append(copy)
+    for copy in copies + [finished]:
+        copy.wait()
 
 
 def channel_scratch(frames, steps, length):
@@ -240,14 +270,15 @@
             jax.ShapeDtypeStruct((length // LANES, (frames - HALO) * stations, LANES), F32),
         ],
         in_specs=[pl.BlockSpec(memory_space=pltpu.SMEM)]
-        + [whole] * 2
+        + [pl.BlockSpec(memory_space=pltpu.HBM), whole]
         + [pl.BlockSpec(memory_space=pltpu.HBM)] * 2,
         out_specs=[whole] * 2,
         scratch_shapes=channel_scratch(HALO, frames, length)
         + [
+            pltpu.VMEM(samples.shape, BF),
             pltpu.VMEM(pairs.shape, BF),
             pltpu.VMEM(ends.shape, BF),
-            pltpu.SemaphoreType.DMA((2,)),
+            pltpu.SemaphoreType.DMA((3,)),
         ],
         compiler_params=pltpu.CompilerParams(vmem_limit_bytes=22 << 20),
         cost_estimate=pl.CostEstimate(
@@ -256,7 +287,7 @@
         name="own",
     )(
         keep,
-        samples,
+        pltpu.with_memory_space_constraint(samples, pltpu.HBM),
         taps,
         pltpu.with_memory_space_constraint(pairs, pltpu.HBM),
         pltpu.with_memory_space_constraint(ends, pltpu.HBM),
@@ -272,8 +303,12 @@
         rest_kernel,
         out_shape=jax.ShapeDtypeStruct((dests, 2 * RADIX, part.shape[1] + done.shape[2]), BF),
         in_specs=[whole] * 7,
-        out_specs=whole,
-        scratch_shapes=channel_scratch(frames, 2 * HALO, length),
+        out_specs=pl.BlockSpec(memory_space=pltpu.HBM),
+        scratch_shapes=channel_scratch(frames, 2 * HALO, length)
+        + [
+            pltpu.VMEM((dests, 2 * RADIX, part.shape[1]), BF),
+            pltpu.SemaphoreType.DMA((PIECES + 1,)),
+        ],
         compiler_params=pltpu.CompilerParams(vmem_limit_bytes=28 << 20),
         name="rest",
     )(before, after, taps, pairs, ends, done, part)

time: 102 us -> 98.9 us (0.970)
  waiting for transfers between devices: 31.1 us -> 28.7 us
    pallas_call x1, Pallas kernels: 8.69 us -> 6.57 us  [channelize_rest(): pl.pallas_call(rest_kernel, out_shape=jax.ShapeDtypeStruct((dests, 2 * RA...]
    pallas_call x1, Pallas kernels: 8.83 us -> 10.9 us  [channelize_own(): pl.pallas_call(own_kernel, out_shape=[jax.ShapeDtypeStruct((dests, 2 * RA...]
    ppermute x1, waiting for transfers between devices: 2 us -> 0.01 us  [body(): lax.ppermute(first, 'tm', [((i + 1) % tm_size, i) for i in range(tm_size)])]
    unnamed x18 -> x16, local copies, waits for them, and re-layouts: 7.92 us -> 7.92 us
  transfers between devices with their start and end apart: 3 -> 3, of which waited for: 3 -> 2; matrix products, arithmetic and copies ran while one was open for 0% -> 0% of each run, Pallas kernels for 14% -> 17%
where the time goes in v5:
time: 98.9 us; the launch traced here: 98.5 us
  Pallas kernels  31.7 us (32%)
  waiting for transfers between devices  28.7 us (29%)
  starting transfers between devices  15.9 us (16%)
  local copies, waits for them, and re-layouts  11.8 us (12%)
  blocking collectives  10.2 us (10%)
    all_to_all x1, waiting for transfers between devices, body(): lax.all_to_all(spectra, ('chan', 'tm'), split_axis=0, concat_axis=0, tile...  27.9 us
    all_to_all x1, starting transfers between devices, body(): lax.all_to_all(spectra, ('chan', 'tm'), split_axis=0, concat_axis=0, tile...  11 us
    pallas_call x1, Pallas kernels, channelize_own(): pl.pallas_call(own_kernel, out_shape=[jax.ShapeDtypeStruct((dests, 2 * RA...  10.9 us
    all_to_all x1, blocking collectives, body(): lax.all_to_all(partial_value, 'tm', split_axis=0, concat_axis=1, tiled=True)  10.2 us
    pallas_call x1, Pallas kernels, correlate(): pl.pallas_call(functools.partial(correlate_kernel, (owners, times, frames...  8.8 us
    unnamed x16, local copies, waits for them, and re-layouts  7.92 us
    pallas_call x1, Pallas kernels, channelize_rest(): pl.pallas_call(rest_kernel, out_shape=jax.ShapeDtypeStruct((dests, 2 * RA...  6.57 us
    pallas_call x1, Pallas kernels, grid_weights(): pl.pallas_call(weights_kernel, grid=(count // step,), out_shape=jax.Shape...  5.46 us
  transfers between devices with their start and end apart: 3, of which 2 were waited for; matrix products, arithmetic and copies ran while one was open for 0% of the time, Pallas kernels for 17%

profile of v5, /device:TPU:1, one launch (start us, length us, event | category | flops | bytes accessed | tf_op | source)
XLA Modules:
  0.0 98.5 jit_solution(7733510319121528546)
XLA Ops:
  0.0 0.0 copy-start.4
  0.0 2.7 %fusion = (bf16[16,8,4096]{2,1,0:T(8,128)(2,1)}, bf16[16,8,4096]{2,1,0:T(8,128)(2,1)S(1)}) fusion(bf16[16,24,4096]{2,1,0:T(8,128)(2,1)} %x_hbm.1), kind=kLoop, calls=%fused_computation.1 | loop fusion | bytes 4194304 | tf_op jit(solution)/shard_map/slice | solution.py:457
  2.7 1.4 %collective-permute-start.1 = (bf16[16,8,4096]{2,1,0:T(8,128)(2,1)}, bf16[16,8,4096]{2,1,0:T(8,128)(2,1)S(1)}, u32[]{:S(2)}, u32[]{:S(2)}) collective-permute-start(bf16[16,8,4096]{2,1,0:T(8,128)(2,1)} %get-tuple-element.9), channel_id=1, source_target_pairs={{1,0},{2,1},{3,2},{4,3},{5,4},{6,5},{7,6},{0,7},{9,8},{10,9},{11,1... | collective-permute-start | bytes 3145736 | tf_op jit(solution)/shard_map/ppermute | solution.py:459
  4.2 3.5 %collective-permute-start = (bf16[16,8,4096]{2,1,0:T(8,128)(2,1)S(1)}, bf16[16,8,4096]{2,1,0:T(8,128)(2,1)S(1)}, u32[]{:S(2)}, u32[]{:S(2)}) collective-permute-start(bf16[16,8,4096]{2,1,0:T(8,128)(2,1)S(1)} %get-tuple-element.10), channel_id=1, source_target_pairs={{0,1},{1,2},{2,3},{3,4},{4,5},{5,6},{6,7},{8,9},{9,10},{10,11},{11... | collective-permute-start | bytes 3145736 | tf_op jit(solution)/shard_map/ppermute | solution.py:458
  7.7 0.0 copy-done.4
  7.7 0.0 copy-start.1
  7.7 0.0 copy-start.5
  7.7 10.9 %own.1 = (bf16[128,32,128]{2,1,0:T(8,128)(2,1)S(1)}, f32[32,256,128]{2,1,0:T(8,128)S(1)}) custom-call(f32[1]{0:T(128)} %bitcast.keep_ref, bf16[16,24,4096]{2,1,0:T(8,128)(2,1)} %x_hbm.1, f32[16,4096]{1,0:T(8,128)S(1)} %copy-done.4, bf16[7,512,512]{2,1,0:T(8,128)(2,1)} %constant.12.clone.pairs_hbm.pairs_ref, bf16[2,256,256]{2,1,0:T(8,128)(2,1)} %constant.13.clone.ends_hbm.ends_ref), custom_call_target="tpu_custom_call" | custom-call | flops 15728640000 | bytes 20971520 | tf_op jit(solution)/shard_map/own/pallas_call | solution.py:266
  18.6 0.0 collective-permute-done.1.right_ref
  18.6 0.8 collective-permute-done.left_ref
  19.4 0.0 copy-done.1
  19.4 0.0 copy-done.5
  19.4 6.6 %rest.1 = bf16[128,32,384]{2,1,0:T(8,128)(2,1)} custom-call(bf16[16,8,4096]{2,1,0:T(8,128)(2,1)S(1)} %collective-permute-done.left_ref, bf16[16,8,4096]{2,1,0:T(8,128)(2,1)S(1)} %collective-permute-done.1.right_ref, f32[16,4096]{1,0:T(8,128)S(1)} %copy-done.4, bf16[7,512,512]{2,1,0:T(8,128)(2,1)S(1)} %copy-done.1, bf16[2,256,256]{2,1,0:T(8,128)(2,1)S(1)} %copy-done.5, ...), custom_call_target="tpu_custom_call" | custom-call | tf_op jit(solution)/shard_map/rest/pallas_call | solution.py:302
  26.0 11.0 %all-to-all-start = ((bf16[128,32,384]{2,1,0:T(8,128)(2,1)}), bf16[128,32,384]{2,1,0:T(8,128)(2,1)S(1)}, u32[]{:S(2)}, u32[]{:S(2)}) async-start(bf16[128,32,384]{2,1,0:T(8,128)(2,1)} %rest.1), calls=%async_computation | async-start | bytes 6291456 | tf_op jit(solution)/shard_map/all_to_all | solution.py:465
  36.9 0.0 copy-start.2
  37.0 1.2 %copy-done.2 = bf16[16,30720]{1,0:T(8,128)(2,1)S(1)} copy-done((bf16[16,30720]{1,0:T(8,128)(2,1)S(1)}, bf16[16,30720]{1,0:T(8,128)(2,1)}, u32[]{:S(2)}) %copy-start.2) | copy-done | bytes 983064
  38.1 0.0 copy-start.3
  38.1 1.2 %copy-done.3 = bf16[16,30720]{1,0:T(8,128)(2,1)S(1)} copy-done((bf16[16,30720]{1,0:T(8,128)(2,1)S(1)}, bf16[16,30720]{1,0:T(8,128)(2,1)}, u32[]{:S(2)}) %copy-start.3) | copy-done | bytes 983064
  39.4 0.0 copy-start.6
  39.4 0.0 copy-start.7
  39.4 5.5 %grid_weights.1.k_ref = bf16[120,256,256]{2,1,0:T(8,128)(2,1)S(1)} custom-call(bf16[16,30720]{1,0:T(8,128)(2,1)S(1)} %copy-done.2, bf16[16,30720]{1,0:T(8,128)(2,1)S(1)} %copy-done.3), custom_call_target="tpu_custom_call" | custom-call | flops 7864320 | bytes 15728640 | tf_op jit(solution)/shard_map/grid_weights/pallas_call | solution.py:341
  44.8 0.0 copy-start
  44.8 5.5 %copy-done = bf16[120,256,256]{2,1,0:T(8,128)(2,1)} copy-done((bf16[120,256,256]{2,1,0:T(8,128)(2,1)}, bf16[120,256,256]{2,1,0:T(8,128)(2,1)S(1)}, u32[]{:S(2)}) %copy-start) | copy-done | bytes 15728664
  50.3 0.0 copy-done.6
  50.3 0.0 copy-done.7
  50.3 0.1 select_reduce_fusion.slots_ref
  50.4 27.9 %all-to-all-done.r_ref = bf16[128,32,384]{2,1,0:T(8,128)(2,1)S(1)} async-done(((bf16[128,32,384]{2,1,0:T(8,128)(2,1)}), bf16[128,32,384]{2,1,0:T(8,128)(2,1)S(1)}, u32[]{:S(2)}, u32[]{:S(2)}) %all-to-all-start) | async-done | bytes 3145760 | tf_op jit(solution)/shard_map/all_to_all | solution.py:465
  78.4 8.8 %correlate.1 = bf16[16,32,256]{2,1,0:T(8,128)(2,1)S(1)} custom-call(s32[120]{0:T(128)S(1)} %select_reduce_fusion.slots_ref, bf16[128,32,384]{2,1,0:T(8,128)(2,1)S(1)} %all-to-all-done.r_ref, bf16[120,256,256]{2,1,0:T(8,128)(2,1)} %copy-done), custom_call_target="tpu_custom_call" | custom-call | tf_op jit(solution)/shard_map/correlate/pallas_call | solution.py:436
  87.2 0.1 reshape.16
  87.3 10.2 %all_to_all.14 = bf16[16,16,2,256]{3,2,1,0:T(2,128)(2,1)S(1)} all-to-all(bf16[16,16,2,256]{3,2,1,0:T(2,128)(2,1)S(1)} %reshape.16), channel_id=1, replica_groups=mesh['chan'=16,'tm'=8] {'tm'}, dimensions={0} | all-to-all | bytes 524288 | tf_op jit(solution)/shard_map/all_to_all | solution.py:474
  97.5 1.0 %copy.10 = f32[8,2,16,2,256]{4,3,2,0,1:T(2,128)} copy(bf16[8,2,16,2,256]{4,3,2,1,0:T(2,128)(2,1)S(1)} %bitcast.6) | data formatting | bytes 786432 | tf_op jit(solution)/shard_map/convert_element_type | solution.py:474
Async XLA Ops:
  0.0 7.7 %copy-start.4 = (f32[16,4096]{1,0:T(8,128)S(1)}, f32[16,4096]{1,0:T(8,128)}, u32[]{:S(2)}) copy-start(f32[16,4096]{1,0:T(8,128)} %taps_ref.3) | copy-start | bytes 786436
  2.7 15.9 %collective-permute-start.1 = (bf16[16,8,4096]{2,1,0:T(8,128)(2,1)}, bf16[16,8,4096]{2,1,0:T(8,128)(2,1)S(1)}, u32[]{:S(2)}, u32[]{:S(2)}) collective-permute-start(bf16[16,8,4096]{2,1,0:T(8,128)(2,1)} %get-tuple-element.9), channel_id=1, source_target_pairs={{1,0},{2,1},{3,2},{4,3},{5,4},{6,5},{7,6},{0,7},{9,8},{10,9},{11,1... | collective-permute-start | bytes 3145736 | tf_op jit(solution)/shard_map/ppermute | solution.py:459
  4.2 15.2 %collective-permute-start = (bf16[16,8,4096]{2,1,0:T(8,128)(2,1)S(1)}, bf16[16,8,4096]{2,1,0:T(8,128)(2,1)S(1)}, u32[]{:S(2)}, u32[]{:S(2)}) collective-permute-start(bf16[16,8,4096]{2,1,0:T(8,128)(2,1)S(1)} %get-tuple-element.10), channel_id=1, source_target_pairs={{0,1},{1,2},{2,3},{3,4},{4,5},{5,6},{6,7},{8,9},{9,10},{10,11},{11... | collective-permute-start | bytes 3145736 | tf_op jit(solution)/shard_map/ppermute | solution.py:458
  7.7 11.7 %copy-start.1 = (bf16[7,512,512]{2,1,0:T(8,128)(2,1)S(1)}, bf16[7,512,512]{2,1,0:T(8,128)(2,1)}, u32[]{:S(2)}) copy-start(bf16[7,512,512]{2,1,0:T(8,128)(2,1)} %constant.12.clone.pairs_hbm.pairs_ref) | copy-start | bytes 11010052
  7.7 11.7 %copy-start.5 = (bf16[2,256,256]{2,1,0:T(8,128)(2,1)S(1)}, bf16[2,256,256]{2,1,0:T(8,128)(2,1)}, u32[]{:S(2)}) copy-start(bf16[2,256,256]{2,1,0:T(8,128)(2,1)} %constant.13.clone.ends_hbm.ends_ref) | copy-start | bytes 786436
  26.0 52.4 %all-to-all-start = ((bf16[128,32,384]{2,1,0:T(8,128)(2,1)}), bf16[128,32,384]{2,1,0:T(8,128)(2,1)S(1)}, u32[]{:S(2)}, u32[]{:S(2)}) async-start(bf16[128,32,384]{2,1,0:T(8,128)(2,1)} %rest.1), calls=%async_computation | async-start | bytes 6291456 | tf_op jit(solution)/shard_map/all_to_all | solution.py:465
  36.9 1.2 %copy-start.2 = (bf16[16,30720]{1,0:T(8,128)(2,1)S(1)}, bf16[16,30720]{1,0:T(8,128)(2,1)}, u32[]{:S(2)}) copy-start(bf16[16,30720]{1,0:T(8,128)(2,1)} %u_ref.1) | copy-start | bytes 2949124
  38.1 1.2 %copy-start.3 = (bf16[16,30720]{1,0:T(8,128)(2,1)S(1)}, bf16[16,30720]{1,0:T(8,128)(2,1)}, u32[]{:S(2)}) copy-start(bf16[16,30720]{1,0:T(8,128)(2,1)} %v_ref.1) | copy-start | bytes 2949124
  39.4 11.0 %copy-start.6 = (s32[120]{0:T(128)S(1)}, s32[120]{0:T(128)}, u32[]{:S(2)}) copy-start(s32[120]{0:T(128)} %param.10) | copy-start | bytes 1444
  39.4 11.0 %copy-start.7 = (s32[16]{0:T(128)S(1)}, s32[16]{0:T(128)}, u32[]{:S(2)}) copy-start(s32[16]{0:T(128)} %param.11) | copy-start | bytes 196
  44.8 5.5 %copy-start = (bf16[120,256,256]{2,1,0:T(8,128)(2,1)}, bf16[120,256,256]{2,1,0:T(8,128)(2,1)S(1)}, u32[]{:S(2)}) copy-start(bf16[120,256,256]{2,1,0:T(8,128)(2,1)S(1)} %grid_weights.1.k_ref) | copy-start | bytes 47185924

commit v6 on v5

--- a/solution.py
+++ b/solution.py
@@ -71,19 +71,19 @@
         target[pl.ds(first * PITCH + s, source.shape[1], stride=PITCH), :] = source[s, :, at].astype(F32)
 
 
-def butterflies(filt, low, half):
-    to = slice(half * LANES, (half + 1) * LANES)
-
+def butterflies(filt, low):
     def butterfly(b, _):
         at = pl.ds(pl.multiple_of(b * SBLK, SBLK), SBLK)
-        parts = real_dft([filt[tile, at, :].astype(F32) for tile in range(RADIX)])
-        for k, (re, im) in enumerate(parts):
-            low[k, at, to] = re.astype(BF)
-            if im is not None:
-                low[RADIX // 2 + k, at, to] = im.astype(BF)
-        return 0
-
-    lax.fori_loop(0, filt.shape[1] // SBLK, butterfly, 0, unroll=2)
+        for half in range(filt.shape[2] // LANES):
+            to = slice(half * LANES, (half + 1) * LANES)
+            parts = real_dft([filt[tile, at, to].astype(F32) for tile in range(RADIX)])
+            for k, (re, im) in enumerate(parts):
+                low[k, at, to] = re.astype(BF)
+                if im is not None:
+                    low[RADIX // 2 + k, at, to] = im.astype(BF)
+        return 0
+
+    lax.fori_loop(0, filt.shape[1] // SBLK, butterfly, 0)
 
 
 def products(low, turned, pairs_ref, ends_ref):
@@ -137,8 +137,12 @@
     ends_ref,
     sems,
 ):
-    samples = pltpu.make_async_copy(x_hbm, x_ref, sems.at[2])
-    samples.start()
+    piece = x_hbm.shape[2] // PIECES
+    samples = []
+    for i in range(PIECES):
+        part = (slice(None), slice(None), pl.ds(i * piece, piece))
+        samples.append(pltpu.make_async_copy(x_hbm.at[part], x_ref.at[part], sems.at[2 + i]))
+        samples[i].start()
     fetches = [
         pltpu.make_async_copy(pairs_hbm, pairs_ref, sems.at[0]),
         pltpu.make_async_copy(ends_hbm, ends_ref, sems.at[1]),
@@ -150,11 +154,9 @@
     span = length // RADIX
     own = keep_ref[0]
     done = range(HALO, 2 * HALO)
-    samples.wait()
-
-    for half in range(span // LANES):
-
-        def fir(tile, _):
+
+    def fir(tile, _):
+        for half in range(span // LANES):
             at = pl.ds(pl.multiple_of(tile * span + half * LANES, LANES), LANES)
             spread(x_ref, xs, 0, at)
             weights = [taps_ref[pl.ds(k, 1), at] for k in range(taps)]
@@ -171,17 +173,19 @@
                     value = sums.pop(b)
                     if b in done:
                         place = b - done.start
-                        filt[tile, place * stations : (place + 1) * stations, :] = value.astype(BF)
+                        to = slice(half * LANES, (half + 1) * LANES)
+                        filt[tile, place * stations : (place + 1) * stations, to] = value.astype(BF)
                     else:
                         place = b if b < done.start else b - len(done)
                         if b + taps - 1 >= HALO + frames:
                             value = own * value
                         part_ref[2 * tile + half, place * stations : (place + 1) * stations, :] = value
-            return 0
-
-        lax.fori_loop(0, RADIX, fir, 0)
-        butterflies(filt, low, half)
-
+        return 0
+
+    for i in range(PIECES):
+        samples[i].wait()
+        lax.fori_loop(i * RADIX // PIECES, (i + 1) * RADIX // PIECES, fir, 0)
+    butterflies(filt, low)
     for fetch in fetches:
         fetch.wait()
     products(low, turned, pairs_ref, ends_ref)
@@ -205,10 +209,10 @@
     span = length // RADIX
     count = part_ref.shape[1] // stations
 
-    for half in range(span // LANES):
-
-        def fir(tile, _):
+    def fir(tile, _):
+        for half in range(span // LANES):
             at = pl.ds(pl.multiple_of(tile * span + half * LANES, LANES), LANES)
+            lanes = slice(half * LANES, (half + 1) * LANES)
             spread(left_ref, xs, 0, at)
             spread(right_ref, xs, HALO, at)
             weights = [taps_ref[pl.ds(k, 1), at] for k in range(taps)]
@@ -223,12 +227,11 @@
                     terms = [(HALO + j, first - j) for j in range(first + 1)]
                 for j, k in terms:
                     value = value + weights[k] * x[j]
-                filt[tile, to, :] = value.astype(BF)
-            return 0
-
-        lax.fori_loop(0, RADIX, fir, 0)
-        butterflies(filt, low, half)
-
+                filt[tile, to, lanes] = value.astype(BF)
+        return 0
+
+    lax.fori_loop(0, RADIX, fir, 0)
+    butterflies(filt, low)
     products(low, turned, pairs_ref, ends_ref)
     count = stage.shape[0] // PIECES
     copies = []
@@ -253,7 +256,7 @@
     rows = frames * SBLK
     return [
         pltpu.VMEM((steps * PITCH, LANES), F32),
-        pltpu.VMEM((RADIX, rows, LANES), BF),
+        pltpu.VMEM((RADIX, rows, length // RADIX), BF),
         pltpu.VMEM((RADIX, rows, length // RADIX), BF),
         pltpu.VMEM((rows // LANES, length // (2 * RADIX) * (2 * RADIX + PAD), LANES), F32),
     ]
@@ -278,7 +281,7 @@
             pltpu.VMEM(samples.shape, BF),
             pltpu.VMEM(pairs.shape, BF),
             pltpu.VMEM(ends.shape, BF),
-            pltpu.SemaphoreType.DMA((3,)),
+            pltpu.SemaphoreType.DMA((2 + PIECES,)),
         ],
         compiler_params=pltpu.CompilerParams(vmem_limit_bytes=22 << 20),
         cost_estimate=pl.CostEstimate(

time: 98.9 us -> 98.7 us (level)
  Pallas kernels: 31.7 us -> 30.7 us
  transfers between devices with their start and end apart: 3 -> 3, of which waited for: 2 -> 3; matrix products, arithmetic and copies ran while one was open for 0% -> 0% of each run, Pallas kernels for 17% -> 16%
where the time goes in v6:
time: 98.7 us; the launch traced here: 98.3 us
  Pallas kernels  30.7 us (31%)
  waiting for transfers between devices  29.5 us (30%)
  starting transfers between devices  15.9 us (16%)
  local copies, waits for them, and re-layouts  11.8 us (12%)
  blocking collectives  10.2 us (10%)
    all_to_all x1, waiting for transfers between devices, body(): lax.all_to_all(spectra, ('chan', 'tm'), split_axis=0, concat_axis=0, tile...  27.9 us
    all_to_all x1, starting transfers between devices, body(): lax.all_to_all(spectra, ('chan', 'tm'), split_axis=0, concat_axis=0, tile...  11 us
    all_to_all x1, blocking collectives, body(): lax.all_to_all(partial_value, 'tm', split_axis=0, concat_axis=1, tiled=True)  10.2 us
    pallas_call x1, Pallas kernels, channelize_own(): pl.pallas_call(own_kernel, out_shape=[jax.ShapeDtypeStruct((dests, 2 * RA...  10.1 us
    pallas_call x1, Pallas kernels, correlate(): pl.pallas_call(functools.partial(correlate_kernel, (owners, times, frames...  8.8 us
    unnamed x16, local copies, waits for them, and re-layouts  7.92 us
    pallas_call x1, Pallas kernels, channelize_rest(): pl.pallas_call(rest_kernel, out_shape=jax.ShapeDtypeStruct((dests, 2 * RA...  6.39 us
    pallas_call x1, Pallas kernels, grid_weights(): pl.pallas_call(weights_kernel, grid=(count // step,), out_shape=jax.Shape...  5.46 us
  transfers between devices with their start and end apart: 3, of which 3 were waited for; matrix products, arithmetic and copies ran while one was open for 0% of the time, Pallas kernels for 16%

profile of v6, /device:TPU:1, one launch (start us, length us, event | category | flops | bytes accessed | tf_op | source)
XLA Modules:
  0.0 98.3 jit_solution(7590110973207756613)
XLA Ops:
  0.0 0.0 copy-start.4
  0.0 2.7 %fusion = (bf16[16,8,4096]{2,1,0:T(8,128)(2,1)}, bf16[16,8,4096]{2,1,0:T(8,128)(2,1)S(1)}) fusion(bf16[16,24,4096]{2,1,0:T(8,128)(2,1)} %x_hbm.1), kind=kLoop, calls=%fused_computation.1 | loop fusion | bytes 4194304 | tf_op jit(solution)/shard_map/slice | solution.py:460
  2.7 1.4 %collective-permute-start.1 = (bf16[16,8,4096]{2,1,0:T(8,128)(2,1)}, bf16[16,8,4096]{2,1,0:T(8,128)(2,1)S(1)}, u32[]{:S(2)}, u32[]{:S(2)}) collective-permute-start(bf16[16,8,4096]{2,1,0:T(8,128)(2,1)} %get-tuple-element.9), channel_id=1, source_target_pairs={{1,0},{2,1},{3,2},{4,3},{5,4},{6,5},{7,6},{0,7},{9,8},{10,9},{11,1... | collective-permute-start | bytes 3145736 | tf_op jit(solution)/shard_map/ppermute | solution.py:462
  4.2 3.5 %collective-permute-start = (bf16[16,8,4096]{2,1,0:T(8,128)(2,1)S(1)}, bf16[16,8,4096]{2,1,0:T(8,128)(2,1)S(1)}, u32[]{:S(2)}, u32[]{:S(2)}) collective-permute-start(bf16[16,8,4096]{2,1,0:T(8,128)(2,1)S(1)} %get-tuple-element.10), channel_id=1, source_target_pairs={{0,1},{1,2},{2,3},{3,4},{4,5},{5,6},{6,7},{8,9},{9,10},{10,11},{11... | collective-permute-start | bytes 3145736 | tf_op jit(solution)/shard_map/ppermute | solution.py:461
  7.7 0.0 copy-done.4
  7.7 0.0 copy-start.1
  7.7 0.0 copy-start.5
  7.7 10.1 %own.1 = (bf16[128,32,128]{2,1,0:T(8,128)(2,1)S(1)}, f32[32,256,128]{2,1,0:T(8,128)S(1)}) custom-call(f32[1]{0:T(128)} %bitcast.keep_ref, bf16[16,24,4096]{2,1,0:T(8,128)(2,1)} %x_hbm.1, f32[16,4096]{1,0:T(8,128)S(1)} %copy-done.4, bf16[7,512,512]{2,1,0:T(8,128)(2,1)} %constant.12.clone.pairs_hbm.pairs_ref, bf16[2,256,256]{2,1,0:T(8,128)(2,1)} %constant.13.clone.ends_hbm.ends_ref), custom_call_target="tpu_custom_call" | custom-call | flops 15728640000 | bytes 20971520 | tf_op jit(solution)/shard_map/own/pallas_call | solution.py:269
  17.8 0.7 collective-permute-done.1.right_ref
  18.5 0.9 collective-permute-done.left_ref
  19.4 0.0 copy-done.1
  19.4 0.0 copy-done.5
  19.4 6.4 %rest.1 = bf16[128,32,384]{2,1,0:T(8,128)(2,1)} custom-call(bf16[16,8,4096]{2,1,0:T(8,128)(2,1)S(1)} %collective-permute-done.left_ref, bf16[16,8,4096]{2,1,0:T(8,128)(2,1)S(1)} %collective-permute-done.1.right_ref, f32[16,4096]{1,0:T(8,128)S(1)} %copy-done.4, bf16[7,512,512]{2,1,0:T(8,128)(2,1)S(1)} %copy-done.1, bf16[2,256,256]{2,1,0:T(8,128)(2,1)S(1)} %copy-done.5, ...), custom_call_target="tpu_custom_call" | custom-call | tf_op jit(solution)/shard_map/rest/pallas_call | solution.py:305
  25.8 11.0 %all-to-all-start = ((bf16[128,32,384]{2,1,0:T(8,128)(2,1)}), bf16[128,32,384]{2,1,0:T(8,128)(2,1)S(1)}, u32[]{:S(2)}, u32[]{:S(2)}) async-start(bf16[128,32,384]{2,1,0:T(8,128)(2,1)} %rest.1), calls=%async_computation | async-start | bytes 6291456 | tf_op jit(solution)/shard_map/all_to_all | solution.py:468
  36.8 0.0 copy-start.2
  36.8 1.2 %copy-done.2 = bf16[16,30720]{1,0:T(8,128)(2,1)S(1)} copy-done((bf16[16,30720]{1,0:T(8,128)(2,1)S(1)}, bf16[16,30720]{1,0:T(8,128)(2,1)}, u32[]{:S(2)}) %copy-start.2) | copy-done | bytes 983064
  38.0 0.0 copy-start.3
  38.0 1.2 %copy-done.3 = bf16[16,30720]{1,0:T(8,128)(2,1)S(1)} copy-done((bf16[16,30720]{1,0:T(8,128)(2,1)S(1)}, bf16[16,30720]{1,0:T(8,128)(2,1)}, u32[]{:S(2)}) %copy-start.3) | copy-done | bytes 983064
  39.2 0.0 copy-start.6
  39.2 0.0 copy-start.7
  39.2 5.5 %grid_weights.1.k_ref = bf16[120,256,256]{2,1,0:T(8,128)(2,1)S(1)} custom-call(bf16[16,30720]{1,0:T(8,128)(2,1)S(1)} %copy-done.2, bf16[16,30720]{1,0:T(8,128)(2,1)S(1)} %copy-done.3), custom_call_target="tpu_custom_call" | custom-call | flops 7864320 | bytes 15728640 | tf_op jit(solution)/shard_map/grid_weights/pallas_call | solution.py:344
  44.6 0.0 copy-start
  44.6 5.5 %copy-done = bf16[120,256,256]{2,1,0:T(8,128)(2,1)} copy-done((bf16[120,256,256]{2,1,0:T(8,128)(2,1)}, bf16[120,256,256]{2,1,0:T(8,128)(2,1)S(1)}, u32[]{:S(2)}) %copy-start) | copy-done | bytes 15728664
  50.1 0.0 copy-done.6
  50.1 0.0 copy-done.7
  50.1 0.1 select_reduce_fusion.slots_ref
  50.2 27.9 %all-to-all-done.r_ref = bf16[128,32,384]{2,1,0:T(8,128)(2,1)S(1)} async-done(((bf16[128,32,384]{2,1,0:T(8,128)(2,1)}), bf16[128,32,384]{2,1,0:T(8,128)(2,1)S(1)}, u32[]{:S(2)}, u32[]{:S(2)}) %all-to-all-start) | async-done | bytes 3145760 | tf_op jit(solution)/shard_map/all_to_all | solution.py:468
  78.2 8.8 %correlate.1 = bf16[16,32,256]{2,1,0:T(8,128)(2,1)S(1)} custom-call(s32[120]{0:T(128)S(1)} %select_reduce_fusion.slots_ref, bf16[128,32,384]{2,1,0:T(8,128)(2,1)S(1)} %all-to-all-done.r_ref, bf16[120,256,256]{2,1,0:T(8,128)(2,1)} %copy-done), custom_call_target="tpu_custom_call" | custom-call | tf_op jit(solution)/shard_map/correlate/pallas_call | solution.py:439
  87.0 0.1 reshape.16
  87.1 10.2 %all_to_all.14 = bf16[16,16,2,256]{3,2,1,0:T(2,128)(2,1)S(1)} all-to-all(bf16[16,16,2,256]{3,2,1,0:T(2,128)(2,1)S(1)} %reshape.16), channel_id=1, replica_groups=mesh['chan'=16,'tm'=8] {'tm'}, dimensions={0} | all-to-all | bytes 524288 | tf_op jit(solution)/shard_map/all_to_all | solution.py:477
  97.3 1.0 %copy.10 = f32[8,2,16,2,256]{4,3,2,0,1:T(2,128)} copy(bf16[8,2,16,2,256]{4,3,2,1,0:T(2,128)(2,1)S(1)} %bitcast.6) | data formatting | bytes 786432 | tf_op jit(solution)/shard_map/convert_element_type | solution.py:477
Async XLA Ops:
  0.0 7.7 %copy-start.4 = (f32[16,4096]{1,0:T(8,128)S(1)}, f32[16,4096]{1,0:T(8,128)}, u32[]{:S(2)}) copy-start(f32[16,4096]{1,0:T(8,128)} %taps_ref.3) | copy-start | bytes 786436
  2.7 15.7 %collective-permute-start.1 = (bf16[16,8,4096]{2,1,0:T(8,128)(2,1)}, bf16[16,8,4096]{2,1,0:T(8,128)(2,1)S(1)}, u32[]{:S(2)}, u32[]{:S(2)}) collective-permute-start(bf16[16,8,4096]{2,1,0:T(8,128)(2,1)} %get-tuple-element.9), channel_id=1, source_target_pairs={{1,0},{2,1},{3,2},{4,3},{5,4},{6,5},{7,6},{0,7},{9,8},{10,9},{11,1... | collective-permute-start | bytes 3145736 | tf_op jit(solution)/shard_map/ppermute | solution.py:462
  4.2 15.2 %collective-permute-start = (bf16[16,8,4096]{2,1,0:T(8,128)(2,1)S(1)}, bf16[16,8,4096]{2,1,0:T(8,128)(2,1)S(1)}, u32[]{:S(2)}, u32[]{:S(2)}) collective-permute-start(bf16[16,8,4096]{2,1,0:T(8,128)(2,1)S(1)} %get-tuple-element.10), channel_id=1, source_target_pairs={{0,1},{1,2},{2,3},{3,4},{4,5},{5,6},{6,7},{8,9},{9,10},{10,11},{11... | collective-permute-start | bytes 3145736 | tf_op jit(solution)/shard_map/ppermute | solution.py:461
  7.7 11.7 %copy-start.1 = (bf16[7,512,512]{2,1,0:T(8,128)(2,1)S(1)}, bf16[7,512,512]{2,1,0:T(8,128)(2,1)}, u32[]{:S(2)}) copy-start(bf16[7,512,512]{2,1,0:T(8,128)(2,1)} %constant.12.clone.pairs_hbm.pairs_ref) | copy-start | bytes 11010052
  7.7 11.7 %copy-start.5 = (bf16[2,256,256]{2,1,0:T(8,128)(2,1)S(1)}, bf16[2,256,256]{2,1,0:T(8,128)(2,1)}, u32[]{:S(2)}) copy-start(bf16[2,256,256]{2,1,0:T(8,128)(2,1)} %constant.13.clone.ends_hbm.ends_ref) | copy-start | bytes 786436
  25.8 52.4 %all-to-all-start = ((bf16[128,32,384]{2,1,0:T(8,128)(2,1)}), bf16[128,32,384]{2,1,0:T(8,128)(2,1)S(1)}, u32[]{:S(2)}, u32[]{:S(2)}) async-start(bf16[128,32,384]{2,1,0:T(8,128)(2,1)} %rest.1), calls=%async_computation | async-start | bytes 6291456 | tf_op jit(solution)/shard_map/all_to_all | solution.py:468
  36.8 1.2 %copy-start.2 = (bf16[16,30720]{1,0:T(8,128)(2,1)S(1)}, bf16[16,30720]{1,0:T(8,128)(2,1)}, u32[]{:S(2)}) copy-start(bf16[16,30720]{1,0:T(8,128)(2,1)} %u_ref.1) | copy-start | bytes 2949124
  38.0 1.2 %copy-start.3 = (bf16[16,30720]{1,0:T(8,128)(2,1)S(1)}, bf16[16,30720]{1,0:T(8,128)(2,1)}, u32[]{:S(2)}) copy-start(bf16[16,30720]{1,0:T(8,128)(2,1)} %v_ref.1) | copy-start | bytes 2949124
  39.2 11.0 %copy-start.6 = (s32[120]{0:T(128)S(1)}, s32[120]{0:T(128)}, u32[]{:S(2)}) copy-start(s32[120]{0:T(128)} %param.10) | copy-start | bytes 1444
  39.2 11.0 %copy-start.7 = (s32[16]{0:T(128)S(1)}, s32[16]{0:T(128)}, u32[]{:S(2)}) copy-start(s32[16]{0:T(128)} %param.11) | copy-start | bytes 196
  44.6 5.5 %copy-start = (bf16[120,256,256]{2,1,0:T(8,128)(2,1)}, bf16[120,256,256]{2,1,0:T(8,128)(2,1)S(1)}, u32[]{:S(2)}) copy-start(bf16[120,256,256]{2,1,0:T(8,128)(2,1)S(1)} %grid_weights.1.k_ref) | copy-start | bytes 47185924

commit v7 on v6

--- a/solution.py
+++ b/solution.py
@@ -255,10 +255,10 @@
 def channel_scratch(frames, steps, length):
     rows = frames * SBLK
     return [
-        pltpu.VMEM((steps * PITCH, LANES), F32),
+        pltpu.VMEM(((steps + 1) * PITCH, LANES), F32),
         pltpu.VMEM((RADIX, rows, length // RADIX), BF),
         pltpu.VMEM((RADIX, rows, length // RADIX), BF),
-        pltpu.VMEM((rows // LANES, length // (2 * RADIX) * (2 * RADIX + PAD), LANES), F32),
+        pltpu.VMEM((rows // LANES, (length // (2 * RADIX) + 1) * (2 * RADIX + PAD), LANES), F32),
     ]
 
 
@@ -442,8 +442,8 @@
         in_specs=[smem, whole, pl.BlockSpec(memory_space=pl.ANY)],
         out_specs=whole,
         scratch_shapes=[
-            pltpu.VMEM((stations // LANES, group2 * (times * frames + PAD), LANES), F32),
-            pltpu.VMEM((stations // LANES, stations * (group2 + PAD), LANES), F32),
+            pltpu.VMEM((stations // LANES, (group2 + 1) * (times * frames + PAD), LANES), F32),
+            pltpu.VMEM((stations // LANES, (stations + 1) * (group2 + PAD), LANES), F32),
             pltpu.VMEM(weights.shape, BF),
             pltpu.VMEM((tiles, group2, GRID * GRID), F32),
             pltpu.SemaphoreType.DMA,

time: 98.7 us -> 98.7 us (level)
  no operation moved by 1% of the time
where the time goes in v7:
time: 98.7 us; the launch traced here: 98.3 us
  Pallas kernels  30.7 us (31%)
  waiting for transfers between devices  29.5 us (30%)
  starting transfers between devices  15.9 us (16%)
  local copies, waits for them, and re-layouts  11.8 us (12%)
  blocking collectives  10.2 us (10%)
    all_to_all x1, waiting for transfers between devices, body(): lax.all_to_all(spectra, ('chan', 'tm'), split_axis=0, concat_axis=0, tile...  27.9 us
    all_to_all x1, starting transfers between devices, body(): lax.all_to_all(spectra, ('chan', 'tm'), split_axis=0, concat_axis=0, tile...  11 us
    all_to_all x1, blocking collectives, body(): lax.all_to_all(partial_value, 'tm', split_axis=0, concat_axis=1, tiled=True)  10.2 us
    pallas_call x1, Pallas kernels, channelize_own(): pl.pallas_call(own_kernel, out_shape=[jax.ShapeDtypeStruct((dests, 2 * RA...  10.1 us
    pallas_call x1, Pallas kernels, correlate(): pl.pallas_call(functools.partial(correlate_kernel, (owners, times, frames...  8.79 us
    unnamed x16, local copies, waits for them, and re-layouts  7.92 us
    pallas_call x1, Pallas kernels, channelize_rest(): pl.pallas_call(rest_kernel, out_shape=jax.ShapeDtypeStruct((dests, 2 * RA...  6.38 us
    pallas_call x1, Pallas kernels, grid_weights(): pl.pallas_call(weights_kernel, grid=(count // step,), out_shape=jax.Shape...  5.46 us
  transfers between devices with their start and end apart: 3, of which 3 were waited for; matrix products, arithmetic and copies ran while one was open for 0% of the time, Pallas kernels for 16%

profile of v7, /device:TPU:1, one launch (start us, length us, event | category | flops | bytes accessed | tf_op | source)
XLA Modules:
  0.0 98.3 jit_solution(8695175412002202644)
XLA Ops:
  0.0 0.0 copy-start.4
  0.0 2.7 %fusion = (bf16[16,8,4096]{2,1,0:T(8,128)(2,1)}, bf16[16,8,4096]{2,1,0:T(8,128)(2,1)S(1)}) fusion(bf16[16,24,4096]{2,1,0:T(8,128)(2,1)} %x_hbm.1), kind=kLoop, calls=%fused_computation.1 | loop fusion | bytes 4194304 | tf_op jit(solution)/shard_map/slice | solution.py:460
  2.7 1.4 %collective-permute-start.1 = (bf16[16,8,4096]{2,1,0:T(8,128)(2,1)}, bf16[16,8,4096]{2,1,0:T(8,128)(2,1)S(1)}, u32[]{:S(2)}, u32[]{:S(2)}) collective-permute-start(bf16[16,8,4096]{2,1,0:T(8,128)(2,1)} %get-tuple-element.9), channel_id=1, source_target_pairs={{1,0},{2,1},{3,2},{4,3},{5,4},{6,5},{7,6},{0,7},{9,8},{10,9},{11,1... | collective-permute-start | bytes 3145736 | tf_op jit(solution)/shard_map/ppermute | solution.py:462
  4.2 3.5 %collective-permute-start = (bf16[16,8,4096]{2,1,0:T(8,128)(2,1)S(1)}, bf16[16,8,4096]{2,1,0:T(8,128)(2,1)S(1)}, u32[]{:S(2)}, u32[]{:S(2)}) collective-permute-start(bf16[16,8,4096]{2,1,0:T(8,128)(2,1)S(1)} %get-tuple-element.10), channel_id=1, source_target_pairs={{0,1},{1,2},{2,3},{3,4},{4,5},{5,6},{6,7},{8,9},{9,10},{10,11},{11... | collective-permute-start | bytes 3145736 | tf_op jit(solution)/shard_map/ppermute | solution.py:461
  7.7 0.0 copy-done.4
  7.7 0.0 copy-start.1
  7.7 0.0 copy-start.5
  7.7 10.1 %own.1 = (bf16[128,32,128]{2,1,0:T(8,128)(2,1)S(1)}, f32[32,256,128]{2,1,0:T(8,128)S(1)}) custom-call(f32[1]{0:T(128)} %bitcast.keep_ref, bf16[16,24,4096]{2,1,0:T(8,128)(2,1)} %x_hbm.1, f32[16,4096]{1,0:T(8,128)S(1)} %copy-done.4, bf16[7,512,512]{2,1,0:T(8,128)(2,1)} %constant.12.clone.pairs_hbm.pairs_ref, bf16[2,256,256]{2,1,0:T(8,128)(2,1)} %constant.13.clone.ends_hbm.ends_ref), custom_call_target="tpu_custom_call" | custom-call | flops 15728640000 | bytes 20971520 | tf_op jit(solution)/shard_map/own/pallas_call | solution.py:269
  17.8 0.7 collective-permute-done.1.right_ref
  18.5 0.9 collective-permute-done.left_ref
  19.4 0.0 copy-done.1
  19.4 0.0 copy-done.5
  19.4 6.4 %rest.1 = bf16[128,32,384]{2,1,0:T(8,128)(2,1)} custom-call(bf16[16,8,4096]{2,1,0:T(8,128)(2,1)S(1)} %collective-permute-done.left_ref, bf16[16,8,4096]{2,1,0:T(8,128)(2,1)S(1)} %collective-permute-done.1.right_ref, f32[16,4096]{1,0:T(8,128)S(1)} %copy-done.4, bf16[7,512,512]{2,1,0:T(8,128)(2,1)S(1)} %copy-done.1, bf16[2,256,256]{2,1,0:T(8,128)(2,1)S(1)} %copy-done.5, ...), custom_call_target="tpu_custom_call" | custom-call | tf_op jit(solution)/shard_map/rest/pallas_call | solution.py:305
  25.8 11.0 %all-to-all-start = ((bf16[128,32,384]{2,1,0:T(8,128)(2,1)}), bf16[128,32,384]{2,1,0:T(8,128)(2,1)S(1)}, u32[]{:S(2)}, u32[]{:S(2)}) async-start(bf16[128,32,384]{2,1,0:T(8,128)(2,1)} %rest.1), calls=%async_computation | async-start | bytes 6291456 | tf_op jit(solution)/shard_map/all_to_all | solution.py:468
  36.8 0.0 copy-start.2
  36.8 1.2 %copy-done.2 = bf16[16,30720]{1,0:T(8,128)(2,1)S(1)} copy-done((bf16[16,30720]{1,0:T(8,128)(2,1)S(1)}, bf16[16,30720]{1,0:T(8,128)(2,1)}, u32[]{:S(2)}) %copy-start.2) | copy-done | bytes 983064
  38.0 0.0 copy-start.3
  38.0 1.2 %copy-done.3 = bf16[16,30720]{1,0:T(8,128)(2,1)S(1)} copy-done((bf16[16,30720]{1,0:T(8,128)(2,1)S(1)}, bf16[16,30720]{1,0:T(8,128)(2,1)}, u32[]{:S(2)}) %copy-start.3) | copy-done | bytes 983064
  39.2 0.0 copy-start.6
  39.2 0.0 copy-start.7
  39.2 5.5 %grid_weights.1.k_ref = bf16[120,256,256]{2,1,0:T(8,128)(2,1)S(1)} custom-call(bf16[16,30720]{1,0:T(8,128)(2,1)S(1)} %copy-done.2, bf16[16,30720]{1,0:T(8,128)(2,1)S(1)} %copy-done.3), custom_call_target="tpu_custom_call" | custom-call | flops 7864320 | bytes 15728640 | tf_op jit(solution)/shard_map/grid_weights/pallas_call | solution.py:344
  44.6 0.0 copy-start
  44.6 5.5 %copy-done = bf16[120,256,256]{2,1,0:T(8,128)(2,1)} copy-done((bf16[120,256,256]{2,1,0:T(8,128)(2,1)}, bf16[120,256,256]{2,1,0:T(8,128)(2,1)S(1)}, u32[]{:S(2)}) %copy-start) | copy-done | bytes 15728664
  50.1 0.0 copy-done.6
  50.1 0.0 copy-done.7
  50.1 0.1 select_reduce_fusion.slots_ref
  50.2 27.9 %all-to-all-done.r_ref = bf16[128,32,384]{2,1,0:T(8,128)(2,1)S(1)} async-done(((bf16[128,32,384]{2,1,0:T(8,128)(2,1)}), bf16[128,32,384]{2,1,0:T(8,128)(2,1)S(1)}, u32[]{:S(2)}, u32[]{:S(2)}) %all-to-all-start) | async-done | bytes 3145760 | tf_op jit(solution)/shard_map/all_to_all | solution.py:468
  78.2 8.8 %correlate.1 = bf16[16,32,256]{2,1,0:T(8,128)(2,1)S(1)} custom-call(s32[120]{0:T(128)S(1)} %select_reduce_fusion.slots_ref, bf16[128,32,384]{2,1,0:T(8,128)(2,1)S(1)} %all-to-all-done.r_ref, bf16[120,256,256]{2,1,0:T(8,128)(2,1)} %copy-done), custom_call_target="tpu_custom_call" | custom-call | tf_op jit(solution)/shard_map/correlate/pallas_call | solution.py:439
  87.0 0.1 reshape.16
  87.1 10.2 %all_to_all.14 = bf16[16,16,2,256]{3,2,1,0:T(2,128)(2,1)S(1)} all-to-all(bf16[16,16,2,256]{3,2,1,0:T(2,128)(2,1)S(1)} %reshape.16), channel_id=1, replica_groups=mesh['chan'=16,'tm'=8] {'tm'}, dimensions={0} | all-to-all | bytes 524288 | tf_op jit(solution)/shard_map/all_to_all | solution.py:477
  97.3 1.0 %copy.10 = f32[8,2,16,2,256]{4,3,2,0,1:T(2,128)} copy(bf16[8,2,16,2,256]{4,3,2,1,0:T(2,128)(2,1)S(1)} %bitcast.6) | data formatting | bytes 786432 | tf_op jit(solution)/shard_map/convert_element_type | solution.py:477
Async XLA Ops:
  0.0 7.7 %copy-start.4 = (f32[16,4096]{1,0:T(8,128)S(1)}, f32[16,4096]{1,0:T(8,128)}, u32[]{:S(2)}) copy-start(f32[16,4096]{1,0:T(8,128)} %taps_ref.3) | copy-start | bytes 786436
  2.7 15.7 %collective-permute-start.1 = (bf16[16,8,4096]{2,1,0:T(8,128)(2,1)}, bf16[16,8,4096]{2,1,0:T(8,128)(2,1)S(1)}, u32[]{:S(2)}, u32[]{:S(2)}) collective-permute-start(bf16[16,8,4096]{2,1,0:T(8,128)(2,1)} %get-tuple-element.9), channel_id=1, source_target_pairs={{1,0},{2,1},{3,2},{4,3},{5,4},{6,5},{7,6},{0,7},{9,8},{10,9},{11,1... | collective-permute-start | bytes 3145736 | tf_op jit(solution)/shard_map/ppermute | solution.py:462
  4.2 15.2 %collective-permute-start = (bf16[16,8,4096]{2,1,0:T(8,128)(2,1)S(1)}, bf16[16,8,4096]{2,1,0:T(8,128)(2,1)S(1)}, u32[]{:S(2)}, u32[]{:S(2)}) collective-permute-start(bf16[16,8,4096]{2,1,0:T(8,128)(2,1)S(1)} %get-tuple-element.10), channel_id=1, source_target_pairs={{0,1},{1,2},{2,3},{3,4},{4,5},{5,6},{6,7},{8,9},{9,10},{10,11},{11... | collective-permute-start | bytes 3145736 | tf_op jit(solution)/shard_map/ppermute | solution.py:461
  7.7 11.7 %copy-start.1 = (bf16[7,512,512]{2,1,0:T(8,128)(2,1)S(1)}, bf16[7,512,512]{2,1,0:T(8,128)(2,1)}, u32[]{:S(2)}) copy-start(bf16[7,512,512]{2,1,0:T(8,128)(2,1)} %constant.12.clone.pairs_hbm.pairs_ref) | copy-start | bytes 11010052
  7.7 11.7 %copy-start.5 = (bf16[2,256,256]{2,1,0:T(8,128)(2,1)S(1)}, bf16[2,256,256]{2,1,0:T(8,128)(2,1)}, u32[]{:S(2)}) copy-start(bf16[2,256,256]{2,1,0:T(8,128)(2,1)} %constant.13.clone.ends_hbm.ends_ref) | copy-start | bytes 786436
  25.8 52.4 %all-to-all-start = ((bf16[128,32,384]{2,1,0:T(8,128)(2,1)}), bf16[128,32,384]{2,1,0:T(8,128)(2,1)S(1)}, u32[]{:S(2)}, u32[]{:S(2)}) async-start(bf16[128,32,384]{2,1,0:T(8,128)(2,1)} %rest.1), calls=%async_computation | async-start | bytes 6291456 | tf_op jit(solution)/shard_map/all_to_all | solution.py:468
  36.8 1.2 %copy-start.2 = (bf16[16,30720]{1,0:T(8,128)(2,1)S(1)}, bf16[16,30720]{1,0:T(8,128)(2,1)}, u32[]{:S(2)}) copy-start(bf16[16,30720]{1,0:T(8,128)(2,1)} %u_ref.1) | copy-start | bytes 2949124
  38.0 1.2 %copy-start.3 = (bf16[16,30720]{1,0:T(8,128)(2,1)S(1)}, bf16[16,30720]{1,0:T(8,128)(2,1)}, u32[]{:S(2)}) copy-start(bf16[16,30720]{1,0:T(8,128)(2,1)} %v_ref.1) | copy-start | bytes 2949124
  39.2 11.0 %copy-start.6 = (s32[120]{0:T(128)S(1)}, s32[120]{0:T(128)}, u32[]{:S(2)}) copy-start(s32[120]{0:T(128)} %param.10) | copy-start | bytes 1444
  39.2 11.0 %copy-start.7 = (s32[16]{0:T(128)S(1)}, s32[16]{0:T(128)}, u32[]{:S(2)}) copy-start(s32[16]{0:T(128)} %param.11) | copy-start | bytes 196
  44.6 5.5 %copy-start = (bf16[120,256,256]{2,1,0:T(8,128)(2,1)}, bf16[120,256,256]{2,1,0:T(8,128)(2,1)S(1)}, u32[]{:S(2)}) copy-start(bf16[120,256,256]{2,1,0:T(8,128)(2,1)S(1)} %grid_weights.1.k_ref) | copy-start | bytes 47185924

commit v8 on v7

--- a/solution.py
+++ b/solution.py
@@ -199,7 +199,7 @@
 
 
 def rest_kernel(
-    left_ref, right_ref, taps_ref, pairs_ref, ends_ref, done_ref, part_ref, out_hbm, xs, filt, low, turned, stage, sems
+    right_ref, left_ref, taps_ref, pairs_ref, ends_ref, done_ref, part_ref, out_hbm, xs, filt, low, turned, stage, sems
 ):
     width = stage.shape[2]
     finished = pltpu.make_async_copy(done_ref, out_hbm.at[:, :, width:], sems.at[PIECES])
@@ -260,6 +260,31 @@
         pltpu.VMEM((RADIX, rows, length // RADIX), BF),
         pltpu.VMEM((rows // LANES, (length // (2 * RADIX) + 1) * (2 * RADIX + PAD), LANES), F32),
     ]
+
+
+def ends_kernel(x_ref, first_ref, last_ref, sems):
+    frames = x_ref.shape[1]
+    copies = [
+        pltpu.make_async_copy(x_ref.at[:, :HALO, :], first_ref, sems.at[0]),
+        pltpu.make_async_copy(x_ref.at[:, frames - HALO :, :], last_ref, sems.at[1]),
+    ]
+    for copy in copies:
+        copy.start()
+    for copy in copies:
+        copy.wait()
+
+
+def end_frames(samples):
+    stations, _, length = samples.shape
+    return pl.pallas_call(
+        ends_kernel,
+        out_shape=[jax.ShapeDtypeStruct((stations, HALO, length), BF)] * 2,
+        in_specs=[pl.BlockSpec(memory_space=pltpu.HBM)],
+        out_specs=[pl.BlockSpec(memory_space=pltpu.VMEM)] * 2,
+        scratch_shapes=[pltpu.SemaphoreType.DMA((2,))],
+        compiler_params=pltpu.CompilerParams(vmem_limit_bytes=8 << 20),
+        name="end_frames",
+    )(pltpu.with_memory_space_constraint(samples, pltpu.HBM))
 
 
 def channelize_own(keep, samples, taps, pairs, ends):
@@ -314,7 +339,7 @@
         ],
         compiler_params=pltpu.CompilerParams(vmem_limit_bytes=28 << 20),
         name="rest",
-    )(before, after, taps, pairs, ends, done, part)
+    )(after, before, taps, pairs, ends, done, part)
 
 
 def swap_groups(v):
@@ -458,8 +483,9 @@
     chan_size = lax.axis_size("chan")
     tm_size = lax.axis_size("tm")
     last, first = samples[:, frame_count - HALO :], samples[:, :HALO]
+    first, last = end_frames(samples)
+    after = lax.ppermute(first, "tm", [((i + 1) % tm_size, i) for i in range(tm_size)])
     before = lax.ppermute(last, "tm", [(i, i + 1) for i in range(tm_size - 1)])
-    after = lax.ppermute(first, "tm", [((i + 1) % tm_size, i) for i in range(tm_size)])
     keep = (lax.axis_index("tm") < tm_size - 1).astype(F32).reshape(1)
     weights = grid_weights(kern_u, kern_v)
     pairs, ends = (jnp.asarray(table) for table in dft_tables(samples.shape[2]))

time: 98.7 us -> 98.5 us (level)
  Pallas kernels: 30.7 us -> 33.2 us
  local copies, waits for them, and re-layouts: 11.8 us -> 9.97 us
    slice x1 -> x0, local copies, waits for them, and re-layouts: 2.73 us -> none  [body(): last, first = (samples[:, frame_count - HALO:], samples[:, :HALO])]
    pallas_call x0 -> x1, Pallas kernels: none -> 2.53 us  [end_frames(): pl.pallas_call(ends_kernel, out_shape=[jax.ShapeDtypeStruct((stations, HA...]
    unnamed x16 -> x18, local copies, waits for them, and re-layouts: 7.92 us -> 8.85 us
  transfers between devices with their start and end apart: 3 -> 3, of which waited for: 3 -> 2; matrix products, arithmetic and copies ran while one was open for 0% -> 0% of each run, Pallas kernels for 16% -> 16%
where the time goes in v8:
time: 98.5 us; the launch traced here: 98.1 us
  Pallas kernels  33.2 us (34%)
  waiting for transfers between devices  28.6 us (29%)
  starting transfers between devices  15.9 us (16%)
  blocking collectives  10.2 us (10%)
  local copies, waits for them, and re-layouts  9.97 us (10%)
    all_to_all x1, waiting for transfers between devices, body(): lax.all_to_all(spectra, ('chan', 'tm'), split_axis=0, concat_axis=0, tile...  28 us
    all_to_all x1, starting transfers between devices, body(): lax.all_to_all(spectra, ('chan', 'tm'), split_axis=0, concat_axis=0, tile...  11 us
    all_to_all x1, blocking collectives, body(): lax.all_to_all(partial_value, 'tm', split_axis=0, concat_axis=1, tiled=True)  10.2 us
    pallas_call x1, Pallas kernels, channelize_own(): pl.pallas_call(own_kernel, out_shape=[jax.ShapeDtypeStruct((dests, 2 * RA...  10.1 us
    unnamed x18, local copies, waits for them, and re-layouts  8.85 us
    pallas_call x1, Pallas kernels, correlate(): pl.pallas_call(functools.partial(correlate_kernel, (owners, times, frames...  8.79 us
    pallas_call x1, Pallas kernels, channelize_rest(): pl.pallas_call(rest_kernel, out_shape=jax.ShapeDtypeStruct((dests, 2 * RA...  6.36 us
    pallas_call x1, Pallas kernels, grid_weights(): pl.pallas_call(weights_kernel, grid=(count // step,), out_shape=jax.Shape...  5.46 us
  transfers between devices with their start and end apart: 3, of which 2 were waited for; matrix products, arithmetic and copies ran while one was open for 0% of the time, Pallas kernels for 16%

profile of v8, /device:TPU:1, one launch (start us, length us, event | category | flops | bytes accessed | tf_op | source)
XLA Modules:
  0.0 98.1 jit_solution(1480261882893315978)
XLA Ops:
  0.0 2.5 %end_frames.1 = (bf16[16,8,4096]{2,1,0:T(8,128)(2,1)}, bf16[16,8,4096]{2,1,0:T(8,128)(2,1)S(1)}) custom-call(bf16[16,24,4096]{2,1,0:T(8,128)(2,1)} %x_hbm.1), custom_call_target="tpu_custom_call" | custom-call | tf_op jit(solution)/shard_map/end_frames/pallas_call | solution.py:279
  2.5 1.4 %collective-permute-start = (bf16[16,8,4096]{2,1,0:T(8,128)(2,1)}, bf16[16,8,4096]{2,1,0:T(8,128)(2,1)S(1)}, u32[]{:S(2)}, u32[]{:S(2)}) collective-permute-start(bf16[16,8,4096]{2,1,0:T(8,128)(2,1)} %get-tuple-element.9), channel_id=1, source_target_pairs={{1,0},{2,1},{3,2},{4,3},{5,4},{6,5},{7,6},{0,7},{9,8},{10,9},{11,1... | collective-permute-start | bytes 3145736 | tf_op jit(solution)/shard_map/ppermute | solution.py:487
  4.0 3.5 %collective-permute-start.1 = (bf16[16,8,4096]{2,1,0:T(8,128)(2,1)S(1)}, bf16[16,8,4096]{2,1,0:T(8,128)(2,1)S(1)}, u32[]{:S(2)}, u32[]{:S(2)}) collective-permute-start(bf16[16,8,4096]{2,1,0:T(8,128)(2,1)S(1)} %get-tuple-element.10), channel_id=1, source_target_pairs={{0,1},{1,2},{2,3},{3,4},{4,5},{5,6},{6,7},{8,9},{9,10},{10,11},{11... | collective-permute-start | bytes 3145736 | tf_op jit(solution)/shard_map/ppermute | solution.py:488
  7.5 0.0 copy-start.4
  7.5 0.9 copy-done.4
  8.5 0.0 copy-start.1
  8.5 0.0 copy-start.5
  8.5 0.0 copy-start.6
  8.5 10.1 %own.1 = (bf16[128,32,128]{2,1,0:T(8,128)(2,1)S(1)}, f32[32,256,128]{2,1,0:T(8,128)S(1)}) custom-call(f32[1]{0:T(128)} %bitcast.keep_ref, bf16[16,24,4096]{2,1,0:T(8,128)(2,1)} %x_hbm.1, f32[16,4096]{1,0:T(8,128)S(1)} %copy-done.4, bf16[7,512,512]{2,1,0:T(8,128)(2,1)} %constant.12.clone.pairs_hbm.pairs_ref, bf16[2,256,256]{2,1,0:T(8,128)(2,1)} %constant.13.clone.ends_hbm.ends_ref), custom_call_target="tpu_custom_call" | custom-call | flops 15728640000 | bytes 20971520 | tf_op jit(solution)/shard_map/own/pallas_call | solution.py:294
  18.6 0.0 collective-permute-done.right_ref
  18.6 0.7 collective-permute-done.1.left_ref
  19.2 0.0 copy-done.1
  19.2 0.0 copy-done.5
  19.2 0.0 copy-done.6
  19.2 6.4 %rest.1 = bf16[128,32,384]{2,1,0:T(8,128)(2,1)} custom-call(bf16[16,8,4096]{2,1,0:T(8,128)(2,1)S(1)} %collective-permute-done.right_ref, bf16[16,8,4096]{2,1,0:T(8,128)(2,1)S(1)} %collective-permute-done.1.left_ref, f32[16,4096]{1,0:T(8,128)S(1)} %copy-done.5, bf16[7,512,512]{2,1,0:T(8,128)(2,1)S(1)} %copy-done.1, bf16[2,256,256]{2,1,0:T(8,128)(2,1)S(1)} %copy-done.6, ...), custom_call_target="tpu_custom_call" | custom-call | tf_op jit(solution)/shard_map/rest/pallas_call | solution.py:330
  25.6 11.0 %all-to-all-start = ((bf16[128,32,384]{2,1,0:T(8,128)(2,1)}), bf16[128,32,384]{2,1,0:T(8,128)(2,1)S(1)}, u32[]{:S(2)}, u32[]{:S(2)}) async-start(bf16[128,32,384]{2,1,0:T(8,128)(2,1)} %rest.1), calls=%async_computation | async-start | bytes 6291456 | tf_op jit(solution)/shard_map/all_to_all | solution.py:494
  36.6 0.0 copy-start.2
  36.6 1.2 %copy-done.2 = bf16[16,30720]{1,0:T(8,128)(2,1)S(1)} copy-done((bf16[16,30720]{1,0:T(8,128)(2,1)S(1)}, bf16[16,30720]{1,0:T(8,128)(2,1)}, u32[]{:S(2)}) %copy-start.2) | copy-done | bytes 983064
  37.8 0.0 copy-start.3
  37.8 1.2 %copy-done.3 = bf16[16,30720]{1,0:T(8,128)(2,1)S(1)} copy-done((bf16[16,30720]{1,0:T(8,128)(2,1)S(1)}, bf16[16,30720]{1,0:T(8,128)(2,1)}, u32[]{:S(2)}) %copy-start.3) | copy-done | bytes 983064
  39.0 0.0 copy-start.7
  39.0 0.0 copy-start.8
  39.0 5.5 %grid_weights.1.k_ref = bf16[120,256,256]{2,1,0:T(8,128)(2,1)S(1)} custom-call(bf16[16,30720]{1,0:T(8,128)(2,1)S(1)} %copy-done.2, bf16[16,30720]{1,0:T(8,128)(2,1)S(1)} %copy-done.3), custom_call_target="tpu_custom_call" | custom-call | flops 7864320 | bytes 15728640 | tf_op jit(solution)/shard_map/grid_weights/pallas_call | solution.py:369
  44.4 0.0 copy-start
  44.5 5.5 %copy-done = bf16[120,256,256]{2,1,0:T(8,128)(2,1)} copy-done((bf16[120,256,256]{2,1,0:T(8,128)(2,1)}, bf16[120,256,256]{2,1,0:T(8,128)(2,1)S(1)}, u32[]{:S(2)}) %copy-start) | copy-done | bytes 15728664
  49.9 0.0 copy-done.7
  49.9 0.0 copy-done.8
  50.0 0.1 select_reduce_fusion.slots_ref
  50.0 28.0 %all-to-all-done.r_ref = bf16[128,32,384]{2,1,0:T(8,128)(2,1)S(1)} async-done(((bf16[128,32,384]{2,1,0:T(8,128)(2,1)}), bf16[128,32,384]{2,1,0:T(8,128)(2,1)S(1)}, u32[]{:S(2)}, u32[]{:S(2)}) %all-to-all-start) | async-done | bytes 3145760 | tf_op jit(solution)/shard_map/all_to_all | solution.py:494
  78.0 8.8 %correlate.1 = bf16[16,32,256]{2,1,0:T(8,128)(2,1)S(1)} custom-call(s32[120]{0:T(128)S(1)} %select_reduce_fusion.slots_ref, bf16[128,32,384]{2,1,0:T(8,128)(2,1)S(1)} %all-to-all-done.r_ref, bf16[120,256,256]{2,1,0:T(8,128)(2,1)} %copy-done), custom_call_target="tpu_custom_call" | custom-call | tf_op jit(solution)/shard_map/correlate/pallas_call | solution.py:464
  86.8 0.1 reshape.16
  86.9 10.2 %all_to_all.14 = bf16[16,16,2,256]{3,2,1,0:T(2,128)(2,1)S(1)} all-to-all(bf16[16,16,2,256]{3,2,1,0:T(2,128)(2,1)S(1)} %reshape.16), channel_id=1, replica_groups=mesh['chan'=16,'tm'=8] {'tm'}, dimensions={0} | all-to-all | bytes 524288 | tf_op jit(solution)/shard_map/all_to_all | solution.py:503
  97.1 1.0 %copy.10 = f32[8,2,16,2,256]{4,3,2,0,1:T(2,128)} copy(bf16[8,2,16,2,256]{4,3,2,1,0:T(2,128)(2,1)S(1)} %bitcast.6) | data formatting | bytes 786432 | tf_op jit(solution)/shard_map/convert_element_type | solution.py:503
Async XLA Ops:
  2.5 16.0 %collective-permute-start = (bf16[16,8,4096]{2,1,0:T(8,128)(2,1)}, bf16[16,8,4096]{2,1,0:T(8,128)(2,1)S(1)}, u32[]{:S(2)}, u32[]{:S(2)}) collective-permute-start(bf16[16,8,4096]{2,1,0:T(8,128)(2,1)} %get-tuple-element.9), channel_id=1, source_target_pairs={{1,0},{2,1},{3,2},{4,3},{5,4},{6,5},{7,6},{0,7},{9,8},{10,9},{11,1... | collective-permute-start | bytes 3145736 | tf_op jit(solution)/shard_map/ppermute | solution.py:487
  4.0 15.3 %collective-permute-start.1 = (bf16[16,8,4096]{2,1,0:T(8,128)(2,1)S(1)}, bf16[16,8,4096]{2,1,0:T(8,128)(2,1)S(1)}, u32[]{:S(2)}, u32[]{:S(2)}) collective-permute-start(bf16[16,8,4096]{2,1,0:T(8,128)(2,1)S(1)} %get-tuple-element.10), channel_id=1, source_target_pairs={{0,1},{1,2},{2,3},{3,4},{4,5},{5,6},{6,7},{8,9},{9,10},{10,11},{11... | collective-permute-start | bytes 3145736 | tf_op jit(solution)/shard_map/ppermute | solution.py:488
  7.5 1.0 copy-start.4
  8.5 10.8 %copy-start.1 = (bf16[7,512,512]{2,1,0:T(8,128)(2,1)S(1)}, bf16[7,512,512]{2,1,0:T(8,128)(2,1)}, u32[]{:S(2)}) copy-start(bf16[7,512,512]{2,1,0:T(8,128)(2,1)} %constant.12.clone.pairs_hbm.pairs_ref) | copy-start | bytes 11010052
  8.5 10.8 %copy-start.5 = (f32[16,4096]{1,0:T(8,128)S(1)}, f32[16,4096]{1,0:T(8,128)}, u32[]{:S(2)}) copy-start(f32[16,4096]{1,0:T(8,128)} %taps_ref.3) | copy-start | bytes 786436
  8.5 10.8 %copy-start.6 = (bf16[2,256,256]{2,1,0:T(8,128)(2,1)S(1)}, bf16[2,256,256]{2,1,0:T(8,128)(2,1)}, u32[]{:S(2)}) copy-start(bf16[2,256,256]{2,1,0:T(8,128)(2,1)} %constant.13.clone.ends_hbm.ends_ref) | copy-start | bytes 786436
  25.6 52.4 %all-to-all-start = ((bf16[128,32,384]{2,1,0:T(8,128)(2,1)}), bf16[128,32,384]{2,1,0:T(8,128)(2,1)S(1)}, u32[]{:S(2)}, u32[]{:S(2)}) async-start(bf16[128,32,384]{2,1,0:T(8,128)(2,1)} %rest.1), calls=%async_computation | async-start | bytes 6291456 | tf_op jit(solution)/shard_map/all_to_all | solution.py:494
  36.6 1.2 %copy-start.2 = (bf16[16,30720]{1,0:T(8,128)(2,1)S(1)}, bf16[16,30720]{1,0:T(8,128)(2,1)}, u32[]{:S(2)}) copy-start(bf16[16,30720]{1,0:T(8,128)(2,1)} %u_ref.1) | copy-start | bytes 2949124
  37.8 1.2 %copy-start.3 = (bf16[16,30720]{1,0:T(8,128)(2,1)S(1)}, bf16[16,30720]{1,0:T(8,128)(2,1)}, u32[]{:S(2)}) copy-start(bf16[16,30720]{1,0:T(8,128)(2,1)} %v_ref.1) | copy-start | bytes 2949124
  39.0 11.0 %copy-start.7 = (s32[120]{0:T(128)S(1)}, s32[120]{0:T(128)}, u32[]{:S(2)}) copy-start(s32[120]{0:T(128)} %param.10) | copy-start | bytes 1444
  39.0 11.0 %copy-start.8 = (s32[16]{0:T(128)S(1)}, s32[16]{0:T(128)}, u32[]{:S(2)}) copy-start(s32[16]{0:T(128)} %param.11) | copy-start | bytes 196
  44.4 5.5 %copy-start = (bf16[120,256,256]{2,1,0:T(8,128)(2,1)}, bf16[120,256,256]{2,1,0:T(8,128)(2,1)S(1)}, u32[]{:S(2)}) copy-start(bf16[120,256,256]{2,1,0:T(8,128)(2,1)S(1)} %grid_weights.1.k_ref) | copy-start | bytes 47185924

commit v9 on v8

--- a/solution.py
+++ b/solution.py
@@ -230,7 +230,7 @@
                 filt[tile, to, lanes] = value.astype(BF)
         return 0
 
-    lax.fori_loop(0, RADIX, fir, 0)
+    lax.fori_loop(0, RADIX, fir, 0, unroll=2)
     butterflies(filt, low)
     products(low, turned, pairs_ref, ends_ref)
     count = stage.shape[0] // PIECES

time: 98.5 us -> 98.4 us (level)
  no operation moved by 1% of the time
where the time goes in v9:
time: 98.4 us; the launch traced here: 98 us
  Pallas kernels  33.1 us (34%)
  waiting for transfers between devices  28.6 us (29%)
  starting transfers between devices  15.9 us (16%)
  blocking collectives  10.2 us (10%)
  local copies, waits for them, and re-layouts  9.97 us (10%)
    all_to_all x1, waiting for transfers between devices, body(): lax.all_to_all(spectra, ('chan', 'tm'), split_axis=0, concat_axis=0, tile...  28 us
    all_to_all x1, starting transfers between devices, body(): lax.all_to_all(spectra, ('chan', 'tm'), split_axis=0, concat_axis=0, tile...  11 us
    all_to_all x1, blocking collectives, body(): lax.all_to_all(partial_value, 'tm', split_axis=0, concat_axis=1, tiled=True)  10.2 us
    pallas_call x1, Pallas kernels, channelize_own(): pl.pallas_call(own_kernel, out_shape=[jax.ShapeDtypeStruct((dests, 2 * RA...  10.1 us
    unnamed x18, local copies, waits for them, and re-layouts  8.85 us
    pallas_call x1, Pallas kernels, correlate(): pl.pallas_call(functools.partial(correlate_kernel, (owners, times, frames...  8.8 us
    pallas_call x1, Pallas kernels, channelize_rest(): pl.pallas_call(rest_kernel, out_shape=jax.ShapeDtypeStruct((dests, 2 * RA...  6.21 us
    pallas_call x1, Pallas kernels, grid_weights(): pl.pallas_call(weights_kernel, grid=(count // step,), out_shape=jax.Shape...  5.46 us
  transfers between devices with their start and end apart: 3, of which 2 were waited for; matrix products, arithmetic and copies ran while one was open for 0% of the time, Pallas kernels for 16%

profile of v9, /device:TPU:1, one launch (start us, length us, event | category | flops | bytes accessed | tf_op | source)
XLA Modules:
  0.0 98.0 jit_solution(15090310745130252568)
XLA Ops:
  0.0 2.5 %end_frames.1 = (bf16[16,8,4096]{2,1,0:T(8,128)(2,1)}, bf16[16,8,4096]{2,1,0:T(8,128)(2,1)S(1)}) custom-call(bf16[16,24,4096]{2,1,0:T(8,128)(2,1)} %x_hbm.1), custom_call_target="tpu_custom_call" | custom-call | tf_op jit(solution)/shard_map/end_frames/pallas_call | solution.py:279
  2.5 1.4 %collective-permute-start = (bf16[16,8,4096]{2,1,0:T(8,128)(2,1)}, bf16[16,8,4096]{2,1,0:T(8,128)(2,1)S(1)}, u32[]{:S(2)}, u32[]{:S(2)}) collective-permute-start(bf16[16,8,4096]{2,1,0:T(8,128)(2,1)} %get-tuple-element.9), channel_id=1, source_target_pairs={{1,0},{2,1},{3,2},{4,3},{5,4},{6,5},{7,6},{0,7},{9,8},{10,9},{11,1... | collective-permute-start | bytes 3145736 | tf_op jit(solution)/shard_map/ppermute | solution.py:487
  4.0 3.5 %collective-permute-start.1 = (bf16[16,8,4096]{2,1,0:T(8,128)(2,1)S(1)}, bf16[16,8,4096]{2,1,0:T(8,128)(2,1)S(1)}, u32[]{:S(2)}, u32[]{:S(2)}) collective-permute-start(bf16[16,8,4096]{2,1,0:T(8,128)(2,1)S(1)} %get-tuple-element.10), channel_id=1, source_target_pairs={{0,1},{1,2},{2,3},{3,4},{4,5},{5,6},{6,7},{8,9},{9,10},{10,11},{11... | collective-permute-start | bytes 3145736 | tf_op jit(solution)/shard_map/ppermute | solution.py:488
  7.5 0.0 copy-start.4
  7.5 0.9 copy-done.4
  8.5 0.0 copy-start.1
  8.5 0.0 copy-start.5
  8.5 0.0 copy-start.6
  8.5 10.1 %own.1 = (bf16[128,32,128]{2,1,0:T(8,128)(2,1)S(1)}, f32[32,256,128]{2,1,0:T(8,128)S(1)}) custom-call(f32[1]{0:T(128)} %bitcast.keep_ref, bf16[16,24,4096]{2,1,0:T(8,128)(2,1)} %x_hbm.1, f32[16,4096]{1,0:T(8,128)S(1)} %copy-done.4, bf16[7,512,512]{2,1,0:T(8,128)(2,1)} %constant.12.clone.pairs_hbm.pairs_ref, bf16[2,256,256]{2,1,0:T(8,128)(2,1)} %constant.13.clone.ends_hbm.ends_ref), custom_call_target="tpu_custom_call" | custom-call | flops 15728640000 | bytes 20971520 | tf_op jit(solution)/shard_map/own/pallas_call | solution.py:294
  18.6 0.0 collective-permute-done.right_ref
  18.6 0.7 collective-permute-done.1.left_ref
  19.2 0.0 copy-done.1
  19.2 0.0 copy-done.5
  19.2 0.0 copy-done.6
  19.2 6.2 %rest.1 = bf16[128,32,384]{2,1,0:T(8,128)(2,1)} custom-call(bf16[16,8,4096]{2,1,0:T(8,128)(2,1)S(1)} %collective-permute-done.right_ref, bf16[16,8,4096]{2,1,0:T(8,128)(2,1)S(1)} %collective-permute-done.1.left_ref, f32[16,4096]{1,0:T(8,128)S(1)} %copy-done.5, bf16[7,512,512]{2,1,0:T(8,128)(2,1)S(1)} %copy-done.1, bf16[2,256,256]{2,1,0:T(8,128)(2,1)S(1)} %copy-done.6, ...), custom_call_target="tpu_custom_call" | custom-call | tf_op jit(solution)/shard_map/rest/pallas_call | solution.py:330
  25.5 11.0 %all-to-all-start = ((bf16[128,32,384]{2,1,0:T(8,128)(2,1)}), bf16[128,32,384]{2,1,0:T(8,128)(2,1)S(1)}, u32[]{:S(2)}, u32[]{:S(2)}) async-start(bf16[128,32,384]{2,1,0:T(8,128)(2,1)} %rest.1), calls=%async_computation | async-start | bytes 6291456 | tf_op jit(solution)/shard_map/all_to_all | solution.py:494
  36.4 0.0 copy-start.2
  36.4 1.2 %copy-done.2 = bf16[16,30720]{1,0:T(8,128)(2,1)S(1)} copy-done((bf16[16,30720]{1,0:T(8,128)(2,1)S(1)}, bf16[16,30720]{1,0:T(8,128)(2,1)}, u32[]{:S(2)}) %copy-start.2) | copy-done | bytes 983064
  37.6 0.0 copy-start.3
  37.6 1.2 %copy-done.3 = bf16[16,30720]{1,0:T(8,128)(2,1)S(1)} copy-done((bf16[16,30720]{1,0:T(8,128)(2,1)S(1)}, bf16[16,30720]{1,0:T(8,128)(2,1)}, u32[]{:S(2)}) %copy-start.3) | copy-done | bytes 983064
  38.8 0.0 copy-start.7
  38.8 0.0 copy-start.8
  38.8 5.5 %grid_weights.1.k_ref = bf16[120,256,256]{2,1,0:T(8,128)(2,1)S(1)} custom-call(bf16[16,30720]{1,0:T(8,128)(2,1)S(1)} %copy-done.2, bf16[16,30720]{1,0:T(8,128)(2,1)S(1)} %copy-done.3), custom_call_target="tpu_custom_call" | custom-call | flops 7864320 | bytes 15728640 | tf_op jit(solution)/shard_map/grid_weights/pallas_call | solution.py:369
  44.3 0.0 copy-start
  44.3 5.5 %copy-done = bf16[120,256,256]{2,1,0:T(8,128)(2,1)} copy-done((bf16[120,256,256]{2,1,0:T(8,128)(2,1)}, bf16[120,256,256]{2,1,0:T(8,128)(2,1)S(1)}, u32[]{:S(2)}) %copy-start) | copy-done | bytes 15728664
  49.8 0.0 copy-done.7
  49.8 0.0 copy-done.8
  49.8 0.1 select_reduce_fusion.slots_ref
  49.9 28.0 %all-to-all-done.r_ref = bf16[128,32,384]{2,1,0:T(8,128)(2,1)S(1)} async-done(((bf16[128,32,384]{2,1,0:T(8,128)(2,1)}), bf16[128,32,384]{2,1,0:T(8,128)(2,1)S(1)}, u32[]{:S(2)}, u32[]{:S(2)}) %all-to-all-start) | async-done | bytes 3145760 | tf_op jit(solution)/shard_map/all_to_all | solution.py:494
  77.8 8.8 %correlate.1 = bf16[16,32,256]{2,1,0:T(8,128)(2,1)S(1)} custom-call(s32[120]{0:T(128)S(1)} %select_reduce_fusion.slots_ref, bf16[128,32,384]{2,1,0:T(8,128)(2,1)S(1)} %all-to-all-done.r_ref, bf16[120,256,256]{2,1,0:T(8,128)(2,1)} %copy-done), custom_call_target="tpu_custom_call" | custom-call | tf_op jit(solution)/shard_map/correlate/pallas_call | solution.py:464
  86.7 0.1 reshape.16
  86.8 10.2 %all_to_all.14 = bf16[16,16,2,256]{3,2,1,0:T(2,128)(2,1)S(1)} all-to-all(bf16[16,16,2,256]{3,2,1,0:T(2,128)(2,1)S(1)} %reshape.16), channel_id=1, replica_groups=mesh['chan'=16,'tm'=8] {'tm'}, dimensions={0} | all-to-all | bytes 524288 | tf_op jit(solution)/shard_map/all_to_all | solution.py:503
  97.0 1.0 %copy.10 = f32[8,2,16,2,256]{4,3,2,0,1:T(2,128)} copy(bf16[8,2,16,2,256]{4,3,2,1,0:T(2,128)(2,1)S(1)} %bitcast.6) | data formatting | bytes 786432 | tf_op jit(solution)/shard_map/convert_element_type | solution.py:503
Async XLA Ops:
  2.5 16.0 %collective-permute-start = (bf16[16,8,4096]{2,1,0:T(8,128)(2,1)}, bf16[16,8,4096]{2,1,0:T(8,128)(2,1)S(1)}, u32[]{:S(2)}, u32[]{:S(2)}) collective-permute-start(bf16[16,8,4096]{2,1,0:T(8,128)(2,1)} %get-tuple-element.9), channel_id=1, source_target_pairs={{1,0},{2,1},{3,2},{4,3},{5,4},{6,5},{7,6},{0,7},{9,8},{10,9},{11,1... | collective-permute-start | bytes 3145736 | tf_op jit(solution)/shard_map/ppermute | solution.py:487
  4.0 15.3 %collective-permute-start.1 = (bf16[16,8,4096]{2,1,0:T(8,128)(2,1)S(1)}, bf16[16,8,4096]{2,1,0:T(8,128)(2,1)S(1)}, u32[]{:S(2)}, u32[]{:S(2)}) collective-permute-start(bf16[16,8,4096]{2,1,0:T(8,128)(2,1)S(1)} %get-tuple-element.10), channel_id=1, source_target_pairs={{0,1},{1,2},{2,3},{3,4},{4,5},{5,6},{6,7},{8,9},{9,10},{10,11},{11... | collective-permute-start | bytes 3145736 | tf_op jit(solution)/shard_map/ppermute | solution.py:488
  7.5 1.0 copy-start.4
  8.5 10.8 %copy-start.1 = (bf16[7,512,512]{2,1,0:T(8,128)(2,1)S(1)}, bf16[7,512,512]{2,1,0:T(8,128)(2,1)}, u32[]{:S(2)}) copy-start(bf16[7,512,512]{2,1,0:T(8,128)(2,1)} %constant.12.clone.pairs_hbm.pairs_ref) | copy-start | bytes 11010052
  8.5 10.8 %copy-start.5 = (f32[16,4096]{1,0:T(8,128)S(1)}, f32[16,4096]{1,0:T(8,128)}, u32[]{:S(2)}) copy-start(f32[16,4096]{1,0:T(8,128)} %taps_ref.3) | copy-start | bytes 786436
  8.5 10.8 %copy-start.6 = (bf16[2,256,256]{2,1,0:T(8,128)(2,1)S(1)}, bf16[2,256,256]{2,1,0:T(8,128)(2,1)}, u32[]{:S(2)}) copy-start(bf16[2,256,256]{2,1,0:T(8,128)(2,1)} %constant.13.clone.ends_hbm.ends_ref) | copy-start | bytes 786436
  25.5 52.4 %all-to-all-start = ((bf16[128,32,384]{2,1,0:T(8,128)(2,1)}), bf16[128,32,384]{2,1,0:T(8,128)(2,1)S(1)}, u32[]{:S(2)}, u32[]{:S(2)}) async-start(bf16[128,32,384]{2,1,0:T(8,128)(2,1)} %rest.1), calls=%async_computation | async-start | bytes 6291456 | tf_op jit(solution)/shard_map/all_to_all | solution.py:494
  36.4 1.2 %copy-start.2 = (bf16[16,30720]{1,0:T(8,128)(2,1)S(1)}, bf16[16,30720]{1,0:T(8,128)(2,1)}, u32[]{:S(2)}) copy-start(bf16[16,30720]{1,0:T(8,128)(2,1)} %u_ref.1) | copy-start | bytes 2949124
  37.6 1.2 %copy-start.3 = (bf16[16,30720]{1,0:T(8,128)(2,1)S(1)}, bf16[16,30720]{1,0:T(8,128)(2,1)}, u32[]{:S(2)}) copy-start(bf16[16,30720]{1,0:T(8,128)(2,1)} %v_ref.1) | copy-start | bytes 2949124
  38.8 11.0 %copy-start.7 = (s32[120]{0:T(128)S(1)}, s32[120]{0:T(128)}, u32[]{:S(2)}) copy-start(s32[120]{0:T(128)} %param.10) | copy-start | bytes 1444
  38.8 11.0 %copy-start.8 = (s32[16]{0:T(128)S(1)}, s32[16]{0:T(128)}, u32[]{:S(2)}) copy-start(s32[16]{0:T(128)} %param.11) | copy-start | bytes 196
  44.3 5.5 %copy-start = (bf16[120,256,256]{2,1,0:T(8,128)(2,1)}, bf16[120,256,256]{2,1,0:T(8,128)(2,1)S(1)}, u32[]{:S(2)}) copy-start(bf16[120,256,256]{2,1,0:T(8,128)(2,1)S(1)} %grid_weights.1.k_ref) | copy-start | bytes 47185924
